TPU v7x, 32 devices: a whole 2x2x4 slice. The times are simulated.
32 devices in a mesh: wide: 16 (over z, y, core), narrow: 2 (over x).
Axes of the slice: x: 2, y: 2, z: 4, core: 2. Of those that a mesh axis runs over, the one named last changes fastest.
Arguments:
- tokens: bfloat16 [32, 2048, 1024], P('wide', 'narrow'), may hold values from -6 to 6
- cotangent: bfloat16 [32, 2048, 1024], P('wide', 'narrow'), may hold values from -6 to 6
- lengths: int32 [32], P('wide'), may hold values from 256 to 2048, as said below
- routes: int32 [32, 256], P('wide'), may hold values from 0 to 2047, as said below
- w_qkv: bfloat16 [1024, 3072], P('wide'), may hold values from -0.1875 to 0.1875
- w_out: bfloat16 [1024, 1024], P('wide'), may hold values from -0.75 to 0.75
- w_up: bfloat16 [1024, 4096], P('wide'), may hold values from -0.1875 to 0.1875
- w_down: bfloat16 [4096, 1024], P('wide'), may hold values from -0.09375 to 0.09375
- gain_attn: bfloat16 [1024], P('wide'), may hold values from 0.099609375 to 1.8984375
- gain_mlp: bfloat16 [1024], P('wide'), may hold values from 0.099609375 to 1.8984375
- router: bfloat16 [1024], replicated, may hold values from -0.1875 to 0.1875
Outputs:
- mixed: bfloat16 [32, 2048, 1024], P('wide', 'narrow')
- grad_tokens: bfloat16 [32, 2048, 1024], P('wide', 'narrow')
- grad_qkv: float32 [1024, 3072], P('wide')
- grad_out: float32 [1024, 1024], P('wide')
- grad_up: float32 [1024, 4096], P('wide')
- grad_down: float32 [4096, 1024], P('wide')
- grad_gain_attn: float32 [1024], P('wide')
- grad_gain_mlp: float32 [1024], P('wide')
- grad_router: float32 [1024], replicated
Inputs may be any that keep to these rules, and one draw needn't show every extreme that they name: `lengths`: each run of 2 consecutive sequences holds one of length 2048. `routes`: the first lengths[s] // 8 entries of row s are distinct positions below lengths[s], ascending; the remaining entries are 2047 and unused.
All inputs are finite; a program needn't handle non-finite values.
Results may differ from a plain program's by a relative error of at most 0.012.
Values may be sent and summed in bfloat16 or wider, within the bound.
A program may use at most 192 MiB of HBM per device.

v0:
```python
import jax
import jax.numpy as jnp
from jax import lax
from jax.sharding import PartitionSpec as P

HEAD_DIM = 64


epsilon = 1e-06
masked_score = -1e30


def rms_parts(values):
    inverse = lax.rsqrt(jnp.mean(values * values, axis=-1, keepdims=True) + epsilon)
    return (values * inverse, inverse)


def rms_back(grad_normed, normed, inverse):
    return inverse * (grad_normed - normed * jnp.mean(grad_normed * normed, axis=-1, keepdims=True))


def attend_scores(queries, keys_all, allowed):
    scores = (
        jnp.einsum("sqhe,skhe->shqk", queries, keys_all, preferred_element_type=jnp.float32) * 0.125
    )
    return jnp.where(allowed, scores, masked_score)


def attend_forward(queries, keys_all, values_all, allowed):
    scores = attend_scores(queries, keys_all, allowed)
    top_score = jnp.max(scores, axis=-1, keepdims=True)
    expo = jnp.exp(scores - top_score)
    total = jnp.sum(expo, axis=-1, keepdims=True)
    log_total = top_score + jnp.log(total)
    probs_low = (expo / total).astype(jnp.bfloat16)
    heads_out = jnp.einsum(
        "shqk,skhe->sqhe", probs_low, values_all, preferred_element_type=jnp.float32
    )
    return (heads_out, log_total)


def attend_backward(queries, keys_all, values_all, allowed, log_total, d_heads):
    probs_again = jnp.exp(attend_scores(queries, keys_all, allowed) - log_total)
    d_probs = jnp.einsum("sqhe,skhe->shqk", d_heads, values_all, preferred_element_type=jnp.float32)
    row_dot = jnp.sum(probs_again * d_probs, axis=-1, keepdims=True)
    d_scores = (probs_again * (d_probs - row_dot)).astype(jnp.bfloat16)
    d_queries = (
        jnp.einsum("shqk,skhe->sqhe", d_scores, keys_all, preferred_element_type=jnp.float32)
        * 0.125
    )
    d_key_part = (
        jnp.einsum("shqk,sqhe->skhe", d_scores, queries, preferred_element_type=jnp.float32) * 0.125
    )
    d_value_part = jnp.einsum(
        "shqk,sqhe->skhe",
        probs_again.astype(jnp.bfloat16),
        d_heads,
        preferred_element_type=jnp.float32,
    )
    return (d_queries, d_key_part, d_value_part)


def body(
    tokens, cotangent, lengths, routes, w_qkv, w_out, w_up, w_down, gain_attn, gain_mlp, router
):
    parts_narrow = lax.axis_size("narrow")
    place = lax.axis_index("narrow")
    seqs, span, width = tokens.shape
    list_len = routes.shape[1]
    own_entries = list_len // parts_narrow
    rows_total = seqs * own_entries
    counts = lengths // 8
    entry = jnp.arange(list_len, dtype=jnp.int32)
    live = entry[None, :] < counts[:, None]
    local_slot = routes - place * span
    mine = live & (local_slot >= 0) & (local_slot < span)
    pick = jnp.clip(local_slot, 0, span - 1)
    keep = mine[:, :, None]
    taken_in = jnp.take_along_axis(tokens, pick[:, :, None], axis=1)
    taken_cot = jnp.take_along_axis(cotangent, pick[:, :, None], axis=1)
    blank = jnp.zeros_like(taken_in)
    rows_in, rows_cot = (
        lax.psum_scatter(
            jnp.where(keep, taken_in, blank), "narrow", scatter_dimension=1, tiled=True
        ).astype(jnp.float32),
        lax.psum_scatter(
            jnp.where(keep, taken_cot, blank), "narrow", scatter_dimension=1, tiled=True
        ).astype(jnp.float32),
    )
    inputs_rows = rows_in.reshape(rows_total, width)
    inputs_low = inputs_rows.astype(jnp.bfloat16)
    dout = rows_cot.reshape(rows_total, width)
    gathered = (
        lax.all_gather(w_qkv, "wide", axis=0, tiled=True),
        lax.all_gather(w_out, "wide", axis=0, tiled=True),
        lax.all_gather(w_up, "wide", axis=0, tiled=True),
        lax.all_gather(w_down, "wide", axis=0, tiled=True),
        lax.all_gather(gain_attn, "wide", axis=0, tiled=True),
        lax.all_gather(gain_mlp, "wide", axis=0, tiled=True),
    )
    weight_qkv, weight_out, weight_up, weight_down, gain_first, gain_second = gathered
    scale_first = gain_first.astype(jnp.float32)
    scale_second = gain_second.astype(jnp.float32)
    normed_one, inverse_one = rms_parts(inputs_rows)
    normed_low = (normed_one * scale_first).astype(jnp.bfloat16)
    project = jnp.dot(normed_low, weight_qkv, preferred_element_type=jnp.float32).astype(
        jnp.bfloat16
    )
    queries = project[:, :width].reshape(seqs, own_entries, -1, HEAD_DIM)
    key_own = project[:, width : 2 * width].reshape(seqs, own_entries, width)
    value_own = project[:, 2 * width :].reshape(seqs, own_entries, width)
    keys_all, values_all = (
        lax.all_gather(key_own, "narrow", axis=1, tiled=True),
        lax.all_gather(value_own, "narrow", axis=1, tiled=True),
    )
    keys_all = keys_all.reshape(seqs, list_len, -1, HEAD_DIM)
    values_all = values_all.reshape(seqs, list_len, -1, HEAD_DIM)
    query_pos = place * own_entries + jnp.arange(own_entries, dtype=jnp.int32)
    allowed = (entry[None, None, None, :] <= query_pos[None, None, :, None]) & (
        entry[None, None, None, :] < counts[:, None, None, None]
    )
    heads_out, log_total = attend_forward(queries, keys_all, values_all, allowed)
    heads_low = heads_out.reshape(rows_total, width).astype(jnp.bfloat16)
    attend_out = jnp.dot(heads_low, weight_out, preferred_element_type=jnp.float32)
    middle = inputs_rows + attend_out
    normed_two, inverse_two = rms_parts(middle)
    second_low = (normed_two * scale_second).astype(jnp.bfloat16)
    pre_act = jnp.dot(second_low, weight_up, preferred_element_type=jnp.float32)
    activ_full, gelu_back = jax.vjp(jax.nn.gelu, pre_act)
    activ_low = activ_full.astype(jnp.bfloat16)
    mlp_out = jnp.dot(activ_low, weight_down, preferred_element_type=jnp.float32)
    branch = attend_out + mlp_out
    router_val = jnp.dot(inputs_low, router, preferred_element_type=jnp.float32)
    out_low = (inputs_rows + router_val[:, None] * branch).astype(jnp.bfloat16)
    back_set = (
        lax.all_gather(w_qkv, "wide", axis=0, tiled=True),
        lax.all_gather(w_out, "wide", axis=0, tiled=True),
        lax.all_gather(w_up, "wide", axis=0, tiled=True),
        lax.all_gather(w_down, "wide", axis=0, tiled=True),
        lax.all_gather(gain_attn, "wide", axis=0, tiled=True),
        lax.all_gather(gain_mlp, "wide", axis=0, tiled=True),
    )
    back_qkv, back_out, back_up, back_down, back_gain_a, back_gain_m = back_set
    back_first = back_gain_a.astype(jnp.float32)
    back_second = back_gain_m.astype(jnp.float32)
    d_branch = router_val[:, None] * dout
    d_router_val = jnp.sum(dout * branch, axis=-1)
    d_mlp = d_branch.astype(jnp.bfloat16)
    grad_down_full = jnp.einsum("rf,rd->fd", activ_low, d_mlp, preferred_element_type=jnp.float32)
    d_act = jnp.einsum("rd,fd->rf", d_mlp, back_down, preferred_element_type=jnp.float32)
    d_pre = gelu_back(d_act)[0].astype(jnp.bfloat16)
    grad_up_full = jnp.einsum("rd,rf->df", second_low, d_pre, preferred_element_type=jnp.float32)
    d_normed_two = jnp.einsum("rf,df->rd", d_pre, back_up, preferred_element_type=jnp.float32)
    grad_gain_two = jnp.sum(d_normed_two * normed_two, axis=0)
    d_middle = rms_back(d_normed_two * back_second, normed_two, inverse_two)
    d_attend = (d_branch + d_middle).astype(jnp.bfloat16)
    grad_out_full = jnp.einsum("rd,re->de", heads_low, d_attend, preferred_element_type=jnp.float32)
    d_heads = jnp.einsum(
        "re,de->rd", d_attend, back_out, preferred_element_type=jnp.float32
    ).astype(jnp.bfloat16)
    d_heads_own = d_heads.reshape(seqs, own_entries, -1, HEAD_DIM)
    d_queries, d_key_part, d_value_part = attend_backward(
        queries, keys_all, values_all, allowed, log_total, d_heads_own
    )
    d_key_own, d_value_own = (
        lax.psum_scatter(
            d_key_part.reshape(seqs, list_len, width), "narrow", scatter_dimension=1, tiled=True
        ),
        lax.psum_scatter(
            d_value_part.reshape(seqs, list_len, width), "narrow", scatter_dimension=1, tiled=True
        ),
    )
    d_project = jnp.concatenate(
        [
            d_queries.reshape(rows_total, width),
            d_key_own.reshape(rows_total, width),
            d_value_own.reshape(rows_total, width),
        ],
        axis=-1,
    ).astype(jnp.bfloat16)
    grad_qkv_full = jnp.einsum(
        "rd,re->de", normed_low, d_project, preferred_element_type=jnp.float32
    )
    d_normed = jnp.einsum("re,de->rd", d_project, back_qkv, preferred_element_type=jnp.float32)
    grad_gain_one = jnp.sum(d_normed * normed_one, axis=0)
    d_norm_rows = rms_back(d_normed * back_first, normed_one, inverse_one)
    d_rows = dout + d_middle + d_norm_rows + d_router_val[:, None] * router.astype(jnp.float32)
    grad_router_part = jnp.dot(d_router_val, inputs_rows, precision=lax.Precision.HIGHEST)
    grad_low = d_rows.astype(jnp.bfloat16)
    out_all, grad_all = (
        lax.all_gather(out_low.reshape(seqs, own_entries, width), "narrow", axis=1, tiled=True),
        lax.all_gather(grad_low.reshape(seqs, own_entries, width), "narrow", axis=1, tiled=True),
    )
    target = jnp.where(mine, pick, span)
    put = jax.vmap(lambda base, where_to, fresh: base.at[where_to].set(fresh, mode="drop"))
    mixed = put(tokens, target, out_all)
    grad_tokens = put(cotangent, target, grad_all)
    shards = (
        lax.psum_scatter(grad_qkv_full, "wide", scatter_dimension=0, tiled=True),
        lax.psum_scatter(grad_out_full, "wide", scatter_dimension=0, tiled=True),
        lax.psum_scatter(grad_up_full, "wide", scatter_dimension=0, tiled=True),
        lax.psum_scatter(grad_down_full, "wide", scatter_dimension=0, tiled=True),
        lax.psum_scatter(grad_gain_one, "wide", scatter_dimension=0, tiled=True),
        lax.psum_scatter(grad_gain_two, "wide", scatter_dimension=0, tiled=True),
    )
    summed = lax.psum((shards[0], shards[1], shards[2], shards[3], shards[4], shards[5]), "narrow")
    grad_router = lax.psum(grad_router_part, ("wide", "narrow"))
    return (
        mixed,
        grad_tokens,
        summed[0],
        summed[1],
        summed[2],
        summed[3],
        summed[4],
        summed[5],
        grad_router,
    )


def solution(mesh):
    in_specs = (
        P("wide", "narrow", None),
        P("wide", "narrow", None),
        P("wide"),
        P("wide", None),
        P("wide", None),
        P("wide", None),
        P("wide", None),
        P("wide", None),
        P("wide"),
        P("wide"),
        P(),
    )
    out_specs = (
        P("wide", "narrow", None),
        P("wide", "narrow", None),
        P("wide", None),
        P("wide", None),
        P("wide", None),
        P("wide", None),
        P("wide"),
        P("wide"),
        P(),
    )
    return jax.shard_map(body, mesh=mesh, in_specs=in_specs, out_specs=out_specs, check_vma=False)
```

profile of v0, /device:TPU:0, one launch (start us, length us, event | category | flops | bytes accessed | tf_op | source)
XLA Modules:
  0.0 1275.2 jit_solution(6805245020634665069)
XLA Ops:
  8.1 4.8 copy.85
  12.9 2.0 copy.84
  15.0 18.2 %gather_fusion.1 = bf16[512,1024]{1,0:T(8,128)(2,1)S(1)} fusion(bf16[2,1024,1024]{2,1,0:T(8,128)(2,1)} %copy.85, s32[512]{0:T(512)S(1)} %bitcast.135), kind=kCustom, calls=%fused_computation.1.clone | custom fusion | bytes 2101248 | tf_op jit(solution)/shard_map/jit(take_along_axis)/gather | solution.py:80
  33.3 18.2 %gather_fusion = bf16[512,1024]{1,0:T(8,128)(2,1)S(1)} fusion(bf16[2,1024,1024]{2,1,0:T(8,128)(2,1)} %copy.84, s32[512]{0:T(512)S(1)} %bitcast.136), kind=kCustom, calls=%fused_computation.clone | custom fusion | bytes 2101248 | tf_op jit(solution)/shard_map/jit(take_along_axis)/gather | solution.py:79
  51.6 1.6 select_select_fusion
  56.4 30.3 %all-reduce.7 = (bf16[1024]{0:T(1024)(128)(2,1)S(1)}, bf16[1024]{0:T(1024)(128)(2,1)S(1)}) all-reduce(bf16[1024]{0:T(1024)(128)(2,1)S(1)} %dynamic-update-slice, bf16[1024]{0:T(1024)(128)(2,1)S(1)} %dynamic-update-slice.1), channel_id=1, replica_groups=mesh['wide'=16,'narrow'=2] {'wide'}, use_global_device_ids=true, to_apply=%add | all-reduce | flops 2048 | bytes 8192
  86.7 1.2 fusion.33
  87.9 1.4 fusion.28
  89.3 31.1 %all-gather.9.cloned.1.call-done = bf16[1024,3072]{1,0:T(8,128)(2,1)} async-done(((bf16[64,3072]{1,0:T(8,128)(2,1)}), bf16[1024,3072]{1,0:T(8,128)(2,1)}) %all-gather.9.cloned.1.call-update) | async-done | bytes 6291472 | tf_op jit(solution)/shard_map/all_gather | solution.py:94
  120.5 4.6 convolution_convert_fusion
  125.1 1.1 fusion.54
  128.0 0.7 all-gather.17.cloned.1.call-update
  129.3 2.1 fusion.16
  132.1 0.9 copy.43
  132.9 13.4 %all-gather.13.cloned.1.call-done = bf16[2,256,1024]{2,1,0:T(8,128)(2,1)} async-done(((bf16[2,128,1024]{2,1,0:T(8,128)(2,1)}), bf16[2,256,1024]{2,1,0:T(8,128)(2,1)}) %all-gather.13.cloned.1.call-update) | async-done | bytes 1048592 | tf_op jit(solution)/shard_map/all_gather | solution.py:113
  146.3 1.5 copy.42
  147.8 21.8 %all-gather.11.cloned.1.call-done = bf16[2,256,1024]{2,1,0:T(8,128)(2,1)} async-done(((bf16[2,128,1024]{2,1,0:T(8,128)(2,1)}), bf16[2,256,1024]{2,1,0:T(8,128)(2,1)}) %all-gather.11.cloned.1.call-update) | async-done | bytes 1048592 | tf_op jit(solution)/shard_map/all_gather | solution.py:114
  169.7 1.5 copy.40
  171.2 1.2 fusion.56
  172.3 1.3 fusion.7
  173.7 2.3 fusion.18
  176.5 36.6 %all-gather.15.cloned.1.call-done = bf16[1024,1024]{1,0:T(8,128)(2,1)} async-done(((bf16[64,1024]{1,0:T(8,128)(2,1)}), bf16[1024,1024]{1,0:T(8,128)(2,1)}) %all-gather.15.cloned.1.call-update) | async-done | bytes 2097168 | tf_op jit(solution)/shard_map/all_gather | solution.py:95
  213.1 3.3 multiply_reduce_fusion.3
  216.4 72.4 %all-gather.19.cloned.1.call-done = bf16[4096,1024]{1,0:T(8,128)(2,1)} async-done(((bf16[256,1024]{1,0:T(8,128)(2,1)}), bf16[4096,1024]{1,0:T(8,128)(2,1)}) %all-gather.19.cloned.1.call-update) | async-done | bytes 8388624 | tf_op jit(solution)/shard_map/all_gather | solution.py:97
  288.8 7.8 fusion.58
  296.6 67.6 %all-gather.17.cloned.1.call-done = bf16[1024,4096]{1,0:T(8,128)(2,1)} async-done(((bf16[64,4096]{1,0:T(8,128)(2,1)}), bf16[1024,4096]{1,0:T(8,128)(2,1)}) %all-gather.17.cloned.1.call-update) | async-done | bytes 8388624 | tf_op jit(solution)/shard_map/all_gather | solution.py:96
  364.2 9.5 fusion.6
  373.7 8.2 multiply_reduce_fusion.1
  382.2 4.6 fusion.23
  386.9 0.7 convolution_convert_fusion.1
  387.6 1.6 reshape.247
  389.2 2.0 copy.46
  391.3 3.6 multiply_reduce_fusion
  394.9 1.3 multiply_convert_fusion
  396.2 1.7 convolution_multiply_fusion
  398.0 3.0 copy.49
  401.0 4.5 fusion.9
  405.5 3.1 copy.51
  408.6 3.7 fusion.37
  412.4 2.1 fusion.17
  415.2 16.0 %reduce-scatter.13.cloned.1.call-done = f32[2,128,1024]{2,1,0:T(8,128)} async-done(((f32[2,256,1024]{2,1,0:T(8,128)}), f32[2,128,1024]{2,1,0:T(8,128)}) %reduce-scatter.13.cloned.1.call-update) | async-done | bytes 1048592 | tf_op jit(solution)/shard_map/reduce_scatter | solution.py:166
  431.2 1.3 convert.15
  432.7 32.7 %reduce-scatter.15.cloned.1.call-done = f32[2,128,1024]{2,1,0:T(8,128)} async-done(((f32[2,256,1024]{2,1,0:T(8,128)}), f32[2,128,1024]{2,1,0:T(8,128)}) %reduce-scatter.15.cloned.1.call-update) | async-done | bytes 1048592 | tf_op jit(solution)/shard_map/reduce_scatter | solution.py:169
  465.4 1.3 convert.16
  466.9 6.3 fusion.35
  473.6 0.9 copy-done.4
  474.5 10.6 fusion.51
  485.1 1.0 copy-done.18
  486.1 10.9 fusion.53
  498.1 5.2 fusion.32
  503.3 1.5 fusion.22
  504.9 36.6 %reduce-scatter.19.cloned.1.call-done = f32[64,1024]{1,0:T(8,128)} async-done(((f32[1024,1024]{1,0:T(8,128)}), f32[64,1024]{1,0:T(8,128)}) %reduce-scatter.19.cloned.1.call-update) | async-done | bytes 262160 | tf_op jit(solution)/shard_map/reduce_scatter | solution.py:200
  541.5 138.5 %reduce-scatter.17.cloned.1.call-done = f32[64,3072]{1,0:T(8,128)} async-done(((f32[1024,3072]{1,0:T(8,128)}), f32[64,3072]{1,0:T(8,128)}) %reduce-scatter.17.cloned.1.call-update) | async-done | bytes 786448 | tf_op jit(solution)/shard_map/reduce_scatter | solution.py:199
  679.9 182.3 %reduce-scatter.21.cloned.1.call-done = f32[64,4096]{1,0:T(8,128)} async-done(((f32[1024,4096]{1,0:T(8,128)}), f32[64,4096]{1,0:T(8,128)}) %reduce-scatter.21.cloned.1.call-update) | async-done | bytes 1048592 | tf_op jit(solution)/shard_map/reduce_scatter | solution.py:201
  862.2 182.3 %reduce-scatter.23.cloned.1.call-done = f32[256,1024]{1,0:T(8,128)} async-done(((f32[4096,1024]{1,0:T(8,128)}), f32[256,1024]{1,0:T(8,128)}) %reduce-scatter.23.cloned.1.call-update) | async-done | bytes 1048592 | tf_op jit(solution)/shard_map/reduce_scatter | solution.py:202
  1045.5 39.4 %psum.55 = f32[1024]{0:T(1024)} all-reduce(f32[1024]{0:T(1024)S(1)} %bitcast.159), channel_id=1, replica_groups=mesh['wide'=16,'narrow'=2] {'wide','narrow'}, use_global_device_ids=true, to_apply=%region_28.30 | all-reduce | flops 1024 | bytes 8192 | tf_op jit(solution)/shard_map/psum | solution.py:207
  1084.9 68.5 %scatter_fusion = bf16[2,1024,1024]{2,1,0:T(8,128)(2,1)} fusion(bf16[2,1024,1024]{2,1,0:T(8,128)(2,1)} %copy.84, s32[512]{0:T(512)S(1)} %bitcast.133, bf16[512,1024]{1,0:T(8,128)(2,1)} %bitcast.156), kind=kCustom, calls=%fused_computation.2 | custom fusion | bytes 3149824 | tf_op jit(solution)/shard_map/vmap()/scatter | solution.py:195
  1153.4 33.1 %all-reduce.4 = (f32[1024]{0:T(1024)S(1)}, f32[1024]{0:T(1024)S(1)}) all-reduce(f32[1024]{0:T(1024)S(1)} %get-tuple-element.12, f32[1024]{0:T(1024)S(1)} %get-tuple-element.10), channel_id=10, replica_groups=mesh['wide'=16,'narrow'=2] {'wide'}, use_global_device_ids=true, to_apply=%region_23.25.clone | all-reduce | flops 2048 | bytes 16384
  1186.6 5.4 all-reduce.5
  1192.0 68.5 %scatter_fusion.1 = bf16[2,1024,1024]{2,1,0:T(8,128)(2,1)} fusion(bf16[2,1024,1024]{2,1,0:T(8,128)(2,1)} %copy.85, s32[512]{0:T(512)S(1)} %bitcast.134, bf16[512,1024]{1,0:T(8,128)(2,1)} %bitcast.157), kind=kCustom, calls=%fused_computation.3 | custom fusion | bytes 3149824 | tf_op jit(solution)/shard_map/vmap()/scatter | solution.py:195
  1260.5 2.2 copy.86
  1262.7 1.7 copy.87
  1264.4 2.3 copy.88
  1266.6 1.0 copy.89
  (142 shorter events, 9.6 us)
Async XLA Ops:
  8.0 78.7 %reduce-scatter.9.cloned.1.call-start = ((), (), s32[]{:S(2)}) async-start(), calls=%async_computation.8 | async-start | bytes 1572864 | tf_op jit(solution)/shard_map/reduce_scatter | solution.py:83
  8.1 4.8 copy-start.13
  12.9 2.0 copy-start.33
  12.9 2.0 copy-start.30
  51.5 3.1 copy-start.31
  51.5 4.3 copy-start.34
  51.5 4.6 copy-start.35
  53.2 67.2 %all-gather.9.cloned.1.call-start = ((), (), s32[]{:S(2)}) async-start(), calls=%async_computation.9 | async-start | bytes 6684672 | tf_op jit(solution)/shard_map/all_gather | solution.py:94
  53.8 75.5 %reduce-scatter.11.cloned.1.call-start = ((), (), s32[]{:S(2)}) async-start(), calls=%async_computation.16 | async-start | bytes 1572864 | tf_op jit(solution)/shard_map/reduce_scatter | solution.py:86
  54.6 91.8 %all-gather.13.cloned.1.call-start = ((), (), s32[]{:S(2)}) async-start(), calls=%async_computation.11 | async-start | bytes 1572864 | tf_op jit(solution)/shard_map/all_gather | solution.py:113
  89.3 35.7 %copy-start.14 = (bf16[256,1024]{1,0:T(8,128)(2,1)}, bf16[256,1024]{1,0:T(8,128)(2,1)S(1)}, u32[]{:S(2)}) copy-start(bf16[256,1024]{1,0:T(8,128)(2,1)S(1)} %fusion.28) | copy-start | bytes 1572868
  125.1 3.7 copy-start.29
  125.1 4.0 copy-start.2
  126.2 43.4 %all-gather.11.cloned.1.call-start = ((), (), s32[]{:S(2)}) async-start(), calls=%async_computation.10 | async-start | bytes 1572864 | tf_op jit(solution)/shard_map/all_gather | solution.py:114
  126.8 86.3 %all-gather.15.cloned.1.call-start = ((), (), s32[]{:S(2)}) async-start(), calls=%async_computation.12 | async-start | bytes 2228224 | tf_op jit(solution)/shard_map/all_gather | solution.py:95
  127.4 161.4 %all-gather.19.cloned.1.call-start = ((), (), s32[]{:S(2)}) async-start(), calls=%async_computation.14 | async-start | bytes 8912896 | tf_op jit(solution)/shard_map/all_gather | solution.py:97
  128.0 236.2 %all-gather.17.cloned.1.call-start = ((), (), s32[]{:S(2)}) async-start(), calls=%async_computation.13 | async-start | bytes 8912896 | tf_op jit(solution)/shard_map/all_gather | solution.py:96
  128.7 302.5 %reduce-scatter.13.cloned.1.call-start = ((), (), s32[]{:S(2)}) async-start(), calls=%async_computation.17 | async-start | bytes 3145728 | tf_op jit(solution)/shard_map/reduce_scatter | solution.py:166
  147.8 25.8 %copy-start.5 = (bf16[2,256,1024]{1,2,0:T(8,128)(2,1)}, bf16[2,256,1024]{1,2,0:T(8,128)(2,1)S(1)}, u32[]{:S(2)}) copy-start(bf16[2,256,1024]{1,2,0:T(8,128)(2,1)S(1)} %copy.42) | copy-start | bytes 3145732
  171.1 2.5 copy-start.11
  172.3 3.6 copy-start
  176.0 112.9 %copy-start.17 = (bf16[256,1024]{1,0:T(8,128)(2,1)S(1)}, bf16[256,1024]{1,0:T(8,128)(2,1)}, u32[]{:S(2)}) copy-start(bf16[256,1024]{1,0:T(8,128)(2,1)} %fusion.16) | copy-start | bytes 1572868
  176.5 120.1 %copy-start.9 = (bf16[2,128,16,64]{1,0,3,2:T(2,128)(2,1)}, bf16[2,128,16,64]{1,0,3,2:T(2,128)(2,1)S(1)}, u32[]{:S(2)}) copy-start(bf16[2,128,16,64]{1,0,3,2:T(2,128)(2,1)S(1)} %copy.44) | copy-start | bytes 1572868
  216.4 165.6 %copy-start.3 = (f32[256,1024]{1,0:T(8,128)}, f32[256,1024]{1,0:T(8,128)S(1)}, u32[]{:S(2)}) copy-start(f32[256,1024]{1,0:T(8,128)S(1)} %get-tuple-element.25) | copy-start | bytes 3145732
  373.7 8.3 copy-start.16
  373.7 8.3 copy-start.6
  373.7 8.3 copy-start.22
  373.7 8.3 copy-start.27
  373.7 8.5 copy-start.32
  382.0 4.8 copy-start.25
  382.2 4.6 copy-start.21
  386.8 8.0 copy-start.28
  386.8 4.4 copy-start.12
  391.3 3.6 copy-start.7
  391.3 3.6 copy-start.1
  398.0 3.1 copy-start.8
  401.0 64.4 %reduce-scatter.15.cloned.1.call-start = ((), (), s32[]{:S(2)}) async-start(), calls=%async_computation.18 | async-start | bytes 3145728 | tf_op jit(solution)/shard_map/reduce_scatter | solution.py:169
  405.5 3.1 copy-start.10
  408.6 132.9 %reduce-scatter.19.cloned.1.call-start = ((), (), s32[]{:S(2)}) async-start(), calls=%async_computation.21 | async-start | bytes 4456448 | tf_op jit(solution)/shard_map/reduce_scatter | solution.py:200
  412.4 267.5 %reduce-scatter.17.cloned.1.call-start = ((), (), s32[]{:S(2)}) async-start(), calls=%async_computation.20 | async-start | bytes 13369344 | tf_op jit(solution)/shard_map/reduce_scatter | solution.py:199
  414.5 52.4 %copy-start.15 = (bf16[256,1024]{1,0:T(8,128)(2,1)S(1)}, bf16[256,1024]{1,0:T(8,128)(2,1)}, u32[]{:S(2)}) copy-start(bf16[256,1024]{1,0:T(8,128)(2,1)} %copy-done.14) | copy-start | bytes 1572868
  466.9 6.3 copy-start.19
  473.2 1.2 copy-start.4
  473.3 388.9 %reduce-scatter.21.cloned.1.call-start = ((), (), s32[]{:S(2)}) async-start(), calls=%async_computation.22 | async-start | bytes 17825792 | tf_op jit(solution)/shard_map/reduce_scatter | solution.py:201
  485.1 1.1 copy-start.18
  485.1 559.4 %reduce-scatter.23.cloned.1.call-start = ((), (), s32[]{:S(2)}) async-start(), calls=%async_computation.23 | async-start | bytes 17825792 | tf_op jit(solution)/shard_map/reduce_scatter | solution.py:202
  497.1 1.0 copy-start.20
  497.1 587.8 %all-gather.21.cloned.1.call-start = ((), (), s32[]{:S(2)}) async-start(), calls=%async_computation.15 | async-start | bytes 1572864 | tf_op jit(solution)/shard_map/all_gather | solution.py:191
  497.7 694.4 %all-gather.23.cloned.1.call-start = ((), (), s32[]{:S(2)}) async-start(), calls=%async_computation.19 | async-start | bytes 1572864 | tf_op jit(solution)/shard_map/all_gather | solution.py:192
  498.1 5.2 copy-start.23
  498.1 5.2 copy-start.26
  504.9 755.7 %all-reduce.10.cloned.1.call-start = ((), (), s32[]{:S(2)}) async-start(), calls=%async_computation.24 | async-start | bytes 6291456 | tf_op jit(solution)/shard_map/psum | solution.py:206
  1260.5 6.1 copy-start.24
Sparse Core Ops, SparseCore 0:
  53.4 23.0 reduce-scatter.8
  79.4 20.2 reduce-scatter.10
  126.3 19.9 all-gather.12
  148.3 21.2 all-gather.10
  171.7 41.3 all-gather.14
  215.1 73.6 all-gather.18
  291.0 73.1 all-gather.16
  401.1 30.0 reduce-scatter.12
  433.5 31.8 reduce-scatter.14
  469.1 72.3 reduce-scatter.18
  546.1 133.8 reduce-scatter.16
  684.5 177.7 reduce-scatter.20
  866.9 177.5 reduce-scatter.22
  1046.5 20.4 all-gather.20
  1069.1 21.9 all-gather.22
  1093.5 86.2 all-reduce.9
Sparse Core Ops, SparseCore 1:
  56.0 64.4 all-gather.8
where the time goes:
time: 1290 us; the launch traced here: 1280 us
  waiting for transfers between devices  835 us (65%)
  local copies, waits for them, and re-layouts  208 us (16%)
  blocking collectives  108 us (8%)
  matrix products  91.4 us (7%)
  between operations  17.9 us (1%)
  other arithmetic  13.4 us (1%)
    reduce_scatter x1, waiting for transfers between devices, body(): lax.psum_scatter(grad_up_full, 'wide', scatter_dimension=0, tiled=True)  182 us
    reduce_scatter x1, waiting for transfers between devices, body(): lax.psum_scatter(grad_down_full, 'wide', scatter_dimension=0, tiled=True)  182 us
    reduce_scatter x1, waiting for transfers between devices, body(): lax.psum_scatter(grad_qkv_full, 'wide', scatter_dimension=0, tiled=True)  138 us
    scatter x2, local copies, waits for them, and re-layouts, body(): base.at[where_to].set(fresh, mode='drop')  137 us
    all_gather x1, waiting for transfers between devices, body(): lax.all_gather(w_down, 'wide', axis=0, tiled=True)  72.4 us
    all_gather x1, waiting for transfers between devices, body(): lax.all_gather(w_up, 'wide', axis=0, tiled=True)  67.6 us
    unnamed x2, blocking collectives  63.4 us
    psum x1, blocking collectives, body(): grad_router = lax.psum(grad_router_part, ('wide', 'narrow'))  39.4 us
  transfers between devices with their start and end apart: 17, of which 12 were waited for; matrix products, arithmetic and copies ran while one was open for 17% of the time, Pallas kernels for 0%

commit v1 on v0

--- a/solution.py
+++ b/solution.py
@@ -1,10 +1,16 @@
+import functools
+
 import jax
 import jax.numpy as jnp
 from jax import lax
+from jax.experimental import pallas as pl
+from jax.experimental.pallas import tpu as pltpu
 from jax.sharding import PartitionSpec as P
 
 HEAD_DIM = 64
-
+MESH = pl.DeviceIdType.MESH
+F32 = jnp.float32
+BF16 = jnp.bfloat16
 
 epsilon = 1e-06
 masked_score = -1e30
@@ -60,7 +66,7 @@
     return (d_queries, d_key_part, d_value_part)
 
 
-def body(
+def general_body(
     tokens, cotangent, lengths, routes, w_qkv, w_out, w_up, w_down, gain_attn, gain_mlp, router
 ):
     parts_narrow = lax.axis_size("narrow")
@@ -218,6 +224,662 @@
     )
 
 
+def dot(left, right):
+    return jnp.dot(left, right, preferred_element_type=F32)
+
+
+def dot_nt(left, right):
+    return lax.dot_general(left, right, (((1,), (1,)), ((), ())), preferred_element_type=F32)
+
+
+def dot_tn(left, right):
+    return lax.dot_general(left, right, (((0,), (0,)), ((), ())), preferred_element_type=F32)
+
+
+class Place:
+    def __init__(self, wide):
+        self.ring = wide // 2
+        self.length = self.ring // 2
+        self.w = lax.axis_index("wide")
+        self.n = lax.axis_index("narrow")
+        self.c = self.w % 2
+        self.q = self.w // 2
+        row = self.q % 2
+        col = self.q // 2
+        self.r = col + row * (2 * self.length - 1 - 2 * col)
+
+    def chip(self, ring_pos):
+        pos = lax.rem(ring_pos + 2 * self.ring, self.ring)
+        row = pos // self.length
+        col = pos + row * (2 * self.length - 1 - 2 * pos)
+        return col * 2 + row
+
+    def at_ring(self, ring_pos):
+        return (self.chip(ring_pos) * 2 + self.c, self.n)
+
+    def sibling(self):
+        return (self.q * 2 + 1 - self.c, self.n)
+
+    def across(self):
+        return (self.w, 1 - self.n)
+
+    def flipped(self, bit):
+        return ((self.q + bit - 2 * bit * ((self.q // bit) % 2)) * 2 + self.c, self.n)
+
+
+def greet(partners):
+    barrier = pltpu.get_barrier_semaphore()
+    for partner in partners:
+        pl.semaphore_signal(barrier, inc=1, device_id=partner, device_id_type=MESH)
+    pl.semaphore_wait(barrier, len(partners))
+
+
+def remote(src, dst, send, recv, device):
+    return pltpu.make_async_remote_copy(
+        src_ref=src, dst_ref=dst, send_sem=send, recv_sem=recv, device_id=device, device_id_type=MESH
+    )
+
+
+def gather_kernel(
+    wide,
+    gains,
+    wq,
+    wo,
+    wu,
+    wd,
+    rows,
+    gains_all,
+    wq_all,
+    wo_all,
+    wu_all,
+    wd_all,
+    rows_got,
+    own_sem,
+    ring_send,
+    ring_recv,
+    sib_send,
+    sib_recv,
+    x_send,
+    x_recv,
+):
+    at = Place(wide)
+    ring, steps = at.ring, at.ring // 2
+    depth = wo.shape[0]
+    width = wo.shape[1]
+    parts = [(gains, gains_all, gains.shape[0], 0, gains.shape[0], 0, gains.shape[1])]
+    parts += [(wq, wq_all, depth, 0, depth, j * width, width) for j in range(3)]
+    parts += [(wo, wo_all, depth, 0, depth, 0, width)]
+    parts += [(wu, wu_all, depth, 0, depth, j * width, width) for j in range(wu.shape[1] // width)]
+    parts += [
+        (wd, wd_all, wd.shape[0], j * depth, depth, 0, width) for j in range(wd.shape[0] // depth)
+    ]
+
+    def block(k, ring_pos, core, half, own):
+        src, dst, shard, first, taken, col, cols = parts[k]
+        size = taken if half is None else taken // 2
+        low = first + (0 if half is None else half * size)
+        if own:
+            return src.at[pl.ds(low, size), pl.ds(col, cols)]
+        base = (at.chip(ring_pos) * 2 + core) * shard + low
+        return dst.at[pl.ds(pl.multiple_of(base, 8), size), pl.ds(col, cols)]
+
+    def half_of(s, d):
+        return d if s == steps else None
+
+    def ring_out(k, s, d):
+        pos = at.r - (s - 1) if d == 0 else at.r + (s - 1)
+        half = half_of(s, d)
+        src = block(k, pos, at.c, half, s == 1)
+        dst = block(k, pos, at.c, half, False)
+        to = at.at_ring(at.r + 1 if d == 0 else at.r - 1)
+        return remote(src, dst, ring_send.at[k, s - 1, d], ring_recv.at[k, s - 1, d], to)
+
+    def ring_in(k, s, d):
+        pos = at.r - s if d == 0 else at.r + s
+        ref = block(k, pos, at.c, half_of(s, d), False)
+        to = at.at_ring(at.r + 1 if d == 0 else at.r - 1)
+        return remote(ref, ref, ring_send.at[k, s - 1, d], ring_recv.at[k, s - 1, d], to)
+
+    def sib(k, s, d, core):
+        pos = at.r - s if d == 0 else at.r + s
+        half = half_of(s, d)
+        j = 0 if s == 0 else 1 + 2 * (s - 1) + d
+        dst = block(k, pos, core, half, False)
+        src = block(k, pos, core, half, s == 0)
+        return remote(src, dst, sib_send.at[k, j], sib_recv.at[k, j], at.sibling())
+
+    greet([at.at_ring(at.r + 1), at.at_ring(at.r - 1), at.sibling(), at.across()])
+    cross = remote(rows, rows_got, x_send, x_recv, at.across())
+    cross.start()
+    count = len(parts)
+    for i in range(count + steps):
+        if i < count:
+            for d in (0, 1):
+                ring_out(i, 1, d).start()
+            sib(i, 0, 0, at.c).start()
+            pltpu.make_async_copy(
+                block(i, at.r, at.c, None, True), block(i, at.r, at.c, None, False), own_sem.at[i]
+            ).start()
+        for s in range(1, steps + 1):
+            k = i - s
+            if 0 <= k < count:
+                for d in (0, 1):
+                    ring_in(k, s, d).wait_recv()
+                    if s < steps:
+                        if s + 1 < steps or d == 0:
+                            ring_out(k, s + 1, d).start()
+                        else:
+                            ring_out(k, s + 1, d).start()
+                    sib(k, s, d, at.c).start()
+    for k in range(count):
+        pltpu.make_async_copy(
+            block(k, at.r, at.c, None, True), block(k, at.r, at.c, None, False), own_sem.at[k]
+        ).wait()
+        sib(k, 0, 0, at.c).wait_send()
+        sib(k, 0, 0, 1 - at.c).wait_recv()
+        for s in range(1, steps + 1):
+            for d in (0, 1):
+                ring_out(k, s, d).wait_send()
+                sib(k, s, d, at.c).wait_send()
+                sib(k, s, d, 1 - at.c).wait_recv()
+    cross.wait()
+
+
+def gather_weights(wide, gains, wq, wo, wu, wd, rows):
+    count = 1 + 3 + 1 + wu.shape[1] // wo.shape[1] + wd.shape[0] // wo.shape[0]
+    steps = wide // 4
+    full = [jax.ShapeDtypeStruct((wide * a.shape[0], a.shape[1]), a.dtype) for a in (gains, wq, wo, wu, wd)]
+    anywhere = pl.BlockSpec(memory_space=pl.ANY)
+    return pl.pallas_call(
+        functools.partial(gather_kernel, wide),
+        out_shape=full + [jax.ShapeDtypeStruct(rows.shape, rows.dtype)],
+        in_specs=[anywhere] * 6,
+        out_specs=[anywhere] * 6,
+        scratch_shapes=[
+            pltpu.SemaphoreType.DMA((count,)),
+            pltpu.SemaphoreType.DMA((count, steps, 2)),
+            pltpu.SemaphoreType.DMA((count, steps, 2)),
+            pltpu.SemaphoreType.DMA((count, 1 + 2 * steps)),
+            pltpu.SemaphoreType.DMA((count, 1 + 2 * steps)),
+            pltpu.SemaphoreType.DMA,
+            pltpu.SemaphoreType.DMA,
+        ],
+        compiler_params=pltpu.CompilerParams(collective_id=1, has_side_effects=True),
+        name="gather",
+    )(gains, wq, wo, wu, wd, rows)
+
+
+def reduce_kernel(
+    wide,
+    act_t,
+    second_t,
+    heads_t,
+    normed_t,
+    d_mlp,
+    d_pre,
+    d_attend,
+    d_project,
+    small,
+    rows,
+    o_qkv,
+    o_out,
+    o_up,
+    o_down,
+    o_small,
+    rows_got,
+    own,
+    to_sib,
+    mine,
+    moving,
+    x_out,
+    x_in,
+    small_acc,
+    small_in,
+    sib_send,
+    sib_recv,
+    ring_send,
+    ring_recv,
+    x_send,
+    x_recv,
+    small_send,
+    small_recv,
+    row_send,
+    row_recv,
+):
+    at = Place(wide)
+    ring, steps = at.ring, at.ring // 2
+    depth, width = o_out.shape
+    half = depth // 2
+    ups, downs = o_up.shape[1] // width, o_down.shape[0] // depth
+    rows_in = d_mlp.shape[0]
+    count = downs + ups + 1 + 3
+    tile = 256
+
+    def operands(k):
+        if k < downs:
+            return lambda core: act_t[:, core, k], d_mlp, 0
+        k -= downs
+        if k < ups:
+            return lambda core: second_t[:, core], d_pre, k * width
+        k -= ups
+        if k < 1:
+            return lambda core: heads_t[:, core], d_attend, 0
+        return lambda core: normed_t[:, core], d_project, (k - 1) * width
+
+    def product(k, core, put):
+        left, right, first = operands(k)
+        tall = left(core).reshape(ring * depth, rows_in)
+
+        @pl.loop(0, width // tile)
+        def _(t):
+            cols = pl.ds(pl.multiple_of(t * tile, tile), tile)
+            from_cols = pl.ds(pl.multiple_of(first + t * tile, tile), tile)
+            put(cols, dot(tall, right[:, from_cols]).reshape(ring, depth, tile))
+
+    def store(k):
+        if k < downs:
+            return o_down, k * depth, 0
+        k -= downs
+        if k < ups:
+            return o_up, 0, k * width
+        k -= ups
+        if k < 1:
+            return o_out, 0, 0
+        return o_qkv, 0, (k - 1) * width
+
+    def sib(k):
+        return remote(
+            to_sib.at[k % 2], mine.at[k], sib_send.at[k], sib_recv.at[k], at.sibling()
+        )
+
+    def halves(d):
+        return pl.ds(d * half, half)
+
+    def ring_out(k, t, d):
+        to = at.at_ring(at.r + 1 if d == 0 else at.r - 1)
+        if t == 0:
+            src = mine.at[k, at.chip(at.r + steps), halves(d)]
+            dst = moving.at[k, 0, d, halves(d)]
+        else:
+            src = moving.at[k, t - 1, d]
+            dst = moving.at[k, t, d]
+        return remote(src, dst, ring_send.at[k, t, d], ring_recv.at[k, t, d], to)
+
+    def ring_in(k, t, d):
+        to = at.at_ring(at.r + 1 if d == 0 else at.r - 1)
+        ref = moving.at[k, 0, d, halves(d)] if t == 0 else moving.at[k, t, d]
+        return remote(ref, ref, ring_send.at[k, t, d], ring_recv.at[k, t, d], to)
+
+    def cross(k):
+        return remote(x_out.at[k], x_in.at[k], x_send.at[k], x_recv.at[k], at.across())
+
+    bits = [1 << b for b in range(ring.bit_length() - 1)]
+    partners = [at.sibling(), at.across()] + [at.flipped(bit) for bit in bits]
+    stages = len(partners)
+
+    def small_copy(j):
+        return remote(
+            small_acc.at[j], small_in.at[j], small_send.at[j], small_recv.at[j], partners[j]
+        )
+
+    greet(partners + [at.at_ring(at.r + 1), at.at_ring(at.r - 1)])
+    rows_copy = remote(rows, rows_got, row_send, row_recv, at.across())
+    rows_copy.start()
+    small_acc[0] = small[...]
+    step = 16
+
+    for i in range(count + steps + 3):
+        k = i
+        if k < count:
+            if k >= 2:
+                sib(k - 2).wait_send()
+
+            def keep_other(cols, value):
+                to_sib[k % 2, :, :, cols] = value.astype(BF16)
+
+            def keep_own(cols, value):
+                own[k % 2, :, :, cols] = value
+
+            product(k, 1 - at.c, keep_other)
+            sib(k).start()
+            product(k, at.c, keep_own)
+        if i <= stages:
+            if i > 0:
+                small_copy(i - 1).wait_recv()
+                small_acc[i] = small_acc[i - 1] + small_in[i - 1]
+            if i < stages:
+                small_copy(i).start()
+            else:
+                o_small[...] = small_acc[stages]
+        k = i - 1
+        if 0 <= k < count:
+            sib(k).wait_recv()
+
+            @pl.loop(0, ring)
+            def _(chip):
+                mine[k, chip] = (mine[k, chip].astype(F32) + own[k % 2, chip]).astype(BF16)
+
+            for d in (0, 1):
+                ring_out(k, 0, d).start()
+        for t in range(1, steps):
+            k = i - 1 - t
+            if 0 <= k < count:
+                for d in (0, 1):
+                    ring_in(k, t - 1, d).wait_recv()
+                    dest = at.chip(at.r + (steps - t) if d == 0 else at.r - (steps - t))
+                    lows = range(0, depth, half) if t == 1 else (0,)
+                    for low in lows:
+                        size = half if t == 1 else depth
+
+                        @pl.loop(0, size // step)
+                        def _(g):
+                            take = pl.ds(pl.multiple_of(low + g * step, step), step)
+                            value = mine[k, dest, take]
+                            if not (t == 1 and low != d * half):
+                                value = (
+                                    value.astype(F32) + moving[k, t - 1, d, take].astype(F32)
+                                ).astype(BF16)
+                            moving[k, t - 1, d, take] = value
+
+                    ring_out(k, t, d).start()
+        k = i - 1 - steps
+        if 0 <= k < count:
+            for d in (0, 1):
+                ring_in(k, steps - 1, d).wait_recv()
+
+            @pl.loop(0, depth // step)
+            def _(g):
+                take = pl.ds(pl.multiple_of(g * step, step), step)
+                value = mine[k, at.q, take].astype(F32)
+                value = value + moving[k, steps - 1, 0, take].astype(F32)
+                value = value + moving[k, steps - 1, 1, take].astype(F32)
+                x_out[k, take] = value.astype(BF16)
+
+            cross(k).start()
+        k = i - 2 - steps
+        if 0 <= k < count:
+            cross(k).wait_recv()
+            out, low, first = store(k)
+
+            @pl.loop(0, depth // step)
+            def _(g):
+                take = pl.ds(pl.multiple_of(g * step, step), step)
+                put = pl.ds(pl.multiple_of(low + g * step, step), step)
+                out[put, first : first + width] = x_out[k, take].astype(F32) + x_in[
+                    k, take
+                ].astype(F32)
+
+    for k in range(count):
+        if k >= count - 2:
+            sib(k).wait_send()
+        cross(k).wait_send()
+        for t in range(steps):
+            for d in (0, 1):
+                ring_out(k, t, d).wait_send()
+    for j in range(stages):
+        small_copy(j).wait_send()
+    rows_copy.wait()
+
+
+def reduce_grads(
+    wide, act_low, second_low, heads_low, normed_low, d_mlp, d_pre, d_attend, d_project, small, rows
+):
+    width = normed_low.shape[1]
+    ring, steps = wide // 2, wide // 4
+    depth = width // wide
+    tokens_in = normed_low.shape[0]
+
+    def tall(value):
+        return value.T.reshape(ring, 2, depth, tokens_in)
+
+    ff = act_low.shape[1]
+    downs = ff // width
+    act_t = act_low.T.reshape(ring, 2, downs, depth, tokens_in)
+    count = 2 * downs + 4
+    stages = 2 + (ring.bit_length() - 1)
+    vmem = pl.BlockSpec(memory_space=pltpu.VMEM)
+    anywhere = pl.BlockSpec(memory_space=pl.ANY)
+    dma = pltpu.SemaphoreType.DMA
+    return pl.pallas_call(
+        functools.partial(reduce_kernel, wide),
+        out_shape=[
+            jax.ShapeDtypeStruct((depth, 3 * width), F32),
+            jax.ShapeDtypeStruct((depth, width), F32),
+            jax.ShapeDtypeStruct((depth, ff), F32),
+            jax.ShapeDtypeStruct((ff // wide, width), F32),
+            jax.ShapeDtypeStruct(small.shape, F32),
+            jax.ShapeDtypeStruct(rows.shape, rows.dtype),
+        ],
+        in_specs=[vmem] * 9 + [anywhere],
+        out_specs=[vmem] * 5 + [anywhere],
+        scratch_shapes=[
+            pltpu.VMEM((2, ring, depth, width), F32),
+            pltpu.VMEM((2, ring, depth, width), BF16),
+            pltpu.VMEM((count, ring, depth, width), BF16),
+            pltpu.VMEM((count, steps, 2, depth, width), BF16),
+            pltpu.VMEM((count, depth, width), BF16),
+            pltpu.VMEM((count, depth, width), BF16),
+            pltpu.VMEM((stages + 1,) + small.shape, F32),
+            pltpu.VMEM((stages,) + small.shape, F32),
+            dma((count,)),
+            dma((count,)),
+            dma((count, steps, 2)),
+            dma((count, steps, 2)),
+            dma((count,)),
+            dma((count,)),
+            dma((stages,)),
+            dma((stages,)),
+            dma,
+            dma,
+        ],
+        compiler_params=pltpu.CompilerParams(
+            collective_id=2, has_side_effects=True, vmem_limit_bytes=60 * 1024 * 1024
+        ),
+        name="reduce",
+    )(
+        act_t,
+        tall(second_low),
+        tall(heads_low),
+        tall(normed_low),
+        d_mlp,
+        d_pre,
+        d_attend,
+        d_project,
+        small,
+        rows,
+    )
+
+
+def probabilities(count, queries, keys):
+    entries = queries.shape[0]
+    scores = dot_nt(queries, keys) * 0.125
+    q_at = lax.broadcasted_iota(jnp.int32, (entries, entries), 0)
+    k_at = lax.broadcasted_iota(jnp.int32, (entries, entries), 1)
+    scores = jnp.where((k_at <= q_at) & (k_at < count), scores, masked_score)
+    expo = jnp.exp(scores - jnp.max(scores, axis=-1, keepdims=True))
+    return expo / jnp.sum(expo, axis=-1, keepdims=True)
+
+
+def only(value, head):
+    lane = lax.broadcasted_iota(jnp.int32, value.shape, 1)
+    return jnp.where(lane // HEAD_DIM == head, value, jnp.zeros_like(value))
+
+
+def attend_kernel(count, q, k, v, out):
+    total = jnp.zeros(out.shape, F32)
+    for head in (0, 1):
+        probs = probabilities(count[0], only(q[...], head), k[...])
+        total = total + only(dot(probs.astype(BF16), v[...]), head)
+    out[...] = total.astype(BF16)
+
+
+def attend_back_kernel(count, q, k, v, d_heads, d_project):
+    d_q = jnp.zeros(q.shape, F32)
+    d_k = jnp.zeros(q.shape, F32)
+    d_v = jnp.zeros(q.shape, F32)
+    for head in (0, 1):
+        probs = probabilities(count[0], only(q[...], head), k[...])
+        d_own = only(d_heads[...], head)
+        d_probs = dot_nt(d_own, v[...])
+        d_scores = probs * (d_probs - jnp.sum(probs * d_probs, axis=-1, keepdims=True))
+        d_scores = d_scores.astype(BF16)
+        d_q = d_q + only(dot(d_scores, k[...]), head)
+        d_k = d_k + only(dot_tn(d_scores, q[...]), head)
+        d_v = d_v + dot_tn(probs.astype(BF16), d_own)
+    d_project[0] = (d_q * 0.125).astype(BF16)
+    d_project[1] = (d_k * 0.125).astype(BF16)
+    d_project[2] = d_v.astype(BF16)
+
+
+def attend(count, project):
+    entries = project.shape[0]
+    width = project.shape[1] // 3
+    pairs = width // (2 * HEAD_DIM)
+
+    def third(j):
+        return pl.BlockSpec((entries, 2 * HEAD_DIM), lambda p: (0, j * pairs + p))
+
+    return pl.pallas_call(
+        attend_kernel,
+        grid=(pairs,),
+        out_shape=jax.ShapeDtypeStruct((entries, width), BF16),
+        in_specs=[pl.BlockSpec(memory_space=pltpu.SMEM), third(0), third(1), third(2)],
+        out_specs=third(0),
+        name="attend",
+    )(count, project, project, project)
+
+
+def attend_back(count, project, d_heads):
+    entries = project.shape[0]
+    width = project.shape[1] // 3
+    pairs = width // (2 * HEAD_DIM)
+
+    def third(j):
+        return pl.BlockSpec((entries, 2 * HEAD_DIM), lambda p: (0, j * pairs + p))
+
+    return pl.pallas_call(
+        attend_back_kernel,
+        grid=(pairs,),
+        out_shape=jax.ShapeDtypeStruct((3, entries, width), BF16),
+        in_specs=[pl.BlockSpec(memory_space=pltpu.SMEM), third(0), third(1), third(2), third(0)],
+        out_specs=pl.BlockSpec((3, entries, 2 * HEAD_DIM), lambda p: (0, 0, p)),
+        name="attend_back",
+    )(count, project, project, project, d_heads)
+
+
+def paired_body(
+    wide, tokens, cotangent, lengths, routes, w_qkv, w_out, w_up, w_down, gain_attn, gain_mlp, router
+):
+    place = lax.axis_index("narrow")
+    seqs, span, width = tokens.shape
+    list_len = routes.shape[1]
+    depth = gain_attn.shape[0]
+    counts = lengths // 8
+    entry = jnp.arange(list_len, dtype=jnp.int32)
+    live = entry[None, :] < counts[:, None]
+    local_slot = jnp.where(live, routes - place * span, -1)
+    spots = jnp.arange(span, dtype=jnp.int32)
+    chosen = (local_slot[:, :, None] == spots[None, None, :]).astype(BF16)
+
+    def take(source):
+        return jnp.einsum("sep,spd->sed", chosen, source, preferred_element_type=F32).astype(BF16)
+
+    picked = jnp.stack([take(tokens), take(cotangent)])
+    kept = lax.dynamic_index_in_dim(picked, place, 1, keepdims=False)
+    given = lax.dynamic_index_in_dim(picked, 1 - place, 1, keepdims=False)
+    gains = jnp.concatenate([gain_attn, gain_mlp]).reshape(1, 2 * depth)
+    gains = jnp.pad(gains, ((0, 15), (0, 0)))
+    gains_all, weight_qkv, weight_out, weight_up, weight_down, got = gather_weights(
+        wide, gains, w_qkv, w_out, w_up, w_down, given
+    )
+    gains_all = gains_all.reshape(wide, 16, 2 * depth)[:, 0]
+    scale_first = gains_all[:, :depth].reshape(width).astype(F32)
+    scale_second = gains_all[:, depth:].reshape(width).astype(F32)
+    both = kept + got
+    inputs_low = both[0]
+    inputs_rows = inputs_low.astype(F32)
+    dout = both[1].astype(F32)
+    count = lax.dynamic_slice_in_dim(counts, place, 1)
+
+    normed_one, inverse_one = rms_parts(inputs_rows)
+    normed_low = (normed_one * scale_first).astype(BF16)
+    project = dot(normed_low, weight_qkv).astype(BF16)
+    heads_low = attend(count, project)
+    attend_out = dot(heads_low, weight_out)
+    middle = inputs_rows + attend_out
+    normed_two, inverse_two = rms_parts(middle)
+    second_low = (normed_two * scale_second).astype(BF16)
+    pre_act = dot(second_low, weight_up)
+    activ_full, gelu_back = jax.vjp(jax.nn.gelu, pre_act)
+    activ_low = activ_full.astype(BF16)
+    mlp_out = dot(activ_low, weight_down)
+    branch = attend_out + mlp_out
+    router_row = router.astype(F32)[None, :]
+    router_val = jnp.sum(inputs_rows * router_row, axis=-1, keepdims=True)
+    out_low = (inputs_rows + router_val * branch).astype(BF16)
+
+    d_branch = router_val * dout
+    d_router_val = jnp.sum(dout * branch, axis=-1, keepdims=True)
+    d_mlp = d_branch.astype(BF16)
+    d_act = dot_nt(d_mlp, weight_down)
+    d_pre = gelu_back(d_act)[0].astype(BF16)
+    d_normed_two = dot_nt(d_pre, weight_up)
+    grad_gain_two = jnp.sum(d_normed_two * normed_two, axis=0)
+    d_middle = rms_back(d_normed_two * scale_second, normed_two, inverse_two)
+    d_attend = (d_branch + d_middle).astype(BF16)
+    d_heads = dot_nt(d_attend, weight_out).astype(BF16)
+    d_parts = attend_back(count, project, d_heads)
+    d_project = jnp.concatenate([d_parts[0], d_parts[1], d_parts[2]], axis=1)
+    d_normed = dot_nt(d_project, weight_qkv)
+    grad_gain_one = jnp.sum(d_normed * normed_one, axis=0)
+    d_norm_rows = rms_back(d_normed * scale_first, normed_one, inverse_one)
+    d_rows = dout + d_middle + d_norm_rows + d_router_val * router_row
+    grad_router = jnp.sum(d_router_val * inputs_rows, axis=0)
+    grad_low = d_rows.astype(BF16)
+
+    small = jnp.pad(jnp.stack([grad_gain_one, grad_gain_two, grad_router]), ((0, 5), (0, 0)))
+    back = jnp.stack([out_low, grad_low])
+    grad_qkv, grad_out, grad_up, grad_down, small, back_got = reduce_grads(
+        wide,
+        activ_low,
+        second_low,
+        heads_low,
+        normed_low,
+        d_mlp,
+        d_pre,
+        d_attend,
+        d_project,
+        small,
+        back,
+    )
+    first = place == 0
+    rows_out = jnp.stack([jnp.where(first, back, back_got), jnp.where(first, back_got, back)], axis=1)
+    hit = jnp.any(local_slot[:, :, None] == spots[None, None, :], axis=1)
+
+    def put(base, fresh):
+        spread = jnp.einsum("sep,sed->spd", chosen, fresh, preferred_element_type=F32)
+        return jnp.where(hit[:, :, None], spread.astype(BF16), base)
+
+    start = lax.axis_index("wide") * depth
+    return (
+        put(tokens, rows_out[0]),
+        put(cotangent, rows_out[1]),
+        grad_qkv,
+        grad_out,
+        grad_up,
+        grad_down,
+        lax.dynamic_slice_in_dim(small[0], start, depth),
+        lax.dynamic_slice_in_dim(small[1], start, depth),
+        small[2],
+    )
+
+
+def body(wide, narrow, tokens, *others):
+    if narrow == 2 and tokens.shape[0] == 2 and wide >= 8 and wide & (wide - 1) == 0:
+        return paired_body(wide, tokens, *others)
+    return general_body(tokens, *others)
+
+
 def solution(mesh):
     in_specs = (
         P("wide", "narrow", None),
@@ -243,4 +905,5 @@
         P("wide"),
         P(),
     )
-    return jax.shard_map(body, mesh=mesh, in_specs=in_specs, out_specs=out_specs, check_vma=False)
+    sizes = mesh.shape["wide"], mesh.shape["narrow"]
+    return jax.shard_map(functools.partial(body, *sizes), mesh=mesh, in_specs=in_specs, out_specs=out_specs, check_vma=False)

time: 1290 us -> 403 us (0.31)
  waiting for transfers between devices: 835 us -> 0 us
  Pallas kernels: 0 us -> 314 us
  local copies, waits for them, and re-layouts: 208 us -> 17.9 us
  blocking collectives: 108 us -> 0 us
  matrix products: 91.4 us -> 51.4 us
  between operations: 17.9 us -> 1.35 us
    reduce_scatter x8 -> x0, waiting for transfers between devices: 588 us -> none  [the longest x1 182 us: body(): lax.psum_scatter(grad_up_full, 'wide', scatter_dimension=0, tiled=True)]
    pallas_call x0 -> x4, Pallas kernels: none -> 314 us  [the longest x1 160 us: reduce_grads(): pl.pallas_call(functools.partial(reduce_kernel, wide), out_shape=[jax.Sha...]
    all_gather x8 -> x0, waiting for transfers between devices: 243 us -> none  [the longest x1 72.4 us: body(): lax.all_gather(w_down, 'wide', axis=0, tiled=True)]
    scatter x2 -> x0, local copies, waits for them, and re-layouts: 137 us -> none  [body(): base.at[where_to].set(fresh, mode='drop')]
    unnamed x2 -> x0, blocking collectives: 63.4 us -> none
    psum x2 -> x0, blocking collectives: 44.9 us -> none  [the longest x1 39.4 us: body(): grad_router = lax.psum(grad_router_part, ('wide', 'narrow'))]
    dot_general x20 -> x12, matrix products: 91.4 us -> 51.4 us  [the longest x4 22.7 us: dot(): return jnp.dot(left, right, preferred_element_type=F32)]
    gather x2 -> x0, local copies, waits for them, and re-layouts: 36.5 us -> none  [the longest x1 18.2 us: body(): taken_cot = jnp.take_along_axis(cotangent, pick[:, :, None], axis=1)]
  transfers between devices with their start and end apart: 17 -> 0, of which waited for: 12 -> 0; matrix products, arithmetic and copies ran while one was open for 17% -> 0% of each run, Pallas kernels for 0% -> 0%
where the time goes in v1:
time: 403 us; the launch traced here: 396 us
  Pallas kernels  314 us (78%)
  matrix products  51.4 us (13%)
  local copies, waits for them, and re-layouts  17.9 us (4%)
  other arithmetic  11.6 us (3%)
    pallas_call x1, Pallas kernels, reduce_grads(): pl.pallas_call(functools.partial(reduce_kernel, wide), out_shape=[jax.Sha...  160 us
    pallas_call x1, Pallas kernels, gather_weights(): pl.pallas_call(functools.partial(gather_kernel, wide), out_shape=full + [...  131 us
    dot_general x4, matrix products, dot(): return jnp.dot(left, right, preferred_element_type=F32)  22.7 us
    dot_general x4, matrix products, dot_nt(): lax.dot_general(left, right, (((1,), (1,)), ((), ())), preferred_element_...  17.6 us
    pallas_call x1, Pallas kernels, attend_back(): pl.pallas_call(attend_back_kernel, grid=(pairs,), out_shape=jax.ShapeDtyp...  12.6 us
    pallas_call x1, Pallas kernels, attend(): pl.pallas_call(attend_kernel, grid=(pairs,), out_shape=jax.ShapeDtypeStru...  9.95 us

profile of v1, /device:TPU:0, one launch (start us, length us, event | category | flops | bytes accessed | tf_op | source)
XLA Modules:
  0.0 395.8 jit_solution(4972450746856106256)
XLA Ops:
  0.6 0.0 copy-start.15
  0.7 0.8 and_select_fusion
  1.5 0.9 compare_select_fusion
  2.4 3.5 fusion.29
  5.9 0.0 copy-done.15
  5.9 0.0 copy-start.17
  5.9 0.0 copy-start.18
  5.9 1.3 fusion.30
  7.2 1.1 fusion.52.rows
  8.3 0.1 maximum_bitcast_fusion
  8.4 0.6 pad.8.gains
  9.0 131.2 %gather.1 = (bf16[256,128]{1,0:T(8,128)(2,1)}, bf16[1024,3072]{1,0:T(8,128)(2,1)}, bf16[1024,1024]{1,0:T(8,128)(2,1)}, bf16[1024,4096]{1,0:T(8,128)(2,1)}, bf16[...) custom-call(bf16[16,128]{1,0:T(8,128)(2,1)} %pad.8.gains, bf16[64,3072]{1,0:T(8,128)(2,1)} %wq.1, ...), custom_call_target="tpu_custom_call" | custom-call | tf_op jit(solution)/shard_map/gather/pallas_call | solution.py:393
  140.2 1.4 fusion.55
  141.6 0.2 fusion.48
  141.8 0.8 slice.53
  142.6 0.1 slice_convert_fusion
  142.6 0.1 reshape.95
  142.7 5.8 %convolution_convert_fusion.q.k.v = bf16[256,3072]{1,0:T(8,128)(2,1)} fusion(bf16[1024,3072]{1,0:T(8,128)(2,1)} %get-tuple-element.23, f32[1024]{0:T(1024)S(1)} %reshape.95, f32[256]{0:T(256)S(1)} %add_rsqrt_fusion.1, bf16[2,256,1024]{2,1,0:T(8,128)(2,1)S(1)} %fusion.55), kind=kOutput, calls=%fused_computation.21 | convolution fusion | flops 1612447744 | bytes 8393728 | tf_op jit(solution)/shard_map/dot_general | solution.py:228
  148.5 0.6 dynamic_slice.22.count
  149.1 10.0 %attend.1 = bf16[256,1024]{1,0:T(8,128)(2,1)} custom-call(s32[1]{0:T(128)} %dynamic_slice.22.count, bf16[256,3072]{1,0:T(8,128)(2,1)} %convolution_convert_fusion.q.k.v, bf16[256,3072]{1,0:T(8,128)(2,1)} %convolution_convert_fusion.q.k.v, bf16[256,3072]{1,0:T(8,128)(2,1)} %convolution_convert_fusion.q.k.v), custom_call_target="tpu_custom_call" | custom-call | tf_op jit(solution)/shard_map/attend/pallas_call | solution.py:742
  159.1 2.6 multiply_reduce_fusion.2
  161.7 0.1 reshape.96
  161.7 8.0 %fusion.14 = (bf16[4096,256]{0,1:T(8,128)(2,1)}, f32[256,4096]{1,0:T(8,128)S(1)}) fusion(bf16[1024,4096]{1,0:T(8,128)(2,1)} %get-tuple-element.25, f32[256,1024]{1,0:T(8,128)S(1)} %get-tuple-element.41, f32[1024]{0:T(1024)S(1)} %reshape.96, f32[256]{0:T(256)S(1)} %add_rsqrt_fusion), kind=kOutput, calls=%fused_computation.17 | convolution fusion | flops 2157707264 | bytes 15733760 | tf_op jit(solution)/shard_map/dot_general | solution.py:228
  169.8 6.3 %fusion.38 = (f32[256]{0:T(256)S(1)}, f32[256]{0:T(256)S(1)}, f32[256,1024]{1,0:T(8,128)S(1)}) fusion(bf16[2,256,1024]{2,1,0:T(8,128)(2,1)S(1)} %fusion.55, f32[1024]{0:T(1024)S(1)} %convert_element_type.89, f32[256,1024]{1,0:T(8,128)S(1)} %get-tuple-element.57, bf16[4096,1024]{1,0:T(8,128)(2,1)} %get-tuple-element.26, f32[256,4096]{1,0:T(8,128)S(1)} %get-tuple-element.59), kind=kOutput, calls=%fused_computation.63 | convolution fusion | flops 2158755328 | bytes 15734784 | tf_op jit(solution)/shard_map/dot_general | solution.py:228
  176.1 0.3 fusion.63
  176.4 0.0 copy-start.7
  176.4 0.0 slice-start.1
  176.4 8.3 %fusion.6.d_pre = bf16[256,4096]{1,0:T(8,128)(2,1)S(1)} fusion(f32[256,4096]{1,0:T(8,128)S(1)} %get-tuple-element.59, bf16[256,1024]{1,0:T(8,128)(2,1)S(1)} %get-tuple-element.51.d_mlp, bf16[4096,1024]{1,0:T(8,128)(2,1)} %get-tuple-element.26), kind=kOutput, calls=%fused_computation.9 | convolution fusion | flops 2168455168 | bytes 15204352 | tf_op jit(solution)/shard_map/dot_general | solution.py:232
  184.7 0.0 copy-done.7
  184.7 0.0 slice-done
  184.7 0.0 slice-done.1
  184.8 2.8 multiply_reduce_fusion
  187.6 0.0 copy-start.1
  187.6 0.9 copy-done.1
  188.6 0.4 fusion.34.d_attend
  188.9 0.0 copy-done.6
  189.0 0.0 copy-start.3
  189.0 1.5 convolution_convert_fusion.1.d_heads
  190.5 12.6 %attend_back.1 = bf16[3,256,1024]{2,1,0:T(8,128)(2,1)} custom-call(s32[1]{0:T(128)} %dynamic_slice.22.count, bf16[256,3072]{1,0:T(8,128)(2,1)} %convolution_convert_fusion.q.k.v, bf16[256,3072]{1,0:T(8,128)(2,1)} %convolution_convert_fusion.q.k.v, bf16[256,3072]{1,0:T(8,128)(2,1)} %convolution_convert_fusion.q.k.v, ...), custom_call_target="tpu_custom_call" | custom-call | tf_op jit(solution)/shard_map/attend_back/pallas_call | solution.py:760
  203.1 1.5 slice_bitcast_fusion.2
  204.5 0.0 copy-start.2
  204.5 5.0 %fusion.40 = (f32[256]{0:T(256)S(1)}, f32[1024]{0:T(1024)S(1)}, f32[1024]{0:T(1024)S(1)}, f32[256,1024]{1,0:T(8,128)S(1)}) fusion(f32[1024]{0:T(1024)S(1)} %reshape.95, f32[256]{0:T(256)S(1)} %add_rsqrt_fusion.1, bf16[2,256,1024]{2,1,0:T(8,128)(2,1)S(1)} %fusion.55, f32[256]{0:T(256)S(1)} %get-tuple-element.38, bf16[1024,3072]{1,0:T(8,128)(2,1)} %get-tuple-element.23, ...), kind=kOutput, calls=%fused_computation.65 | convolution fusion | flops 1617688320 | bytes 9452544 | tf_op jit(solution)/shard_map/dot_general | solution.py:232
  209.5 1.6 fusion.64
  211.2 1.1 pad_maximum_fusion.2.rows
  212.3 0.6 select_maximum_fusion.small
  212.9 1.2 pad_maximum_fusion.d_project
  214.1 1.0 copy.30
  215.1 0.0 copy-done.4
  215.1 1.0 copy.32
  216.1 4.1 %copy.29 = bf16[4096,256]{1,0:T(8,128)(2,1)} copy(bf16[4096,256]{0,1:T(8,128)(2,1)} %get-tuple-element.58) | data formatting | bytes 4194304 | tf_op jit(solution)/shard_map/convert_element_type | solution.py:814
  220.2 1.0 copy.31
  221.2 159.8 %reduce.1 = (f32[64,3072]{1,0:T(8,128)}, f32[64,1024]{1,0:T(8,128)}, f32[64,4096]{1,0:T(8,128)}, f32[256,1024]{1,0:T(8,128)}, f32[8,1024]{1,0:T(8,128)}, /*index=5*/bf16[2,256,1024]{2,1,0:T(8,128)(2,1)}) custom-call(bf16[8,2,4,64,256]{4,3,2,1,0:T(8,128)(2,1)} %bitcast.105, bf16[8,2,64,256]{3,2,1,0:T(8,128)(2,1)} %bitcast.107, ...), custom_call_target="tpu_custom_call" | custom-call | tf_op jit(solution)/shard_map/reduce/pallas_call | solution.py:643
  381.1 1.5 fusion.78
  382.5 0.6 fusion.67
  383.1 1.5 select_bitcast_fusion
  384.6 0.4 fusion.22
  385.0 0.6 copy-done.14
  385.6 3.1 convert_select_fusion
  388.7 3.1 convert_select_fusion.1
  391.9 0.0 copy-done.11
  391.9 0.9 copy.42
  392.7 0.7 copy.43
  393.4 1.0 copy.44
  394.4 1.0 copy.45
  (32 shorter events, 0.1 us)
Async XLA Ops:
  0.6 5.2 %copy-start.15 = (bf16[2,1024,1024]{2,1,0:T(8,128)(2,1)S(1)}, bf16[2,1024,1024]{2,1,0:T(8,128)(2,1)}, u32[]{:S(2)}) copy-start(bf16[2,1024,1024]{2,1,0:T(8,128)(2,1)} %param.11) | copy-start | bytes 12582916
  5.9 2.4 copy-start.17
  5.9 2.4 copy-start.18
  161.7 8.0 %copy-start.13 = (bf16[1024]{0:T(1024)(128)(2,1)S(1)}, bf16[1024]{0:T(1024)(128)(2,1)}, u32[]{:S(2)}) copy-start(bf16[1024]{0:T(1024)(128)(2,1)} %param.21) | copy-start | bytes 6148
  176.1 8.6 %slice-start = ((s8[8388608]{0:T(1024)(128)(4,1)}), s8[4194304]{0:T(1024)(128)(4,1)S(1)}, s32[]{:S(2)}) async-start(s8[8388608]{0:T(1024)(128)(4,1)} %bitcast.116), calls=%async_computation | async-start | bytes 8388608
  176.4 8.3 %copy-start.7 = (bf16[256,1024]{1,0:T(8,128)(2,1)}, bf16[256,1024]{1,0:T(8,128)(2,1)S(1)}, u32[]{:S(2)}) copy-start(bf16[256,1024]{1,0:T(8,128)(2,1)S(1)} %get-tuple-element.51.d_mlp) | copy-start | bytes 1572868
  176.4 8.3 %slice-start.1 = ((s8[8388608]{0:T(1024)(128)(4,1)}), s8[4194304]{0:T(1024)(128)(4,1)S(1)}, s32[]{:S(2)}) async-start(s8[8388608]{0:T(1024)(128)(4,1)} %bitcast.116), calls=%async_computation.1 | async-start | bytes 8388608
  184.7 2.9 copy-start.8
  184.8 4.2 %copy-start.6 = (bf16[1024,1024]{1,0:T(8,128)(2,1)S(1)}, bf16[1024,1024]{1,0:T(8,128)(2,1)}, u32[]{:S(2)}) copy-start(bf16[1024,1024]{1,0:T(8,128)(2,1)} %get-tuple-element.24) | copy-start | bytes 6291460
  187.6 1.0 copy-start.1
  189.0 14.1 %copy-start.3 = (bf16[256,1024]{1,0:T(8,128)(2,1)}, bf16[256,1024]{1,0:T(8,128)(2,1)S(1)}, u32[]{:S(2)}) copy-start(bf16[256,1024]{1,0:T(8,128)(2,1)S(1)} %fusion.34.d_attend) | copy-start | bytes 1572868
  204.5 5.0 %copy-start.2 = (f32[256,1024]{1,0:T(8,128)S(1)}, f32[256,1024]{1,0:T(8,128)}, u32[]{:S(2)}) copy-start(f32[256,1024]{1,0:T(8,128)} %copy-done.1) | copy-start | bytes 3145732
  211.2 3.0 copy-start.5
  211.2 4.0 copy-start.4
  212.9 7.3 %copy-start = (bf16[256,1024]{1,0:T(8,128)(2,1)S(1)}, bf16[256,1024]{1,0:T(8,128)(2,1)}, u32[]{:S(2)}) copy-start(bf16[256,1024]{1,0:T(8,128)(2,1)} %attend.1) | copy-start | bytes 1572868
  383.1 2.5 copy-start.14
  385.6 3.1 copy-start.16
  388.7 3.1 copy-start.11
  388.7 4.0 %copy-start.12 = (f32[64,1024]{1,0:T(8,128)S(1)}, f32[64,1024]{1,0:T(8,128)}, u32[]{:S(2)}) copy-start(f32[64,1024]{1,0:T(8,128)} %get-tuple-element.77) | copy-start | bytes 786436
  388.7 4.7 %copy-start.10 = (f32[64,4096]{1,0:T(8,128)S(1)}, f32[64,4096]{1,0:T(8,128)}, u32[]{:S(2)}) copy-start(f32[64,4096]{1,0:T(8,128)} %get-tuple-element.78) | copy-start | bytes 3145732
  391.9 2.6 copy-start.9

commit v2 on v1

--- a/solution.py
+++ b/solution.py
@@ -280,20 +280,70 @@
     )
 
 
-def gather_kernel(
+def probabilities(live, queries, keys):
+    entries = queries.shape[0]
+    scores = dot_nt(queries, keys) * 0.125
+    q_at = lax.broadcasted_iota(jnp.int32, (entries, entries), 0)
+    k_at = lax.broadcasted_iota(jnp.int32, (entries, entries), 1)
+    scores = jnp.where((k_at <= q_at) & (live > 0), scores, masked_score)
+    expo = jnp.exp(scores - jnp.max(scores, axis=-1, keepdims=True))
+    return expo / jnp.sum(expo, axis=-1, keepdims=True)
+
+
+def only(value, head):
+    lane = lax.broadcasted_iota(jnp.int32, value.shape, 1)
+    return jnp.where(lane // HEAD_DIM == head, value, jnp.zeros_like(value))
+
+
+def gelu_pair(x):
+    inner = 0.7978845608028654 * (x + 0.044715 * (x * x * x))
+    bent = jnp.tanh(inner)
+    half = 0.5 * (1.0 + bent)
+    slope = 0.7978845608028654 * (1.0 + 0.134145 * (x * x))
+    return x * half, half + 0.5 * x * (1.0 - bent * bent) * slope
+
+
+def forward_kernel(
     wide,
     gains,
     wq,
     wo,
     wu,
     wd,
-    rows,
-    gains_all,
+    kept,
+    given,
+    router,
+    live,
     wq_all,
     wo_all,
+    normed_t,
+    heads_t,
+    second_t,
+    act_t,
+    d_pre,
+    d_mlp,
+    d_attend,
+    project,
+    base,
+    out_low,
+    rows_low,
+    small,
+    scales,
     wu_all,
     wd_all,
-    rows_got,
+    gains_all,
+    got,
+    normed,
+    heads,
+    attend_out,
+    second_n,
+    second,
+    d_act,
+    act,
+    mlp_out,
+    d_second,
+    router_val,
+    inverse_two,
     own_sem,
     ring_send,
     ring_recv,
@@ -301,112 +351,333 @@
     sib_recv,
     x_send,
     x_recv,
+    row_send,
+    row_recv,
 ):
     at = Place(wide)
     ring, steps = at.ring, at.ring // 2
-    depth = wo.shape[0]
-    width = wo.shape[1]
-    parts = [(gains, gains_all, gains.shape[0], 0, gains.shape[0], 0, gains.shape[1])]
-    parts += [(wq, wq_all, depth, 0, depth, j * width, width) for j in range(3)]
-    parts += [(wo, wo_all, depth, 0, depth, 0, width)]
-    parts += [(wu, wu_all, depth, 0, depth, j * width, width) for j in range(wu.shape[1] // width)]
-    parts += [
-        (wd, wd_all, wd.shape[0], j * depth, depth, 0, width) for j in range(wd.shape[0] // depth)
-    ]
-
-    def block(k, ring_pos, core, half, own):
-        src, dst, shard, first, taken, col, cols = parts[k]
-        size = taken if half is None else taken // 2
-        low = first + (0 if half is None else half * size)
-        if own:
-            return src.at[pl.ds(low, size), pl.ds(col, cols)]
-        base = (at.chip(ring_pos) * 2 + core) * shard + low
-        return dst.at[pl.ds(pl.multiple_of(base, 8), size), pl.ds(col, cols)]
-
-    def half_of(s, d):
-        return d if s == steps else None
+    depth, width = wo.shape
+    quarter = depth // 4
+    carried = depth - quarter
+    entries = kept.shape[1]
+    ups, downs = wu.shape[1] // width, wd.shape[0]
+    tile = 256
+    chips_of_tile = tile // (2 * depth)
+    owners_chips = ring // downs
+
+    def column(ref, first, size):
+        return ref.at[:, :, :, pl.ds(first, size)]
+
+    parts = [(gains, gains_all, 0)]
+    parts += [(wq.at[:, pl.ds(j * width, width)], column(wq_all, j * width, width), j) for j in range(3)]
+    parts += [(wo, wo_all, 0)]
+    parts += [(wd.at[j], wd_all.at[:, :, j], 0) for j in range(downs)]
+    parts += [(wu.at[:, pl.ds(j * width, width)], column(wu_all, j * width, width), j) for j in range(ups)]
+    count = len(parts)
+
+    def window(k, s=0, d=0):
+        if k == 0:
+            return pl.ds(0, gains.shape[0]), pl.ds(0, gains.shape[1])
+        rows = pl.ds(pl.multiple_of(at.n * quarter, quarter), carried)
+        if s == steps:
+            return rows, pl.ds(d * (width // 2), width // 2)
+        return rows, pl.ds(0, width)
+
+    def idle(k, s, d):
+        return k == 0 and s == steps and d == 1
+
+    def toward(d):
+        return at.at_ring(at.r + 1 if d == 0 else at.r - 1)
 
     def ring_out(k, s, d):
         pos = at.r - (s - 1) if d == 0 else at.r + (s - 1)
-        half = half_of(s, d)
-        src = block(k, pos, at.c, half, s == 1)
-        dst = block(k, pos, at.c, half, False)
-        to = at.at_ring(at.r + 1 if d == 0 else at.r - 1)
-        return remote(src, dst, ring_send.at[k, s - 1, d], ring_recv.at[k, s - 1, d], to)
+        rows, cols = window(k, s, d)
+        dst = parts[k][1].at[at.chip(pos), at.c, rows, cols]
+        src = parts[k][0].at[rows, cols] if s == 1 else dst
+        return remote(src, dst, ring_send.at[k, s - 1, d], ring_recv.at[k, s - 1, d], toward(d))
 
     def ring_in(k, s, d):
         pos = at.r - s if d == 0 else at.r + s
-        ref = block(k, pos, at.c, half_of(s, d), False)
-        to = at.at_ring(at.r + 1 if d == 0 else at.r - 1)
-        return remote(ref, ref, ring_send.at[k, s - 1, d], ring_recv.at[k, s - 1, d], to)
-
-    def sib(k, s, d, core):
-        pos = at.r - s if d == 0 else at.r + s
-        half = half_of(s, d)
-        j = 0 if s == 0 else 1 + 2 * (s - 1) + d
-        dst = block(k, pos, core, half, False)
-        src = block(k, pos, core, half, s == 0)
-        return remote(src, dst, sib_send.at[k, j], sib_recv.at[k, j], at.sibling())
+        rows, cols = window(k, s, d)
+        ref = parts[k][1].at[at.chip(pos), at.c, rows, cols]
+        return remote(ref, ref, ring_send.at[k, s - 1, d], ring_recv.at[k, s - 1, d], toward(d))
+
+    def own_copy(k):
+        rows, cols = window(k)
+        return pltpu.make_async_copy(
+            parts[k][0].at[rows, cols], parts[k][1].at[at.q, at.c, rows, cols], own_sem.at[k]
+        )
+
+    def cross(k, incoming=False):
+        side = 1 - at.n if incoming else at.n
+        rows = pl.ds(pl.multiple_of(side * carried, quarter), quarter)
+        ref = parts[k][1].at[:, at.c, rows]
+        return remote(ref, ref, x_send.at[k], x_recv.at[k], at.across())
+
+    def sib(k, incoming=False):
+        ref = parts[k][1].at[:, 1 - at.c if incoming else at.c]
+        return remote(ref, ref, sib_send.at[k], sib_recv.at[k], at.sibling())
+
+    def row_copy(j):
+        return remote(given.at[j], got.at[j], row_send.at[j], row_recv.at[j], at.across())
+
+    def over(size, step):
+        def run(piece):
+            @pl.loop(0, size // step)
+            def _(t):
+                piece(pl.multiple_of(t * step, step))
+
+        return run
+
+    def turned(src, dst, first=0):
+        @over(src.shape[1], tile)
+        def _(low):
+            dst[pl.ds(first + low, tile), :] = src[:, pl.ds(low, tile)].T
+
+    def normalise():
+        lane = lax.broadcasted_iota(jnp.int32, (8, 2 * HEAD_DIM), 1)
+        for chip in range(ring):
+            pair = jnp.where(
+                lane < depth, gains_all[chip, 0].astype(F32)[:8], gains_all[chip, 1].astype(F32)[:8]
+            )
+            scales[:, chip * 2 * depth : (chip + 1) * 2 * depth] = pair
+
+        @over(entries, 32)
+        def _(low):
+            rows = pl.ds(low, 32)
+            low_rows = kept[0, rows] + got[0, rows]
+            value = low_rows.astype(F32)
+            rows_low[rows, :] = low_rows
+            inverse = lax.rsqrt(jnp.mean(value * value, axis=-1, keepdims=True) + epsilon)
+            normed[rows, :] = (value * inverse * scales[0:1, :]).astype(BF16)
+            router_val[rows, :] = jnp.sum(value * router[...], axis=-1, keepdims=True)
+
+    def project_part(j):
+        @over(width, tile)
+        def _(low):
+            cols = pl.ds(j * width + low, tile)
+            weight = wq_all[:, :, :, cols].reshape(width, tile)
+            project[:, cols] = dot(normed[...], weight).astype(BF16)
+
+    def attention(first, last):
+        @pl.loop(first, last)
+        def _(p):
+            lanes = 2 * HEAD_DIM
+            q = project[:, pl.ds(pl.multiple_of(p * lanes, lanes), lanes)]
+            k = project[:, pl.ds(pl.multiple_of(width + p * lanes, lanes), lanes)]
+            v = project[:, pl.ds(pl.multiple_of(2 * width + p * lanes, lanes), lanes)]
+            total = jnp.zeros((entries, lanes), F32)
+            for head in (0, 1):
+                probs = probabilities(live[...], only(q, head), k)
+                total = total + only(dot(probs.astype(BF16), v), head)
+            heads[:, pl.ds(pl.multiple_of(p * lanes, lanes), lanes)] = total.astype(BF16)
+
+    def attend_project():
+        @over(width, tile)
+        def _(low):
+            cols = pl.ds(low, tile)
+            weight = wo_all[:, :, :, cols].reshape(width, tile)
+            attend_out[:, cols] = dot(heads[...], weight)
+
+        @over(entries, 32)
+        def _(low):
+            rows = pl.ds(low, 32)
+            middle = rows_low[rows, :].astype(F32) + attend_out[rows, :]
+            inverse = lax.rsqrt(jnp.mean(middle * middle, axis=-1, keepdims=True) + epsilon)
+            value = middle * inverse
+            second_n[rows, :] = value
+            inverse_two[rows, :] = inverse
+            second[rows, :] = (value * scales[1:2, :]).astype(BF16)
+
+    def branch_grad():
+        @over(entries, 32)
+        def _(low):
+            rows = pl.ds(low, 32)
+            dout = (kept[1, rows] + got[1, rows]).astype(F32)
+            d_mlp[rows, :] = (router_val[rows, :] * dout).astype(BF16)
+
+    def act_grad():
+        @pl.loop(0, ring)
+        def _(chip):
+            for core in (0, 1):
+                size = downs * depth
+                cols = pl.ds(pl.multiple_of(chip * (2 * size) + core * size, size), size)
+                d_act[:, cols] = dot_nt(d_mlp[...], wd_all[chip, core].reshape(size, width))
+
+    def up_part(j):
+        @over(width, tile)
+        def _(low):
+            cols = pl.ds(j * width + low, tile)
+            pre = dot(second[...], wu_all[:, :, :, cols].reshape(width, tile))
+            value, slope = gelu_pair(pre)
+            value = value.astype(BF16)
+            act[:, pl.ds(low, tile)] = value
+            d_pre[:, cols] = (d_act[:, cols] * slope).astype(BF16)
+            act_t[cols, :] = value.T
+
+        @over(width, tile)
+        def _(low):
+            cols = pl.ds(low, tile)
+            down = wd_all[j * owners_chips : (j + 1) * owners_chips, :, :, :, cols]
+            part = dot(act[...], down.reshape(width, tile))
+            chip = low // (2 * depth)
+            up = wu_all[pl.ds(chip, chips_of_tile), :, :, pl.ds(j * width, width)]
+            back = dot_nt(d_pre[:, pl.ds(j * width, width)], up.reshape(tile, width))
+            if j == 0:
+                mlp_out[:, cols] = part
+                d_second[:, cols] = back
+            else:
+                mlp_out[:, cols] += part
+                d_second[:, cols] += back
+
+    def close():
+        small[...] = jnp.zeros_like(small)
+
+        @over(entries, 32)
+        def _(low):
+            rows = pl.ds(low, 32)
+            value = rows_low[rows, :].astype(F32)
+            dout = (kept[1, rows] + got[1, rows]).astype(F32)
+            gate = router_val[rows, :]
+            branch = attend_out[rows, :] + mlp_out[rows, :]
+            out_low[rows, :] = (value + gate * branch).astype(BF16)
+            d_gate = jnp.sum(dout * branch, axis=-1, keepdims=True)
+            normed_value = second_n[rows, :]
+            back = d_second[rows, :]
+            small[1:2, :] += jnp.sum(back * normed_value, axis=0, keepdims=True)
+            small[2:3, :] += jnp.sum(d_gate * value, axis=0, keepdims=True)
+            back = back * scales[1:2, :]
+            back = inverse_two[rows, :] * (
+                back - normed_value * jnp.mean(back * normed_value, axis=-1, keepdims=True)
+            )
+            d_attend[rows, :] = (gate * dout + back).astype(BF16)
+            base[rows, :] = dout + back + d_gate * router[...]
+
+    pairs = width // (2 * HEAD_DIM)
+    cuts = [pairs * j // 8 for j in (0, 2, 5, 8)]
+    work = [
+        [normalise, lambda: turned(normed, normed_t)],
+        [lambda: project_part(0)],
+        [lambda: project_part(1)],
+        [lambda: project_part(2), lambda: attention(cuts[0], cuts[1])],
+        [lambda: attention(cuts[1], cuts[2])],
+        [lambda: attention(cuts[2], cuts[3])],
+        [attend_project],
+        [branch_grad, lambda: turned(heads, heads_t), lambda: turned(second, second_t)],
+    ]
+    work += [[]] * (1 + 3 + 1 + downs - 1 - len(work)) + [[act_grad]]
+    work += [[functools.partial(up_part, j)] for j in range(ups)]
 
     greet([at.at_ring(at.r + 1), at.at_ring(at.r - 1), at.sibling(), at.across()])
-    cross = remote(rows, rows_got, x_send, x_recv, at.across())
-    cross.start()
-    count = len(parts)
-    for i in range(count + steps):
+    row_copy(0).start()
+    for i in range(count + steps + 2):
         if i < count:
             for d in (0, 1):
                 ring_out(i, 1, d).start()
-            sib(i, 0, 0, at.c).start()
-            pltpu.make_async_copy(
-                block(i, at.r, at.c, None, True), block(i, at.r, at.c, None, False), own_sem.at[i]
-            ).start()
+            own_copy(i).start()
+        if i == 2:
+            row_copy(1).start()
         for s in range(1, steps + 1):
             k = i - s
             if 0 <= k < count:
                 for d in (0, 1):
-                    ring_in(k, s, d).wait_recv()
-                    if s < steps:
-                        if s + 1 < steps or d == 0:
-                            ring_out(k, s + 1, d).start()
-                        else:
-                            ring_out(k, s + 1, d).start()
-                    sib(k, s, d, at.c).start()
+                    if not idle(k, s, d):
+                        ring_in(k, s, d).wait_recv()
+                    if s < steps and not idle(k, s + 1, d):
+                        ring_out(k, s + 1, d).start()
+                if s == steps:
+                    own_copy(k).wait()
+                    if k > 0:
+                        cross(k).start()
+        k = i - steps - 1
+        if 0 <= k < count:
+            if k > 0:
+                cross(k, True).wait_recv()
+            sib(k).start()
+        k = i - steps - 2
+        if 0 <= k < count:
+            sib(k, True).wait_recv()
+            if k == 0:
+                for j in (0, 1):
+                    row_copy(j).wait_recv()
+            for piece in work[k]:
+                piece()
+    close()
     for k in range(count):
-        pltpu.make_async_copy(
-            block(k, at.r, at.c, None, True), block(k, at.r, at.c, None, False), own_sem.at[k]
-        ).wait()
-        sib(k, 0, 0, at.c).wait_send()
-        sib(k, 0, 0, 1 - at.c).wait_recv()
+        sib(k).wait_send()
+        if k > 0:
+            cross(k).wait_send()
         for s in range(1, steps + 1):
             for d in (0, 1):
-                ring_out(k, s, d).wait_send()
-                sib(k, s, d, at.c).wait_send()
-                sib(k, s, d, 1 - at.c).wait_recv()
-    cross.wait()
-
-
-def gather_weights(wide, gains, wq, wo, wu, wd, rows):
-    count = 1 + 3 + 1 + wu.shape[1] // wo.shape[1] + wd.shape[0] // wo.shape[0]
-    steps = wide // 4
-    full = [jax.ShapeDtypeStruct((wide * a.shape[0], a.shape[1]), a.dtype) for a in (gains, wq, wo, wu, wd)]
+                if not idle(k, s, d):
+                    ring_out(k, s, d).wait_send()
+    for j in (0, 1):
+        row_copy(j).wait_send()
+
+
+def forward(wide, gains, wq, wo, wu, wd, kept, given, router, live):
+    depth, width = wo.shape
+    ring, steps = wide // 2, wide // 4
+    entries = kept.shape[1]
+    ff = wu.shape[1]
+    downs = wd.shape[0] // depth
+    count = 1 + 3 + 1 + downs + ff // width
+    vmem = pl.BlockSpec(memory_space=pltpu.VMEM)
     anywhere = pl.BlockSpec(memory_space=pl.ANY)
+    dma = pltpu.SemaphoreType.DMA
+    shape = jax.ShapeDtypeStruct
     return pl.pallas_call(
-        functools.partial(gather_kernel, wide),
-        out_shape=full + [jax.ShapeDtypeStruct(rows.shape, rows.dtype)],
-        in_specs=[anywhere] * 6,
-        out_specs=[anywhere] * 6,
+        functools.partial(forward_kernel, wide),
+        out_shape=[
+            shape((ring, 2, depth, 3 * width), BF16),
+            shape((ring, 2, depth, width), BF16),
+            shape((width, entries), BF16),
+            shape((width, entries), BF16),
+            shape((width, entries), BF16),
+            shape((ff, entries), BF16),
+            shape((entries, ff), BF16),
+            shape((entries, width), BF16),
+            shape((entries, width), BF16),
+            shape((entries, 3 * width), BF16),
+            shape((entries, width), F32),
+            shape((entries, width), BF16),
+            shape((entries, width), BF16),
+            shape((8, width), F32),
+            shape((8, width), F32),
+        ],
+        in_specs=[anywhere] * 5 + [vmem, anywhere, vmem, vmem],
+        out_specs=[vmem] * 15,
         scratch_shapes=[
-            pltpu.SemaphoreType.DMA((count,)),
-            pltpu.SemaphoreType.DMA((count, steps, 2)),
-            pltpu.SemaphoreType.DMA((count, steps, 2)),
-            pltpu.SemaphoreType.DMA((count, 1 + 2 * steps)),
-            pltpu.SemaphoreType.DMA((count, 1 + 2 * steps)),
-            pltpu.SemaphoreType.DMA,
-            pltpu.SemaphoreType.DMA,
+            pltpu.VMEM((ring, 2, depth, ff), BF16),
+            pltpu.VMEM((ring, 2, downs, depth, width), BF16),
+            pltpu.VMEM((ring, 2) + gains.shape, BF16),
+            pltpu.VMEM((2, entries, width), BF16),
+            pltpu.VMEM((entries, width), BF16),
+            pltpu.VMEM((entries, width), BF16),
+            pltpu.VMEM((entries, width), F32),
+            pltpu.VMEM((entries, width), F32),
+            pltpu.VMEM((entries, width), BF16),
+            pltpu.VMEM((entries, ff), F32),
+            pltpu.VMEM((entries, width), BF16),
+            pltpu.VMEM((entries, width), F32),
+            pltpu.VMEM((entries, width), F32),
+            pltpu.VMEM((entries, 1), F32),
+            pltpu.VMEM((entries, 1), F32),
+            dma((count,)),
+            dma((count, steps, 2)),
+            dma((count, steps, 2)),
+            dma((count,)),
+            dma((count,)),
+            dma((count,)),
+            dma((count,)),
+            dma((2,)),
+            dma((2,)),
         ],
-        compiler_params=pltpu.CompilerParams(collective_id=1, has_side_effects=True),
+        compiler_params=pltpu.CompilerParams(
+            collective_id=1, has_side_effects=True, vmem_limit_bytes=60 * 1024 * 1024
+        ),
         name="gather",
-    )(gains, wq, wo, wu, wd, rows)
+    )(gains, wq, wo, wu, wd.reshape(downs, depth, width), kept, given, router, live)
 
 
 def reduce_kernel(
@@ -622,19 +893,19 @@
 
 
 def reduce_grads(
-    wide, act_low, second_low, heads_low, normed_low, d_mlp, d_pre, d_attend, d_project, small, rows
+    wide, act_t, second_t, heads_t, normed_t, d_mlp, d_pre, d_attend, d_project, small, rows
 ):
-    width = normed_low.shape[1]
+    width = d_mlp.shape[1]
     ring, steps = wide // 2, wide // 4
     depth = width // wide
-    tokens_in = normed_low.shape[0]
+    tokens_in = d_mlp.shape[0]
 
     def tall(value):
-        return value.T.reshape(ring, 2, depth, tokens_in)
-
-    ff = act_low.shape[1]
+        return value.reshape(ring, 2, depth, tokens_in)
+
+    ff = d_pre.shape[1]
     downs = ff // width
-    act_t = act_low.T.reshape(ring, 2, downs, depth, tokens_in)
+    act_t = act_t.reshape(ring, 2, downs, depth, tokens_in)
     count = 2 * downs + 4
     stages = 2 + (ring.bit_length() - 1)
     vmem = pl.BlockSpec(memory_space=pltpu.VMEM)
@@ -678,9 +949,9 @@
         name="reduce",
     )(
         act_t,
-        tall(second_low),
-        tall(heads_low),
-        tall(normed_low),
+        tall(second_t),
+        tall(heads_t),
+        tall(normed_t),
         d_mlp,
         d_pre,
         d_attend,
@@ -690,35 +961,12 @@
     )
 
 
-def probabilities(count, queries, keys):
-    entries = queries.shape[0]
-    scores = dot_nt(queries, keys) * 0.125
-    q_at = lax.broadcasted_iota(jnp.int32, (entries, entries), 0)
-    k_at = lax.broadcasted_iota(jnp.int32, (entries, entries), 1)
-    scores = jnp.where((k_at <= q_at) & (k_at < count), scores, masked_score)
-    expo = jnp.exp(scores - jnp.max(scores, axis=-1, keepdims=True))
-    return expo / jnp.sum(expo, axis=-1, keepdims=True)
-
-
-def only(value, head):
-    lane = lax.broadcasted_iota(jnp.int32, value.shape, 1)
-    return jnp.where(lane // HEAD_DIM == head, value, jnp.zeros_like(value))
-
-
-def attend_kernel(count, q, k, v, out):
-    total = jnp.zeros(out.shape, F32)
-    for head in (0, 1):
-        probs = probabilities(count[0], only(q[...], head), k[...])
-        total = total + only(dot(probs.astype(BF16), v[...]), head)
-    out[...] = total.astype(BF16)
-
-
-def attend_back_kernel(count, q, k, v, d_heads, d_project):
+def attend_back_kernel(live, q, k, v, d_heads, d_project):
     d_q = jnp.zeros(q.shape, F32)
     d_k = jnp.zeros(q.shape, F32)
     d_v = jnp.zeros(q.shape, F32)
     for head in (0, 1):
-        probs = probabilities(count[0], only(q[...], head), k[...])
+        probs = probabilities(live[...], only(q[...], head), k[...])
         d_own = only(d_heads[...], head)
         d_probs = dot_nt(d_own, v[...])
         d_scores = probs * (d_probs - jnp.sum(probs * d_probs, axis=-1, keepdims=True))
@@ -731,25 +979,7 @@
     d_project[2] = d_v.astype(BF16)
 
 
-def attend(count, project):
-    entries = project.shape[0]
-    width = project.shape[1] // 3
-    pairs = width // (2 * HEAD_DIM)
-
-    def third(j):
-        return pl.BlockSpec((entries, 2 * HEAD_DIM), lambda p: (0, j * pairs + p))
-
-    return pl.pallas_call(
-        attend_kernel,
-        grid=(pairs,),
-        out_shape=jax.ShapeDtypeStruct((entries, width), BF16),
-        in_specs=[pl.BlockSpec(memory_space=pltpu.SMEM), third(0), third(1), third(2)],
-        out_specs=third(0),
-        name="attend",
-    )(count, project, project, project)
-
-
-def attend_back(count, project, d_heads):
+def attend_back(live, project, d_heads):
     entries = project.shape[0]
     width = project.shape[1] // 3
     pairs = width // (2 * HEAD_DIM)
@@ -761,10 +991,10 @@
         attend_back_kernel,
         grid=(pairs,),
         out_shape=jax.ShapeDtypeStruct((3, entries, width), BF16),
-        in_specs=[pl.BlockSpec(memory_space=pltpu.SMEM), third(0), third(1), third(2), third(0)],
+        in_specs=[pl.BlockSpec((1, entries), lambda p: (0, 0)), third(0), third(1), third(2), third(0)],
         out_specs=pl.BlockSpec((3, entries, 2 * HEAD_DIM), lambda p: (0, 0, p)),
         name="attend_back",
-    )(count, project, project, project, d_heads)
+    )(live, project, project, project, d_heads)
 
 
 def paired_body(
@@ -787,70 +1017,43 @@
     picked = jnp.stack([take(tokens), take(cotangent)])
     kept = lax.dynamic_index_in_dim(picked, place, 1, keepdims=False)
     given = lax.dynamic_index_in_dim(picked, 1 - place, 1, keepdims=False)
-    gains = jnp.concatenate([gain_attn, gain_mlp]).reshape(1, 2 * depth)
-    gains = jnp.pad(gains, ((0, 15), (0, 0)))
-    gains_all, weight_qkv, weight_out, weight_up, weight_down, got = gather_weights(
-        wide, gains, w_qkv, w_out, w_up, w_down, given
-    )
-    gains_all = gains_all.reshape(wide, 16, 2 * depth)[:, 0]
-    scale_first = gains_all[:, :depth].reshape(width).astype(F32)
-    scale_second = gains_all[:, depth:].reshape(width).astype(F32)
-    both = kept + got
-    inputs_low = both[0]
-    inputs_rows = inputs_low.astype(F32)
-    dout = both[1].astype(F32)
-    count = lax.dynamic_slice_in_dim(counts, place, 1)
-
-    normed_one, inverse_one = rms_parts(inputs_rows)
-    normed_low = (normed_one * scale_first).astype(BF16)
-    project = dot(normed_low, weight_qkv).astype(BF16)
-    heads_low = attend(count, project)
-    attend_out = dot(heads_low, weight_out)
-    middle = inputs_rows + attend_out
-    normed_two, inverse_two = rms_parts(middle)
-    second_low = (normed_two * scale_second).astype(BF16)
-    pre_act = dot(second_low, weight_up)
-    activ_full, gelu_back = jax.vjp(jax.nn.gelu, pre_act)
-    activ_low = activ_full.astype(BF16)
-    mlp_out = dot(activ_low, weight_down)
-    branch = attend_out + mlp_out
+    gains = jnp.stack(
+        [jnp.concatenate([gain_attn, gain_attn]), jnp.concatenate([gain_mlp, gain_mlp])]
+    )
+    gains = jnp.pad(gains, ((0, 14), (0, 0)))
     router_row = router.astype(F32)[None, :]
-    router_val = jnp.sum(inputs_rows * router_row, axis=-1, keepdims=True)
-    out_low = (inputs_rows + router_val * branch).astype(BF16)
-
-    d_branch = router_val * dout
-    d_router_val = jnp.sum(dout * branch, axis=-1, keepdims=True)
-    d_mlp = d_branch.astype(BF16)
-    d_act = dot_nt(d_mlp, weight_down)
-    d_pre = gelu_back(d_act)[0].astype(BF16)
-    d_normed_two = dot_nt(d_pre, weight_up)
-    grad_gain_two = jnp.sum(d_normed_two * normed_two, axis=0)
-    d_middle = rms_back(d_normed_two * scale_second, normed_two, inverse_two)
-    d_attend = (d_branch + d_middle).astype(BF16)
-    d_heads = dot_nt(d_attend, weight_out).astype(BF16)
-    d_parts = attend_back(count, project, d_heads)
+    live_row = lax.dynamic_index_in_dim(live, place, 0, keepdims=True).astype(jnp.int32)
+    (
+        weight_qkv,
+        weight_out,
+        normed_t,
+        heads_t,
+        second_t,
+        act_t,
+        d_pre,
+        d_mlp,
+        d_attend,
+        project,
+        base,
+        out_low,
+        rows_low,
+        small,
+        scales,
+    ) = forward(wide, gains, w_qkv, w_out, w_up, w_down, kept, given, router_row, live_row)
+
+    d_heads = dot_nt(d_attend, weight_out.reshape(width, width)).astype(BF16)
+    d_parts = attend_back(live_row, project, d_heads)
     d_project = jnp.concatenate([d_parts[0], d_parts[1], d_parts[2]], axis=1)
-    d_normed = dot_nt(d_project, weight_qkv)
+    d_normed = dot_nt(d_project, weight_qkv.reshape(width, 3 * width))
+    normed_one, inverse_one = rms_parts(rows_low.astype(F32))
     grad_gain_one = jnp.sum(d_normed * normed_one, axis=0)
-    d_norm_rows = rms_back(d_normed * scale_first, normed_one, inverse_one)
-    d_rows = dout + d_middle + d_norm_rows + d_router_val * router_row
-    grad_router = jnp.sum(d_router_val * inputs_rows, axis=0)
-    grad_low = d_rows.astype(BF16)
-
-    small = jnp.pad(jnp.stack([grad_gain_one, grad_gain_two, grad_router]), ((0, 5), (0, 0)))
+    d_norm_rows = rms_back(d_normed * scales[0:1], normed_one, inverse_one)
+    grad_low = (base + d_norm_rows).astype(BF16)
+
+    small = jnp.concatenate([grad_gain_one[None, :], small[1:]])
     back = jnp.stack([out_low, grad_low])
     grad_qkv, grad_out, grad_up, grad_down, small, back_got = reduce_grads(
-        wide,
-        activ_low,
-        second_low,
-        heads_low,
-        normed_low,
-        d_mlp,
-        d_pre,
-        d_attend,
-        d_project,
-        small,
-        back,
+        wide, act_t, second_t, heads_t, normed_t, d_mlp, d_pre, d_attend, d_project, small, back
     )
     first = place == 0
     rows_out = jnp.stack([jnp.where(first, back, back_got), jnp.where(first, back_got, back)], axis=1)

time: 403 us -> 338 us (0.84); the launches traced: 396 us -> 338 us
  matrix products: 51.4 us -> 19.3 us
  Pallas kernels: 314 us -> 298 us
  local copies, waits for them, and re-layouts: 17.9 us -> 9.68 us
    dot_general x4 -> x0, matrix products: 22.7 us -> none  [dot(): return jnp.dot(left, right, preferred_element_type=F32)]
    pallas_call x2 -> x1, Pallas kernels: 141 us -> 129 us  [forward(): pl.pallas_call(functools.partial(forward_kernel, wide), out_shape=[shape(...]
    dot_general x4 -> x2, matrix products: 17.6 us -> 8.2 us  [dot_nt(): lax.dot_general(left, right, (((1,), (1,)), ((), ())), preferred_element_...]
    convert_element_type x3 -> x0, local copies, waits for them, and re-layouts: 4.2 us -> none  [the longest x1 4.06 us: paired_body(): activ_low = activ_full.astype(BF16)]
where the time goes in v2:
time: 338 us
  Pallas kernels  298 us (88%)
  matrix products  19.3 us (6%)
  other arithmetic  10.3 us (3%)
  local copies, waits for them, and re-layouts  9.68 us (3%)
    pallas_call x1, Pallas kernels, reduce_grads(): pl.pallas_call(functools.partial(reduce_kernel, wide), out_shape=[jax.Sha...  157 us
    pallas_call x1, Pallas kernels, forward(): pl.pallas_call(functools.partial(forward_kernel, wide), out_shape=[shape(...  129 us
    pallas_call x1, Pallas kernels, attend_back(): pl.pallas_call(attend_back_kernel, grid=(pairs,), out_shape=jax.ShapeDtyp...  11.9 us
    dot_general x2, matrix products, dot_nt(): lax.dot_general(left, right, (((1,), (1,)), ((), ())), preferred_element_...  8.2 us

profile of v2, /device:TPU:0, one launch (start us, length us, event | category | flops | bytes accessed | tf_op | source)
XLA Modules:
  0.0 337.7 jit_solution(12370315347798361123)
XLA Ops:
  0.6 0.7 and_select_fusion
  1.3 0.8 subtract_select_fusion
  2.1 0.0 copy-start.12
  2.1 3.6 %fusion.5 = bf16[1,2,256,1024]{3,2,1,0:T(8,128)(2,1)S(1)} fusion(bf16[2,1024,1024]{2,1,0:T(8,128)(2,1)} %param.12, s32[2,256]{1,0:T(2,128)S(1)} %subtract_select_fusion), kind=kOutput, calls=%fused_computation.15 | convolution fusion | flops 1074790400 | bytes 5244928 | tf_op jit(solution)/shard_map/sep,spd->sed/dot_general | solution.py:1015
  5.7 0.0 copy-done.12
  5.7 1.3 fusion.6
  7.0 0.0 copy-start.9
  7.0 0.0 copy-start.10
  7.1 0.0 copy-start.8
  7.1 1.5 fusion.21
  8.6 0.1 iota_compare_fusion.14
  8.7 0.6 dynamic-slice_convert_fusion.live
  9.2 0.0 copy-done.9
  9.2 0.0 copy-done.10
  9.2 0.1 maximum_bitcast_fusion
  9.3 0.6 fusion.34.gains
  9.9 0.0 copy-done.8
  9.9 0.6 broadcast_in_dim.38
  10.5 129.1 %gather.1 = (bf16[8,2,64,3072]{3,2,1,0:T(8,128)(2,1)}, bf16[8,2,64,1024]{3,2,1,0:T(8,128)(2,1)}, bf16[1024,256]{1,0:T(8,128)(2,1)}, bf16[1024,256]{1,0:T(8,128)(...) custom-call(bf16[16,128]{1,0:T(8,128)(2,1)} %fusion.34.gains, ...), custom_call_target="tpu_custom_call" | custom-call | tf_op jit(solution)/shard_map/gather/pallas_call | solution.py:629
  139.6 3.3 convolution_convert_fusion.d_heads
  142.9 11.9 %attend_back.1 = bf16[3,256,1024]{2,1,0:T(8,128)(2,1)} custom-call(s32[1,256]{1,0:T(1,128)} %dynamic-slice_convert_fusion.live, bf16[256,3072]{1,0:T(8,128)(2,1)} %get-tuple-element.33.q.k.v, bf16[256,3072]{1,0:T(8,128)(2,1)} %get-tuple-element.33.q.k.v, bf16[256,3072]{1,0:T(8,128)(2,1)} %get-tuple-element.33.q.k.v, ...), custom_call_target="tpu_custom_call" | custom-call | tf_op jit(solution)/shard_map/attend_back/pallas_call | solution.py:990
  154.8 0.0 copy-start.1
  154.8 1.5 slice_bitcast_fusion.2
  156.3 0.8 slice.33
  157.1 0.0 copy-done.1
  157.1 0.2 fusion.16
  157.3 0.0 copy-start.4
  157.3 4.9 %fusion.10 = (f32[256]{0:T(256)S(1)}, f32[1024]{0:T(1024)S(1)}, f32[256,1024]{1,0:T(8,128)S(1)}) fusion(bf16[256,1024]{1,0:T(8,128)(2,1)S(1)} %copy-done.1, f32[1024]{0:T(1024)S(1)} %bitcast.58, f32[256]{0:T(256)S(1)} %add_rsqrt_fusion, bf16[1024,3072]{1,0:T(8,128)(2,1)} %bitcast.63, bf16[256,1024]{1,0:T(8,128)(2,1)S(1)} %get-tuple-element.58, ...), kind=kOutput, calls=%fused_computation.23 | convolution fusion | flops 1617165056 | bytes 9447424 | tf_op jit(solution)/shard_map/dot_general | solution.py:232
  162.2 0.0 copy-start
  162.2 0.0 copy-done.4
  162.2 0.0 copy-start.7
  162.2 0.3 fusion.31
  162.5 0.7 copy-done
  163.2 1.1 pad_maximum_fusion.2.rows
  164.3 0.0 copy-done.7
  164.3 0.6 pad_maximum_fusion.3.small
  164.9 1.2 pad_maximum_fusion.d_project
  166.2 156.6 %reduce.1 = (f32[64,3072]{1,0:T(8,128)}, f32[64,1024]{1,0:T(8,128)}, f32[64,4096]{1,0:T(8,128)}, f32[256,1024]{1,0:T(8,128)}, f32[8,1024]{1,0:T(8,128)}, /*index=5*/bf16[2,256,1024]{2,1,0:T(8,128)(2,1)}) custom-call(bf16[8,2,4,64,256]{4,3,2,1,0:T(8,128)(2,1)} %bitcast.53, bf16[8,2,64,256]{3,2,1,0:T(8,128)(2,1)} %bitcast.56, ...), custom_call_target="tpu_custom_call" | custom-call | tf_op jit(solution)/shard_map/reduce/pallas_call | solution.py:914
  322.8 0.0 copy-start.11
  322.8 1.6 select_bitcast_fusion
  324.5 0.4 fusion.2
  324.8 0.5 copy-done.11
  325.3 0.0 copy-start.13
  325.3 3.1 convert_select_fusion
  328.4 0.0 copy-done.13
  328.4 0.0 copy-start.5
  328.4 0.0 copy-start.6
  328.4 3.1 convert_select_fusion.1
  331.5 0.0 copy-start.3
  331.5 1.5 fusion.40
  333.0 0.6 fusion.35
  333.6 0.6 fusion.36
  334.2 0.0 copy-done.5
  334.2 0.0 copy-start.2
  334.2 0.9 copy.28
  335.1 0.0 copy-done.6
  335.1 0.7 copy.29
  335.8 0.0 copy-done.3
  335.8 1.0 copy.30
  336.7 0.0 copy-done.2
  336.7 1.0 copy.31
  (3 shorter events, 0.0 us)
Async XLA Ops:
  2.1 3.6 %copy-start.12 = (bf16[2,1024,1024]{2,1,0:T(8,128)(2,1)S(1)}, bf16[2,1024,1024]{2,1,0:T(8,128)(2,1)}, u32[]{:S(2)}) copy-start(bf16[2,1024,1024]{2,1,0:T(8,128)(2,1)} %param.11) | copy-start | bytes 12582916
  7.0 2.2 copy-start.9
  7.0 2.2 copy-start.10
  7.1 2.9 copy-start.8
  154.8 2.3 copy-start.1
  157.3 4.9 %copy-start.4 = (f32[256,1024]{1,0:T(8,128)S(1)}, f32[256,1024]{1,0:T(8,128)}, u32[]{:S(2)}) copy-start(f32[256,1024]{1,0:T(8,128)} %get-tuple-element.31) | copy-start | bytes 3145732
  162.2 1.0 copy-start
  162.2 2.1 copy-start.7
  322.8 2.5 copy-start.11
  325.3 3.1 copy-start.13
  328.4 5.8 %copy-start.5 = (f32[64,3072]{1,0:T(8,128)S(1)}, f32[64,3072]{1,0:T(8,128)}, u32[]{:S(2)}) copy-start(f32[64,3072]{1,0:T(8,128)} %get-tuple-element.77) | copy-start | bytes 2359300
  328.4 6.6 %copy-start.6 = (f32[64,1024]{1,0:T(8,128)S(1)}, f32[64,1024]{1,0:T(8,128)}, u32[]{:S(2)}) copy-start(f32[64,1024]{1,0:T(8,128)} %get-tuple-element.78) | copy-start | bytes 786436
  331.5 4.2 %copy-start.3 = (f32[64,4096]{1,0:T(8,128)S(1)}, f32[64,4096]{1,0:T(8,128)}, u32[]{:S(2)}) copy-start(f32[64,4096]{1,0:T(8,128)} %get-tuple-element.79) | copy-start | bytes 3145732
  334.2 2.6 copy-start.2

commit v3 on v2

--- a/solution.py
+++ b/solution.py
@@ -11,6 +11,13 @@
 MESH = pl.DeviceIdType.MESH
 F32 = jnp.float32
 BF16 = jnp.bfloat16
+LAG = 2
+PIECES = (512, 512)
+FIRST_PIECES = (256, 256, 512)
+LAST_PIECES = (512, 256, 256)
+GIVE = 128
+GIVE_SKIP = (3, 6)
+ROW_PIECES = 8
 
 epsilon = 1e-06
 masked_score = -1e30
@@ -248,14 +255,18 @@
         col = self.q // 2
         self.r = col + row * (2 * self.length - 1 - 2 * col)
 
-    def chip(self, ring_pos):
-        pos = lax.rem(ring_pos + 2 * self.ring, self.ring)
-        row = pos // self.length
-        col = pos + row * (2 * self.length - 1 - 2 * pos)
-        return col * 2 + row
-
-    def at_ring(self, ring_pos):
-        return (self.chip(ring_pos) * 2 + self.c, self.n)
+        self.around = {}
+        for offset in range(-(self.ring // 2), self.ring // 2 + 1):
+            pos = lax.rem(self.r + offset + self.ring, self.ring)
+            row = pos // self.length
+            col = pos + row * (2 * self.length - 1 - 2 * pos)
+            self.around[offset] = col * 2 + row
+
+    def chip(self, offset):
+        return self.around[offset]
+
+    def at_ring(self, offset):
+        return (self.around[offset] * 2 + self.c, self.n)
 
     def sibling(self):
         return (self.q * 2 + 1 - self.c, self.n)
@@ -363,16 +374,27 @@
     ups, downs = wu.shape[1] // width, wd.shape[0]
     tile = 256
     chips_of_tile = tile // (2 * depth)
-    owners_chips = ring // downs
-
-    def column(ref, first, size):
-        return ref.at[:, :, :, pl.ds(first, size)]
-
-    parts = [(gains, gains_all, 0)]
-    parts += [(wq.at[:, pl.ds(j * width, width)], column(wq_all, j * width, width), j) for j in range(3)]
-    parts += [(wo, wo_all, 0)]
-    parts += [(wd.at[j], wd_all.at[:, :, j], 0) for j in range(downs)]
-    parts += [(wu.at[:, pl.ds(j * width, width)], column(wu_all, j * width, width), j) for j in range(ups)]
+
+    parts = [(gains, gains_all)]
+    ready = {0: [0]}
+
+    def add(name, shard, full, first, pieces=PIECES):
+        for size in pieces:
+            cols = pl.ds(first, size)
+            parts.append((shard.at[:, cols], full.at[:, :, :, cols], size))
+            if name is None:
+                ready[len(parts) - 1] = [(first, size)]
+            first += size
+        if name is not None:
+            ready[len(parts) - 1] = [name]
+
+    for j in range(3):
+        add(1 + j, wq, wq_all, j * width)
+    add(4, wo, wo_all, 0)
+    for j in range(downs):
+        add(5 + j, wd.at[j], wd_all.at[:, :, j], 0)
+    for j in range(ups):
+        add(None, wu, wu_all, j * width, LAST_PIECES if j == ups - 1 else PIECES)
     count = len(parts)
 
     def window(k, s=0, d=0):
@@ -380,24 +402,24 @@
             return pl.ds(0, gains.shape[0]), pl.ds(0, gains.shape[1])
         rows = pl.ds(pl.multiple_of(at.n * quarter, quarter), carried)
         if s == steps:
-            return rows, pl.ds(d * (width // 2), width // 2)
-        return rows, pl.ds(0, width)
+            return rows, pl.ds(d * (parts[k][2] // 2), parts[k][2] // 2)
+        return rows, pl.ds(0, parts[k][2])
 
     def idle(k, s, d):
         return k == 0 and s == steps and d == 1
 
     def toward(d):
-        return at.at_ring(at.r + 1 if d == 0 else at.r - 1)
+        return at.at_ring(1 if d == 0 else -1)
 
     def ring_out(k, s, d):
-        pos = at.r - (s - 1) if d == 0 else at.r + (s - 1)
+        pos = -(s - 1) if d == 0 else s - 1
         rows, cols = window(k, s, d)
         dst = parts[k][1].at[at.chip(pos), at.c, rows, cols]
         src = parts[k][0].at[rows, cols] if s == 1 else dst
         return remote(src, dst, ring_send.at[k, s - 1, d], ring_recv.at[k, s - 1, d], toward(d))
 
     def ring_in(k, s, d):
-        pos = at.r - s if d == 0 else at.r + s
+        pos = -s if d == 0 else s
         rows, cols = window(k, s, d)
         ref = parts[k][1].at[at.chip(pos), at.c, rows, cols]
         return remote(ref, ref, ring_send.at[k, s - 1, d], ring_recv.at[k, s - 1, d], toward(d))
@@ -504,10 +526,10 @@
                 cols = pl.ds(pl.multiple_of(chip * (2 * size) + core * size, size), size)
                 d_act[:, cols] = dot_nt(d_mlp[...], wd_all[chip, core].reshape(size, width))
 
-    def up_part(j):
-        @over(width, tile)
+    def up_part(first, size):
+        @over(size, tile)
         def _(low):
-            cols = pl.ds(j * width + low, tile)
+            cols = pl.ds(first + low, tile)
             pre = dot(second[...], wu_all[:, :, :, cols].reshape(width, tile))
             value, slope = gelu_pair(pre)
             value = value.astype(BF16)
@@ -515,15 +537,21 @@
             d_pre[:, cols] = (d_act[:, cols] * slope).astype(BF16)
             act_t[cols, :] = value.T
 
+        owner = 2 * depth * downs
+        chip, core = first // owner, first % owner // (owner // 2)
+
         @over(width, tile)
         def _(low):
             cols = pl.ds(low, tile)
-            down = wd_all[j * owners_chips : (j + 1) * owners_chips, :, :, :, cols]
-            part = dot(act[...], down.reshape(width, tile))
-            chip = low // (2 * depth)
-            up = wu_all[pl.ds(chip, chips_of_tile), :, :, pl.ds(j * width, width)]
-            back = dot_nt(d_pre[:, pl.ds(j * width, width)], up.reshape(tile, width))
-            if j == 0:
+            if size == owner:
+                down = wd_all[chip, :, :, :, cols]
+            else:
+                down = wd_all[chip, core, :, :, cols]
+            part = dot(act[:, 0:size], down.reshape(size, tile))
+            chips = pl.ds(low // (2 * depth), chips_of_tile)
+            up = wu_all[chips, :, :, pl.ds(first, size)]
+            back = dot_nt(d_pre[:, pl.ds(first, size)], up.reshape(tile, size))
+            if first == 0:
                 mlp_out[:, cols] = part
                 d_second[:, cols] = back
             else:
@@ -566,11 +594,11 @@
         [branch_grad, lambda: turned(heads, heads_t), lambda: turned(second, second_t)],
     ]
     work += [[]] * (1 + 3 + 1 + downs - 1 - len(work)) + [[act_grad]]
-    work += [[functools.partial(up_part, j)] for j in range(ups)]
-
-    greet([at.at_ring(at.r + 1), at.at_ring(at.r - 1), at.sibling(), at.across()])
+
+    greet([at.at_ring(1), at.at_ring(-1), at.sibling(), at.across()])
     row_copy(0).start()
-    for i in range(count + steps + 2):
+    lag = LAG
+    for i in range(count + lag * (steps + 1) + 1):
         if i < count:
             for d in (0, 1):
                 ring_out(i, 1, d).start()
@@ -578,7 +606,7 @@
         if i == 2:
             row_copy(1).start()
         for s in range(1, steps + 1):
-            k = i - s
+            k = i - lag * s
             if 0 <= k < count:
                 for d in (0, 1):
                     if not idle(k, s, d):
@@ -589,19 +617,24 @@
                     own_copy(k).wait()
                     if k > 0:
                         cross(k).start()
-        k = i - steps - 1
+        k = i - lag * (steps + 1)
         if 0 <= k < count:
             if k > 0:
                 cross(k, True).wait_recv()
             sib(k).start()
-        k = i - steps - 2
+        k = i - lag * (steps + 1) - 1
         if 0 <= k < count:
             sib(k, True).wait_recv()
             if k == 0:
                 for j in (0, 1):
                     row_copy(j).wait_recv()
-            for piece in work[k]:
-                piece()
+            if k in ready:
+                for piece in ready[k]:
+                    if isinstance(piece, int):
+                        for job in work[piece]:
+                            job()
+                    else:
+                        up_part(*piece)
     close()
     for k in range(count):
         sib(k).wait_send()
@@ -621,7 +654,7 @@
     entries = kept.shape[1]
     ff = wu.shape[1]
     downs = wd.shape[0] // depth
-    count = 1 + 3 + 1 + downs + ff // width
+    count = 1 + (3 + downs + ff // width) * len(PIECES) + len(LAST_PIECES)
     vmem = pl.BlockSpec(memory_space=pltpu.VMEM)
     anywhere = pl.BlockSpec(memory_space=pl.ANY)
     dma = pltpu.SemaphoreType.DMA
@@ -680,8 +713,11 @@
     )(gains, wq, wo, wu, wd.reshape(downs, depth, width), kept, given, router, live)
 
 
-def reduce_kernel(
+def backward_kernel(
     wide,
+    chunks,
+    wq_all,
+    wo_all,
     act_t,
     second_t,
     heads_t,
@@ -689,25 +725,37 @@
     d_mlp,
     d_pre,
     d_attend,
-    d_project,
+    project,
+    base,
+    rows_low,
+    scales,
     small,
-    rows,
+    live,
+    out_low,
     o_qkv,
     o_out,
     o_up,
     o_down,
     o_small,
     rows_got,
+    grad_low,
+    d_heads,
+    d_project,
+    d_normed,
     own,
     to_sib,
     mine,
+    landed,
     moving,
+    x_pre,
     x_out,
     x_in,
     small_acc,
     small_in,
     sib_send,
     sib_recv,
+    pre_send,
+    pre_recv,
     ring_send,
     ring_recv,
     x_send,
@@ -721,68 +769,81 @@
     ring, steps = at.ring, at.ring // 2
     depth, width = o_out.shape
     half = depth // 2
-    ups, downs = o_up.shape[1] // width, o_down.shape[0] // depth
-    rows_in = d_mlp.shape[0]
-    count = downs + ups + 1 + 3
+    entries = d_mlp.shape[0]
+    count = len(chunks)
     tile = 256
-
-    def operands(k):
-        if k < downs:
-            return lambda core: act_t[:, core, k], d_mlp, 0
-        k -= downs
-        if k < ups:
-            return lambda core: second_t[:, core], d_pre, k * width
-        k -= ups
-        if k < 1:
-            return lambda core: heads_t[:, core], d_attend, 0
-        return lambda core: normed_t[:, core], d_project, (k - 1) * width
+    step = 16
+    starts = [sum(c[3] for c in chunks[:k]) for k in range(count)]
+    give_starts = [sum(c[4] for c in chunks[:k]) for k in range(count)]
+
+    def lanes(first, size):
+        return pl.ds(first if isinstance(first, int) else pl.multiple_of(first, 128), size)
+
+    def whole(k):
+        return lanes(starts[k], chunks[k][3])
+
+    def carried(k):
+        size, give = chunks[k][3:]
+        return lanes(starts[k] + give * at.n, size - give)
+
+    def kept_alone(k):
+        size, give = chunks[k][3:]
+        return lanes(starts[k] + (size - give) * at.n, give)
 
     def product(k, core, put):
-        left, right, first = operands(k)
-        tall = left(core).reshape(ring * depth, rows_in)
-
-        @pl.loop(0, width // tile)
+        kind, j, first, size, _ = chunks[k]
+        if kind == "down":
+            left, right = act_t[:, core, j], d_mlp
+        else:
+            tall, right = {
+                "up": (second_t, d_pre),
+                "out": (heads_t, d_attend),
+                "qkv": (normed_t, d_project),
+            }[kind]
+            left = tall[:, core]
+        left = left.reshape(ring * depth, entries)
+
+        @pl.loop(0, size // tile)
         def _(t):
             cols = pl.ds(pl.multiple_of(t * tile, tile), tile)
-            from_cols = pl.ds(pl.multiple_of(first + t * tile, tile), tile)
-            put(cols, dot(tall, right[:, from_cols]).reshape(ring, depth, tile))
+            take = pl.ds(pl.multiple_of(first + t * tile, tile), tile)
+            put(cols, dot(left, right[:, take]).reshape(ring, depth, tile))
 
     def store(k):
-        if k < downs:
-            return o_down, k * depth, 0
-        k -= downs
-        if k < ups:
-            return o_up, 0, k * width
-        k -= ups
-        if k < 1:
-            return o_out, 0, 0
-        return o_qkv, 0, (k - 1) * width
+        kind, j, first, size, _ = chunks[k]
+        out = {"up": o_up, "down": o_down, "out": o_out, "qkv": o_qkv}[kind]
+        return out, j * depth if kind == "down" else 0, first
 
     def sib(k):
+        src = to_sib.at[k % 2, :, :, pl.ds(0, chunks[k][3])]
+        return remote(src, mine.at[:, :, whole(k)], sib_send.at[k], sib_recv.at[k], at.sibling())
+
+    def pre(k):
+        size, give = chunks[k][3:]
+        src = mine.at[:, :, lanes(starts[k] + (size - give) * (1 - at.n), give)]
+        dst = x_pre.at[:, :, lanes(give_starts[k], give)]
+        return remote(src, dst, pre_send.at[k], pre_recv.at[k], at.across())
+
+    def toward(d):
+        return at.at_ring(1 if d == 0 else -1)
+
+    def dest(t, d):
+        return at.chip(steps - t if d == 0 else t - steps)
+
+    def arrival(k, t, d):
+        cols = carried(k)
+        return landed.at[d, :, cols] if t == 0 else moving.at[t - 1, d, :, cols]
+
+    def ring_out(k, t, d):
+        rows = pl.ds(d * half, half) if t == 0 else pl.ds(0, depth)
+        src = mine.at[dest(t, d), rows, carried(k)]
         return remote(
-            to_sib.at[k % 2], mine.at[k], sib_send.at[k], sib_recv.at[k], at.sibling()
+            src, arrival(k, t, d), ring_send.at[k, t, d], ring_recv.at[k, t, d], toward(d)
         )
 
-    def halves(d):
-        return pl.ds(d * half, half)
-
-    def ring_out(k, t, d):
-        to = at.at_ring(at.r + 1 if d == 0 else at.r - 1)
-        if t == 0:
-            src = mine.at[k, at.chip(at.r + steps), halves(d)]
-            dst = moving.at[k, 0, d, halves(d)]
-        else:
-            src = moving.at[k, t - 1, d]
-            dst = moving.at[k, t, d]
-        return remote(src, dst, ring_send.at[k, t, d], ring_recv.at[k, t, d], to)
-
-    def ring_in(k, t, d):
-        to = at.at_ring(at.r + 1 if d == 0 else at.r - 1)
-        ref = moving.at[k, 0, d, halves(d)] if t == 0 else moving.at[k, t, d]
-        return remote(ref, ref, ring_send.at[k, t, d], ring_recv.at[k, t, d], to)
-
     def cross(k):
-        return remote(x_out.at[k], x_in.at[k], x_send.at[k], x_recv.at[k], at.across())
+        cols = carried(k)
+        return remote(x_out.at[:, cols], x_in.at[:, cols], x_send.at[k], x_recv.at[k], at.across())
 
     bits = [1 << b for b in range(ring.bit_length() - 1)]
     partners = [at.sibling(), at.across()] + [at.flipped(bit) for bit in bits]
@@ -793,13 +854,186 @@
             small_acc.at[j], small_in.at[j], small_send.at[j], small_recv.at[j], partners[j]
         )
 
-    greet(partners + [at.at_ring(at.r + 1), at.at_ring(at.r - 1)])
-    rows_copy = remote(rows, rows_got, row_send, row_recv, at.across())
-    rows_copy.start()
-    small_acc[0] = small[...]
-    step = 16
-
-    for i in range(count + steps + 3):
+    def row_copy(j, p):
+        rows = pl.ds(p * (entries // ROW_PIECES), entries // ROW_PIECES)
+        src = out_low if j == 0 else grad_low
+        return remote(
+            src.at[rows], rows_got.at[j, rows], row_send.at[j, p], row_recv.at[j, p], at.across()
+        )
+
+    def over(size, piece_size):
+        def run(piece):
+            @pl.loop(0, size // piece_size)
+            def _(t):
+                piece(pl.multiple_of(t * piece_size, piece_size))
+
+        return run
+
+    def heads_grad():
+        @over(width, tile)
+        def _(low):
+            chips = pl.ds(low // (2 * depth), tile // (2 * depth))
+            weight = wo_all[chips].reshape(tile, width)
+            d_heads[:, pl.ds(low, tile)] = dot_nt(d_attend[...], weight).astype(BF16)
+
+    def attention(first, last):
+        span = 2 * HEAD_DIM
+
+        @pl.loop(first, last)
+        def _(p):
+            places = [lanes(j * width + p * span, span) for j in range(3)]
+            q, k, v = [project[:, place] for place in places]
+            d_pair = d_heads[:, places[0]]
+            d_q = jnp.zeros((entries, span), F32)
+            d_k = jnp.zeros((entries, span), F32)
+            d_v = jnp.zeros((entries, span), F32)
+            for head in (0, 1):
+                probs = probabilities(live[...], only(q, head), k)
+                d_own = only(d_pair, head)
+                d_probs = dot_nt(d_own, v)
+                d_scores = probs * (d_probs - jnp.sum(probs * d_probs, axis=-1, keepdims=True))
+                d_scores = d_scores.astype(BF16)
+                d_q = d_q + only(dot(d_scores, k), head)
+                d_k = d_k + only(dot_tn(d_scores, q), head)
+                d_v = d_v + dot_tn(probs.astype(BF16), d_own)
+            d_project[:, places[0]] = (d_q * 0.125).astype(BF16)
+            d_project[:, places[1]] = (d_k * 0.125).astype(BF16)
+            d_project[:, places[2]] = d_v.astype(BF16)
+
+    def normed_grad(j):
+        @over(width, tile)
+        def _(low):
+            chips = pl.ds(low // (2 * depth), tile // (2 * depth))
+            weight = wq_all[chips, :, :, pl.ds(j * width, width)].reshape(tile, width)
+            part = dot_nt(d_project[:, pl.ds(j * width, width)], weight)
+            cols = pl.ds(low, tile)
+            if j == 0:
+                d_normed[:, cols] = part
+            else:
+                d_normed[:, cols] += part
+
+    def finish():
+        small_acc[0] = small[...]
+
+        @over(entries, 32)
+        def _(low):
+            rows = pl.ds(low, 32)
+            value = rows_low[rows, :].astype(F32)
+            inverse = lax.rsqrt(jnp.mean(value * value, axis=-1, keepdims=True) + epsilon)
+            value = value * inverse
+            back = d_normed[rows, :]
+            small_acc[0, 0:1, :] += jnp.sum(back * value, axis=0, keepdims=True)
+            back = back * scales[0:1, :]
+            back = inverse * (back - value * jnp.mean(back * value, axis=-1, keepdims=True))
+            grad_low[rows, :] = (base[rows, :] + back).astype(BF16)
+
+    pairs = width // (2 * HEAD_DIM)
+    cuts = [pairs * j // 4 for j in range(5)]
+    work = [heads_grad]
+    work += [functools.partial(attention, cuts[j], cuts[j + 1]) for j in range(4)]
+    work += [functools.partial(normed_grad, j) for j in range(3)]
+    work += [finish]
+
+    x_out[...] = jnp.zeros_like(x_out)
+    x_in[...] = jnp.zeros_like(x_in)
+    greet(partners + [at.at_ring(1), at.at_ring(-1)])
+    lag = LAG
+    ring_at = 1 + lag
+    total = count + ring_at + lag * steps + lag + 1
+    small_at = len(work)
+    for i in range(total):
+        k = i - ring_at - lag * steps - lag
+        if 0 <= k < count:
+            cross(k).wait_recv()
+            out, low, first = store(k)
+            size = chunks[k][3]
+
+            @over(depth, step)
+            def _(row):
+                rows = pl.ds(row, step)
+                value = x_out[rows, whole(k)].astype(F32) + x_in[rows, whole(k)].astype(F32)
+                out[pl.ds(low + row, step), first : first + size] = value
+
+        k = i - ring_at - lag * steps
+        if 0 <= k < count:
+            cols = carried(k)
+            for d in (0, 1):
+                remote(
+                    arrival(k, steps - 1, d),
+                    arrival(k, steps - 1, d),
+                    ring_send.at[k, steps - 1, d],
+                    ring_recv.at[k, steps - 1, d],
+                    toward(d),
+                ).wait_recv()
+
+            @over(depth, step)
+            def _(row):
+                rows = pl.ds(row, step)
+                value = mine[at.q, rows, cols].astype(F32)
+                value = value + moving[steps - 2, 0, rows, cols].astype(F32)
+                value = value + moving[steps - 2, 1, rows, cols].astype(F32)
+                x_out[rows, cols] = value.astype(BF16)
+
+            cross(k).start()
+        for t in range(steps - 1, 0, -1):
+            k = i - ring_at - lag * t
+            if 0 <= k < count:
+                cols = carried(k)
+                for d in (0, 1):
+                    remote(
+                        arrival(k, t - 1, d),
+                        arrival(k, t - 1, d),
+                        ring_send.at[k, t - 1, d],
+                        ring_recv.at[k, t - 1, d],
+                        toward(d),
+                    ).wait_recv()
+                    to = dest(t, d)
+                    size = half if t == 1 else depth
+                    base_row = d * half if t == 1 else 0
+
+                    @over(size, step)
+                    def _(row):
+                        into = pl.ds(base_row + row, step)
+                        if t == 1:
+                            got = landed[d, pl.ds(row, step), cols]
+                        else:
+                            got = moving[t - 2, d, pl.ds(row, step), cols]
+                        value = mine[to, into, cols].astype(F32) + got.astype(F32)
+                        mine[to, into, cols] = value.astype(BF16)
+
+                    ring_out(k, t, d).start()
+        k = i - ring_at
+        if 0 <= k < count:
+            if chunks[k][4] > 0:
+                pre(k).wait_recv()
+                cols = kept_alone(k)
+                take = lanes(give_starts[k], chunks[k][4])
+
+                @pl.loop(0, ring)
+                def _(chip):
+                    value = mine[chip, :, cols].astype(F32) + x_pre[chip, :, take].astype(F32)
+                    mine[chip, :, cols] = value.astype(BF16)
+
+            for d in (0, 1):
+                ring_out(k, 0, d).start()
+        k = i - 1
+        if 0 <= k < count:
+            remote(
+                mine.at[:, :, whole(k)],
+                mine.at[:, :, whole(k)],
+                sib_send.at[k],
+                sib_recv.at[k],
+                at.sibling(),
+            ).wait_recv()
+            size = chunks[k][3]
+
+            @pl.loop(0, ring)
+            def _(chip):
+                value = mine[chip, :, whole(k)].astype(F32) + own[chip, :, 0:size]
+                mine[chip, :, whole(k)] = value.astype(BF16)
+
+            if chunks[k][4] > 0:
+                pre(k).start()
         k = i
         if k < count:
             if k >= 2:
@@ -809,129 +1043,124 @@
                 to_sib[k % 2, :, :, cols] = value.astype(BF16)
 
             def keep_own(cols, value):
-                own[k % 2, :, :, cols] = value
+                own[:, :, cols] = value
 
             product(k, 1 - at.c, keep_other)
             sib(k).start()
             product(k, at.c, keep_own)
-        if i <= stages:
-            if i > 0:
-                small_copy(i - 1).wait_recv()
-                small_acc[i] = small_acc[i - 1] + small_in[i - 1]
-            if i < stages:
-                small_copy(i).start()
+        if i < len(work):
+            work[i]()
+        if i < ROW_PIECES:
+            row_copy(0, i).start()
+        p = i - max(len(work), count - ROW_PIECES)
+        if 0 <= p < ROW_PIECES:
+            row_copy(1, p).start()
+        j = i - small_at
+        if 0 <= j <= stages:
+            if j > 0:
+                small_copy(j - 1).wait_recv()
+                small_acc[j] = small_acc[j - 1] + small_in[j - 1]
+            if j < stages:
+                small_copy(j).start()
             else:
                 o_small[...] = small_acc[stages]
-        k = i - 1
-        if 0 <= k < count:
-            sib(k).wait_recv()
-
-            @pl.loop(0, ring)
-            def _(chip):
-                mine[k, chip] = (mine[k, chip].astype(F32) + own[k % 2, chip]).astype(BF16)
-
-            for d in (0, 1):
-                ring_out(k, 0, d).start()
-        for t in range(1, steps):
-            k = i - 1 - t
-            if 0 <= k < count:
-                for d in (0, 1):
-                    ring_in(k, t - 1, d).wait_recv()
-                    dest = at.chip(at.r + (steps - t) if d == 0 else at.r - (steps - t))
-                    lows = range(0, depth, half) if t == 1 else (0,)
-                    for low in lows:
-                        size = half if t == 1 else depth
-
-                        @pl.loop(0, size // step)
-                        def _(g):
-                            take = pl.ds(pl.multiple_of(low + g * step, step), step)
-                            value = mine[k, dest, take]
-                            if not (t == 1 and low != d * half):
-                                value = (
-                                    value.astype(F32) + moving[k, t - 1, d, take].astype(F32)
-                                ).astype(BF16)
-                            moving[k, t - 1, d, take] = value
-
-                    ring_out(k, t, d).start()
-        k = i - 1 - steps
-        if 0 <= k < count:
-            for d in (0, 1):
-                ring_in(k, steps - 1, d).wait_recv()
-
-            @pl.loop(0, depth // step)
-            def _(g):
-                take = pl.ds(pl.multiple_of(g * step, step), step)
-                value = mine[k, at.q, take].astype(F32)
-                value = value + moving[k, steps - 1, 0, take].astype(F32)
-                value = value + moving[k, steps - 1, 1, take].astype(F32)
-                x_out[k, take] = value.astype(BF16)
-
-            cross(k).start()
-        k = i - 2 - steps
-        if 0 <= k < count:
-            cross(k).wait_recv()
-            out, low, first = store(k)
-
-            @pl.loop(0, depth // step)
-            def _(g):
-                take = pl.ds(pl.multiple_of(g * step, step), step)
-                put = pl.ds(pl.multiple_of(low + g * step, step), step)
-                out[put, first : first + width] = x_out[k, take].astype(F32) + x_in[
-                    k, take
-                ].astype(F32)
 
     for k in range(count):
         if k >= count - 2:
             sib(k).wait_send()
+        if chunks[k][4] > 0:
+            pre(k).wait_send()
         cross(k).wait_send()
         for t in range(steps):
             for d in (0, 1):
                 ring_out(k, t, d).wait_send()
     for j in range(stages):
         small_copy(j).wait_send()
-    rows_copy.wait()
-
-
-def reduce_grads(
-    wide, act_t, second_t, heads_t, normed_t, d_mlp, d_pre, d_attend, d_project, small, rows
+    for j in (0, 1):
+        for p in range(ROW_PIECES):
+            row_copy(j, p).wait()
+
+
+def backward(
+    wide,
+    wq_all,
+    wo_all,
+    act_t,
+    second_t,
+    heads_t,
+    normed_t,
+    d_mlp,
+    d_pre,
+    d_attend,
+    project,
+    base,
+    rows_low,
+    scales,
+    small,
+    live,
+    out_low,
 ):
-    width = d_mlp.shape[1]
+    entries, width = d_mlp.shape
     ring, steps = wide // 2, wide // 4
     depth = width // wide
-    tokens_in = d_mlp.shape[0]
-
-    def tall(value):
-        return value.reshape(ring, 2, depth, tokens_in)
-
     ff = d_pre.shape[1]
-    downs = ff // width
-    act_t = act_t.reshape(ring, 2, downs, depth, tokens_in)
-    count = 2 * downs + 4
+    ups = downs = ff // width
+    chunks = []
+    panels = [("up", j, j * width) for j in range(ups)]
+    panels += [("down", j, 0) for j in range(downs)]
+    panels += [("out", 0, 0)]
+    panels += [("qkv", j, j * width) for j in range(3)]
+    last = len(panels) - 1
+    for index, (kind, j, first) in enumerate(panels):
+        for size in FIRST_PIECES if index == 0 else LAST_PIECES if index == last else PIECES:
+            chunks.append((kind, j, first, size))
+            first += size
+    chunks = [
+        c + (GIVE if GIVE_SKIP[0] <= k < len(chunks) - GIVE_SKIP[1] and c[3] == 512 else 0,)
+        for k, c in enumerate(chunks)
+    ]
+    chunks = tuple(chunks)
+    count = len(chunks)
+    everything = sum(c[3] for c in chunks)
+    given = sum(c[4] for c in chunks)
     stages = 2 + (ring.bit_length() - 1)
     vmem = pl.BlockSpec(memory_space=pltpu.VMEM)
     anywhere = pl.BlockSpec(memory_space=pl.ANY)
     dma = pltpu.SemaphoreType.DMA
+    shape = jax.ShapeDtypeStruct
+
+    def tall(value):
+        return value.reshape(ring, 2, depth, entries)
+
     return pl.pallas_call(
-        functools.partial(reduce_kernel, wide),
+        functools.partial(backward_kernel, wide, chunks),
         out_shape=[
-            jax.ShapeDtypeStruct((depth, 3 * width), F32),
-            jax.ShapeDtypeStruct((depth, width), F32),
-            jax.ShapeDtypeStruct((depth, ff), F32),
-            jax.ShapeDtypeStruct((ff // wide, width), F32),
-            jax.ShapeDtypeStruct(small.shape, F32),
-            jax.ShapeDtypeStruct(rows.shape, rows.dtype),
+            shape((depth, 3 * width), F32),
+            shape((depth, width), F32),
+            shape((depth, ff), F32),
+            shape((ff // wide, width), F32),
+            shape((8, width), F32),
+            shape((2, entries, width), BF16),
+            shape((entries, width), BF16),
         ],
-        in_specs=[vmem] * 9 + [anywhere],
-        out_specs=[vmem] * 5 + [anywhere],
+        in_specs=[vmem] * 15 + [anywhere],
+        out_specs=[vmem] * 5 + [anywhere, vmem],
         scratch_shapes=[
-            pltpu.VMEM((2, ring, depth, width), F32),
-            pltpu.VMEM((2, ring, depth, width), BF16),
-            pltpu.VMEM((count, ring, depth, width), BF16),
-            pltpu.VMEM((count, steps, 2, depth, width), BF16),
-            pltpu.VMEM((count, depth, width), BF16),
-            pltpu.VMEM((count, depth, width), BF16),
-            pltpu.VMEM((stages + 1,) + small.shape, F32),
-            pltpu.VMEM((stages,) + small.shape, F32),
+            pltpu.VMEM((entries, width), BF16),
+            pltpu.VMEM((entries, 3 * width), BF16),
+            pltpu.VMEM((entries, width), F32),
+            pltpu.VMEM((ring, depth, 512), F32),
+            pltpu.VMEM((2, ring, depth, 512), BF16),
+            pltpu.VMEM((ring, depth, everything), BF16),
+            pltpu.VMEM((2, depth // 2, everything), BF16),
+            pltpu.VMEM((steps - 1, 2, depth, everything), BF16),
+            pltpu.VMEM((ring, depth, max(given, 128)), BF16),
+            pltpu.VMEM((depth, everything), BF16),
+            pltpu.VMEM((depth, everything), BF16),
+            pltpu.VMEM((stages + 1, 8, width), F32),
+            pltpu.VMEM((stages, 8, width), F32),
+            dma((count,)),
+            dma((count,)),
             dma((count,)),
             dma((count,)),
             dma((count, steps, 2)),
@@ -940,61 +1169,31 @@
             dma((count,)),
             dma((stages,)),
             dma((stages,)),
-            dma,
-            dma,
+            dma((2, ROW_PIECES)),
+            dma((2, ROW_PIECES)),
         ],
         compiler_params=pltpu.CompilerParams(
-            collective_id=2, has_side_effects=True, vmem_limit_bytes=60 * 1024 * 1024
+            collective_id=2, has_side_effects=True, vmem_limit_bytes=62 * 1024 * 1024
         ),
         name="reduce",
     )(
-        act_t,
+        wq_all,
+        wo_all,
+        act_t.reshape(ring, 2, downs, depth, entries),
         tall(second_t),
         tall(heads_t),
         tall(normed_t),
         d_mlp,
         d_pre,
         d_attend,
-        d_project,
+        project,
+        base,
+        rows_low,
+        scales,
         small,
-        rows,
-    )
-
-
-def attend_back_kernel(live, q, k, v, d_heads, d_project):
-    d_q = jnp.zeros(q.shape, F32)
-    d_k = jnp.zeros(q.shape, F32)
-    d_v = jnp.zeros(q.shape, F32)
-    for head in (0, 1):
-        probs = probabilities(live[...], only(q[...], head), k[...])
-        d_own = only(d_heads[...], head)
-        d_probs = dot_nt(d_own, v[...])
-        d_scores = probs * (d_probs - jnp.sum(probs * d_probs, axis=-1, keepdims=True))
-        d_scores = d_scores.astype(BF16)
-        d_q = d_q + only(dot(d_scores, k[...]), head)
-        d_k = d_k + only(dot_tn(d_scores, q[...]), head)
-        d_v = d_v + dot_tn(probs.astype(BF16), d_own)
-    d_project[0] = (d_q * 0.125).astype(BF16)
-    d_project[1] = (d_k * 0.125).astype(BF16)
-    d_project[2] = d_v.astype(BF16)
-
-
-def attend_back(live, project, d_heads):
-    entries = project.shape[0]
-    width = project.shape[1] // 3
-    pairs = width // (2 * HEAD_DIM)
-
-    def third(j):
-        return pl.BlockSpec((entries, 2 * HEAD_DIM), lambda p: (0, j * pairs + p))
-
-    return pl.pallas_call(
-        attend_back_kernel,
-        grid=(pairs,),
-        out_shape=jax.ShapeDtypeStruct((3, entries, width), BF16),
-        in_specs=[pl.BlockSpec((1, entries), lambda p: (0, 0)), third(0), third(1), third(2), third(0)],
-        out_specs=pl.BlockSpec((3, entries, 2 * HEAD_DIM), lambda p: (0, 0, p)),
-        name="attend_back",
-    )(live, project, project, project, d_heads)
+        live,
+        out_low,
+    )
 
 
 def paired_body(
@@ -1041,20 +1240,26 @@
         scales,
     ) = forward(wide, gains, w_qkv, w_out, w_up, w_down, kept, given, router_row, live_row)
 
-    d_heads = dot_nt(d_attend, weight_out.reshape(width, width)).astype(BF16)
-    d_parts = attend_back(live_row, project, d_heads)
-    d_project = jnp.concatenate([d_parts[0], d_parts[1], d_parts[2]], axis=1)
-    d_normed = dot_nt(d_project, weight_qkv.reshape(width, 3 * width))
-    normed_one, inverse_one = rms_parts(rows_low.astype(F32))
-    grad_gain_one = jnp.sum(d_normed * normed_one, axis=0)
-    d_norm_rows = rms_back(d_normed * scales[0:1], normed_one, inverse_one)
-    grad_low = (base + d_norm_rows).astype(BF16)
-
-    small = jnp.concatenate([grad_gain_one[None, :], small[1:]])
+    grad_qkv, grad_out, grad_up, grad_down, small, back_got, grad_low = backward(
+        wide,
+        weight_qkv,
+        weight_out,
+        act_t,
+        second_t,
+        heads_t,
+        normed_t,
+        d_mlp,
+        d_pre,
+        d_attend,
+        project,
+        base,
+        rows_low,
+        scales,
+        small,
+        live_row,
+        out_low,
+    )
     back = jnp.stack([out_low, grad_low])
-    grad_qkv, grad_out, grad_up, grad_down, small, back_got = reduce_grads(
-        wide, act_t, second_t, heads_t, normed_t, d_mlp, d_pre, d_attend, d_project, small, back
-    )
     first = place == 0
     rows_out = jnp.stack([jnp.where(first, back, back_got), jnp.where(first, back_got, back)], axis=1)
     hit = jnp.any(local_slot[:, :, None] == spots[None, None, :], axis=1)
@@ -1078,7 +1283,7 @@
 
 
 def body(wide, narrow, tokens, *others):
-    if narrow == 2 and tokens.shape[0] == 2 and wide >= 8 and wide & (wide - 1) == 0:
+    if narrow == 2 and tokens.shape[0] == 2 and wide == 16:
         return paired_body(wide, tokens, *others)
     return general_body(tokens, *others)
 

time: 338 us -> 300 us (0.89)
  Pallas kernels: 298 us -> 274 us
  matrix products: 19.3 us -> 11.1 us
  other arithmetic: 10.3 us -> 6.85 us
    pallas_call x2 -> x1, Pallas kernels: 169 us -> 145 us  [backward(): pl.pallas_call(functools.partial(backward_kernel, wide, chunks), out_shap...]
    dot_general x2 -> x0, matrix products: 8.2 us -> none  [dot_nt(): lax.dot_general(left, right, (((1,), (1,)), ((), ())), preferred_element_...]
where the time goes in v3:
time: 300 us
  Pallas kernels  274 us (91%)
  matrix products  11.1 us (4%)
  local copies, waits for them, and re-layouts  6.93 us (2%)
  other arithmetic  6.85 us (2%)
    pallas_call x1, Pallas kernels, backward(): pl.pallas_call(functools.partial(backward_kernel, wide, chunks), out_shap...  145 us
    pallas_call x1, Pallas kernels, forward(): pl.pallas_call(functools.partial(forward_kernel, wide), out_shape=[shape(...  129 us
    dot_general x2, matrix products, put(): jnp.einsum('sep,sed->spd', chosen, fresh, preferred_element_type=F32)  6.12 us

profile of v3, /device:TPU:0, one launch (start us, length us, event | category | flops | bytes accessed | tf_op | source)
XLA Modules:
  0.0 300.0 jit_solution(7417957183479210594)
XLA Ops:
  0.6 0.7 and_select_fusion
  1.3 0.8 subtract_select_fusion
  2.1 0.0 copy-start.9
  2.1 3.6 %fusion.5 = bf16[1,2,256,1024]{3,2,1,0:T(8,128)(2,1)S(1)} fusion(bf16[2,1024,1024]{2,1,0:T(8,128)(2,1)} %param.12, s32[2,256]{1,0:T(2,128)S(1)} %subtract_select_fusion), kind=kOutput, calls=%fused_computation.14 | convolution fusion | flops 1074790400 | bytes 5244928 | tf_op jit(solution)/shard_map/sep,spd->sed/dot_general | solution.py:1214
  5.7 0.0 copy-done.9
  5.7 1.3 fusion.6
  7.0 0.0 copy-start.6
  7.0 0.0 copy-start.7
  7.1 0.0 copy-start.5
  7.1 1.5 fusion.11
  8.6 0.1 iota_compare_fusion.14
  8.6 0.6 dynamic-slice_convert_fusion.live
  9.2 0.0 copy-done.6
  9.2 0.0 copy-done.7
  9.2 0.1 maximum_bitcast_fusion
  9.3 0.6 fusion.23.gains
  9.9 0.0 copy-done.5
  9.9 0.6 broadcast_in_dim.32
  10.5 129.0 %gather.1 = (bf16[8,2,64,3072]{3,2,1,0:T(8,128)(2,1)}, bf16[8,2,64,1024]{3,2,1,0:T(8,128)(2,1)}, bf16[1024,256]{1,0:T(8,128)(2,1)}, bf16[1024,256]{1,0:T(8,128)(...) custom-call(bf16[16,128]{1,0:T(8,128)(2,1)} %fusion.23.gains, ...), custom_call_target="tpu_custom_call" | custom-call | tf_op jit(solution)/shard_map/gather/pallas_call | solution.py:662
  139.5 0.0 copy-start
  139.5 145.5 %reduce.1 = (f32[64,3072]{1,0:T(8,128)}, f32[64,1024]{1,0:T(8,128)}, f32[64,4096]{1,0:T(8,128)}, f32[256,1024]{1,0:T(8,128)}, f32[8,1024]{1,0:T(8,128)}, /*index...) custom-call(bf16[8,2,64,3072]{3,2,1,0:T(8,128)(2,1)} %get-tuple-element.32.wq_all, ...), custom_call_target="tpu_custom_call" | custom-call | tf_op jit(solution)/shard_map/reduce/pallas_call | solution.py:1135
  285.0 0.0 copy-done
  285.0 0.0 copy-start.8
  285.0 1.6 select_bitcast_fusion
  286.6 0.4 fusion.2
  287.0 0.6 copy-done.8
  287.6 0.0 copy-start.10
  287.6 3.1 %convert_select_fusion = bf16[2,1024,1024]{2,1,0:T(8,128)(2,1)} fusion(bf16[2,1024,1024]{2,1,0:T(8,128)(2,1)S(1)} %copy-done.8, pred[2,1024]{1,0:T(4,128)(4,1)S(1)} %fusion.2, bf16[2,1,256,1024]{3,2,0,1:T(8,128)(2,1)S(1)} %get-tuple-element.53, bf16[2,1,256,1024]{3,2,0,1:T(8,128)(2,1)S(1)} %get-tuple-element.54, s32[2,256]{1,0:T(2,128)S(1)} %subtract_select_fusion), kind=kOutput, calls=%fused_computation | convolution fusion | flops 1078984704 | bytes 10489856 | tf_op jit(solution)/shard_map/sep,sed->spd/dot_general | solution.py:1268
  290.7 0.1 copy-done.10
  290.8 0.0 copy-start.3
  290.8 0.0 copy-start.4
  290.8 3.1 %convert_select_fusion.1 = bf16[2,1024,1024]{2,1,0:T(8,128)(2,1)} fusion(bf16[2,1024,1024]{2,1,0:T(8,128)(2,1)S(1)} %copy-done.10, pred[2,1024]{1,0:T(4,128)(4,1)S(1)} %fusion.2, bf16[2,1,256,1024]{3,2,0,1:T(8,128)(2,1)S(1)} %get-tuple-element.54, bf16[2,1,256,1024]{3,2,0,1:T(8,128)(2,1)S(1)} %get-tuple-element.53, s32[2,256]{1,0:T(2,128)S(1)} %subtract_select_fusion), kind=kOutput, calls=%fused_computation.1 | convolution fusion | flops 1078984704 | bytes 10489856 | tf_op jit(solution)/shard_map/sep,sed->spd/dot_general | solution.py:1268
  293.8 0.0 copy-start.2
  293.8 1.5 fusion.28
  295.3 0.6 fusion.24
  295.9 0.6 fusion.25
  296.5 0.0 copy-done.3
  296.5 0.0 copy-start.1
  296.5 0.9 copy.28
  297.4 0.0 copy-done.4
  297.4 0.7 copy.29
  298.1 0.0 copy-done.2
  298.1 1.0 copy.30
  299.0 0.0 copy-done.1
  299.1 1.0 copy.31
Async XLA Ops:
  2.1 3.6 %copy-start.9 = (bf16[2,1024,1024]{2,1,0:T(8,128)(2,1)S(1)}, bf16[2,1024,1024]{2,1,0:T(8,128)(2,1)}, u32[]{:S(2)}) copy-start(bf16[2,1024,1024]{2,1,0:T(8,128)(2,1)} %param.11) | copy-start | bytes 12582916
  7.0 2.2 copy-start.6
  7.0 2.2 copy-start.7
  7.1 2.9 copy-start.5
  139.5 145.5 %copy-start = (bf16[256,1024]{1,0:T(8,128)(2,1)S(1)}, bf16[256,1024]{1,0:T(8,128)(2,1)}, u32[]{:S(2)}) copy-start(bf16[256,1024]{1,0:T(8,128)(2,1)} %get-tuple-element.31.out_low) | copy-start | bytes 1572868
  285.0 2.7 copy-start.8
  287.6 3.1 %copy-start.10 = (bf16[2,1024,1024]{2,1,0:T(8,128)(2,1)S(1)}, bf16[2,1024,1024]{2,1,0:T(8,128)(2,1)}, u32[]{:S(2)}) copy-start(bf16[2,1024,1024]{2,1,0:T(8,128)(2,1)} %param.11) | copy-start | bytes 12582916
  290.8 5.7 %copy-start.3 = (f32[64,3072]{1,0:T(8,128)S(1)}, f32[64,3072]{1,0:T(8,128)}, u32[]{:S(2)}) copy-start(f32[64,3072]{1,0:T(8,128)} %get-tuple-element.73) | copy-start | bytes 2359300
  290.8 6.6 %copy-start.4 = (f32[64,1024]{1,0:T(8,128)S(1)}, f32[64,1024]{1,0:T(8,128)}, u32[]{:S(2)}) copy-start(f32[64,1024]{1,0:T(8,128)} %get-tuple-element.74) | copy-start | bytes 786436
  293.8 4.2 %copy-start.2 = (f32[64,4096]{1,0:T(8,128)S(1)}, f32[64,4096]{1,0:T(8,128)}, u32[]{:S(2)}) copy-start(f32[64,4096]{1,0:T(8,128)} %get-tuple-element.75) | copy-start | bytes 3145732
  296.5 2.6 copy-start.1

commit v4 on v0

--- a/solution.py
+++ b/solution.py
@@ -1,10 +1,23 @@
+import functools
+from typing import NamedTuple
+
 import jax
 import jax.numpy as jnp
 from jax import lax
+from jax.experimental import pallas as pl
+from jax.experimental.pallas import tpu as pltpu
 from jax.sharding import PartitionSpec as P
 
 HEAD_DIM = 64
-
+MESH = pl.DeviceIdType.MESH
+F32 = jnp.float32
+BF16 = jnp.bfloat16
+LAG = 2
+PIECES = (512, 512)
+LAST_PIECES = (512, 256, 256)
+GIVE = 128
+GIVE_SKIP = (3, 6)
+ROW_PIECES = 8
 
 epsilon = 1e-06
 masked_score = -1e30
@@ -60,7 +73,7 @@
     return (d_queries, d_key_part, d_value_part)
 
 
-def body(
+def general_body(
     tokens, cotangent, lengths, routes, w_qkv, w_out, w_up, w_down, gain_attn, gain_mlp, router
 ):
     parts_narrow = lax.axis_size("narrow")
@@ -218,6 +231,966 @@
     )
 
 
+def dot(left, right):
+    return jnp.dot(left, right, preferred_element_type=F32)
+
+
+def dot_nt(left, right):
+    return lax.dot_general(left, right, (((1,), (1,)), ((), ())), preferred_element_type=F32)
+
+
+def dot_tn(left, right):
+    return lax.dot_general(left, right, (((0,), (0,)), ((), ())), preferred_element_type=F32)
+
+
+class Place:
+    def __init__(self, wide):
+        self.ring = wide // 2
+        self.length = self.ring // 2
+        self.w = lax.axis_index("wide")
+        self.n = lax.axis_index("narrow")
+        self.c = self.w % 2
+        self.q = self.w // 2
+        row = self.q % 2
+        col = self.q // 2
+        self.r = col + row * (2 * self.length - 1 - 2 * col)
+
+        self.around = {}
+        for offset in range(-(self.ring // 2), self.ring // 2 + 1):
+            pos = lax.rem(self.r + offset + self.ring, self.ring)
+            row = pos // self.length
+            col = pos + row * (2 * self.length - 1 - 2 * pos)
+            self.around[offset] = col * 2 + row
+
+    def chip(self, offset):
+        return self.around[offset]
+
+    def at_ring(self, offset):
+        return (self.around[offset] * 2 + self.c, self.n)
+
+    def sibling(self):
+        return (self.q * 2 + 1 - self.c, self.n)
+
+    def across(self):
+        return (self.w, 1 - self.n)
+
+    def flipped(self, bit):
+        return ((self.q + bit - 2 * bit * ((self.q // bit) % 2)) * 2 + self.c, self.n)
+
+
+def greet(partners):
+    barrier = pltpu.get_barrier_semaphore()
+    for partner in partners:
+        pl.semaphore_signal(barrier, inc=1, device_id=partner, device_id_type=MESH)
+    pl.semaphore_wait(barrier, len(partners))
+
+
+def remote(src, dst, send, recv, device):
+    return pltpu.make_async_remote_copy(
+        src_ref=src, dst_ref=dst, send_sem=send, recv_sem=recv, device_id=device, device_id_type=MESH
+    )
+
+
+def probabilities(live, queries, keys):
+    entries = queries.shape[0]
+    scores = dot_nt(queries, keys) * 0.125
+    q_at = lax.broadcasted_iota(jnp.int32, (entries, entries), 0)
+    k_at = lax.broadcasted_iota(jnp.int32, (entries, entries), 1)
+    scores = jnp.where((k_at <= q_at) & (live > 0), scores, masked_score)
+    expo = jnp.exp(scores - jnp.max(scores, axis=-1, keepdims=True))
+    return expo / jnp.sum(expo, axis=-1, keepdims=True)
+
+
+def only(value, head):
+    lane = lax.broadcasted_iota(jnp.int32, value.shape, 1)
+    return jnp.where(lane // HEAD_DIM == head, value, jnp.zeros_like(value))
+
+
+def gelu_pair(x):
+    inner = 0.7978845608028654 * (x + 0.044715 * (x * x * x))
+    bent = jnp.tanh(inner)
+    half = 0.5 * (1.0 + bent)
+    slope = 0.7978845608028654 * (1.0 + 0.134145 * (x * x))
+    return x * half, half + 0.5 * x * (1.0 - bent * bent) * slope
+
+
+def layer_kernel(
+    wide,
+    chunks,
+    gains,
+    wq,
+    wo,
+    wu,
+    wd,
+    kept,
+    given,
+    router,
+    live,
+    o_qkv,
+    o_out,
+    o_up,
+    o_down,
+    o_small,
+    rows_got,
+    out_low,
+    grad_low,
+    wq_all,
+    wo_all,
+    wu_all,
+    wd_all,
+    gains_all,
+    scales,
+    got,
+    rows_low,
+    normed,
+    project,
+    heads,
+    attend_out,
+    second_n,
+    second,
+    act,
+    d_pre,
+    mlp_out,
+    d_second,
+    d_mlp,
+    d_attend,
+    base,
+    d_project,
+    normed_t,
+    heads_t,
+    second_t,
+    act_t,
+    router_val,
+    inverse_two,
+    own,
+    to_sib,
+    mine,
+    landed,
+    moving,
+    x_pre,
+    x_in,
+    staged,
+    small_acc,
+    small_in,
+    own_sem,
+    g_ring_send,
+    g_ring_recv,
+    g_sib_send,
+    g_sib_recv,
+    g_x_send,
+    g_x_recv,
+    in_send,
+    in_recv,
+    sib_send,
+    sib_recv,
+    pre_send,
+    pre_recv,
+    ring_send,
+    ring_recv,
+    x_send,
+    x_recv,
+    out_sem,
+    small_send,
+    small_recv,
+    row_send,
+    row_recv,
+    free,
+):
+    at = Place(wide)
+    ring, steps = at.ring, at.ring // 2
+    depth, width = wo.shape
+    quarter = depth // 4
+    half = depth // 2
+    most = depth - quarter
+    entries = kept.shape[1]
+    ups, downs = wu.shape[1] // width, wd.shape[0]
+    tile = 256
+    step = 16
+    lag = LAG
+    chips_of_tile = tile // (2 * depth)
+
+    def lanes(first, size):
+        return pl.ds(first if isinstance(first, int) else pl.multiple_of(first, 128), size)
+
+    def over(size, piece_size):
+        def run(piece):
+            @pl.loop(0, size // piece_size)
+            def _(t):
+                piece(pl.multiple_of(t * piece_size, piece_size))
+
+        return run
+
+    def toward(d):
+        return at.at_ring(1 if d == 0 else -1)
+
+    parts = [(gains, gains_all, 0)]
+    ready = {0: [0]}
+
+    def add(name, shard, full, first, pieces=PIECES):
+        for size in pieces:
+            cols = pl.ds(first, size)
+            parts.append((shard.at[:, cols], full.at[:, :, :, cols], size))
+            if name is None:
+                ready[len(parts) - 1] = [(first, size)]
+            first += size
+        if name is not None:
+            ready[len(parts) - 1] = [name]
+
+    for j in range(3):
+        add(1 + j, wq, wq_all, j * width)
+    add(4, wo, wo_all, 0)
+    for j in range(downs):
+        add(5 + j, wd.at[j], wd_all.at[:, :, j], 0)
+    up_at = len(parts)
+    for j in range(ups):
+        add(None, wu, wu_all, j * width, LAST_PIECES if j == ups - 1 else PIECES)
+    parts_count = len(parts)
+    up_chunks = parts_count - up_at
+
+    def window(k, s=0, d=0):
+        if k == 0:
+            return pl.ds(0, gains.shape[0]), pl.ds(0, gains.shape[1])
+        rows = pl.ds(pl.multiple_of(at.n * quarter, quarter), most)
+        if s == steps:
+            return rows, pl.ds(d * (parts[k][2] // 2), parts[k][2] // 2)
+        return rows, pl.ds(0, parts[k][2])
+
+    def idle(k, s, d):
+        return k == 0 and s == steps and d == 1
+
+    def g_ring_out(k, s, d):
+        pos = -(s - 1) if d == 0 else s - 1
+        rows, cols = window(k, s, d)
+        dst = parts[k][1].at[at.chip(pos), at.c, rows, cols]
+        src = parts[k][0].at[rows, cols] if s == 1 else dst
+        return remote(src, dst, g_ring_send.at[k, s - 1, d], g_ring_recv.at[k, s - 1, d], toward(d))
+
+    def g_ring_in(k, s, d):
+        pos = -s if d == 0 else s
+        rows, cols = window(k, s, d)
+        ref = parts[k][1].at[at.chip(pos), at.c, rows, cols]
+        return remote(ref, ref, g_ring_send.at[k, s - 1, d], g_ring_recv.at[k, s - 1, d], toward(d))
+
+    def own_copy(k):
+        rows, cols = window(k)
+        return pltpu.make_async_copy(
+            parts[k][0].at[rows, cols], parts[k][1].at[at.q, at.c, rows, cols], own_sem.at[k]
+        )
+
+    def g_cross(k, incoming=False):
+        side = 1 - at.n if incoming else at.n
+        rows = pl.ds(pl.multiple_of(side * most, quarter), quarter)
+        ref = parts[k][1].at[:, at.c, rows]
+        return remote(ref, ref, g_x_send.at[k], g_x_recv.at[k], at.across())
+
+    def g_sib(k, incoming=False):
+        ref = parts[k][1].at[:, 1 - at.c if incoming else at.c]
+        return remote(ref, ref, g_sib_send.at[k], g_sib_recv.at[k], at.sibling())
+
+    def in_copy(j):
+        return remote(given.at[j], got.at[j], in_send.at[j], in_recv.at[j], at.across())
+
+    def turned(src, dst):
+        @over(width, tile)
+        def _(low):
+            chips = pl.ds(low // (2 * depth), chips_of_tile)
+            dst[chips] = src[:, pl.ds(low, tile)].T.reshape(chips_of_tile, 2, depth, entries)
+
+    def normalise():
+        lane = lax.broadcasted_iota(jnp.int32, (8, 2 * HEAD_DIM), 1)
+        for chip in range(ring):
+            pair = jnp.where(
+                lane < depth, gains_all[chip, 0].astype(F32)[:8], gains_all[chip, 1].astype(F32)[:8]
+            )
+            scales[:, chip * 2 * depth : (chip + 1) * 2 * depth] = pair
+
+        @over(entries, 32)
+        def _(low):
+            rows = pl.ds(low, 32)
+            low_rows = kept[0, rows] + got[0, rows]
+            value = low_rows.astype(F32)
+            rows_low[rows, :] = low_rows
+            inverse = lax.rsqrt(jnp.mean(value * value, axis=-1, keepdims=True) + epsilon)
+            normed[rows, :] = (value * inverse * scales[0:1, :]).astype(BF16)
+            router_val[rows, :] = jnp.sum(value * router[...], axis=-1, keepdims=True)
+
+    def project_part(j):
+        @over(width, tile)
+        def _(low):
+            cols = pl.ds(j * width + low, tile)
+            weight = wq_all[:, :, :, cols].reshape(width, tile)
+            project[:, cols] = dot(normed[...], weight).astype(BF16)
+
+    def attention(first, last):
+        @pl.loop(first, last)
+        def _(p):
+            span = 2 * HEAD_DIM
+            q, k, v = [project[:, lanes(j * width + p * span, span)] for j in range(3)]
+            total = jnp.zeros((entries, span), F32)
+            for head in (0, 1):
+                probs = probabilities(live[...], only(q, head), k)
+                total = total + only(dot(probs.astype(BF16), v), head)
+            heads[:, lanes(p * span, span)] = total.astype(BF16)
+
+    def attend_project():
+        @over(width, tile)
+        def _(low):
+            cols = pl.ds(low, tile)
+            weight = wo_all[:, :, :, cols].reshape(width, tile)
+            attend_out[:, cols] = dot(heads[...], weight)
+
+        @over(entries, 32)
+        def _(low):
+            rows = pl.ds(low, 32)
+            middle = rows_low[rows, :].astype(F32) + attend_out[rows, :]
+            inverse = lax.rsqrt(jnp.mean(middle * middle, axis=-1, keepdims=True) + epsilon)
+            value = middle * inverse
+            second_n[rows, :] = value
+            inverse_two[rows, :] = inverse
+            second[rows, :] = (value * scales[1:2, :]).astype(BF16)
+
+    def branch_grad():
+        @over(entries, 32)
+        def _(low):
+            rows = pl.ds(low, 32)
+            dout = (kept[1, rows] + got[1, rows]).astype(F32)
+            d_mlp[rows, :] = (router_val[rows, :] * dout).astype(BF16)
+
+    def up_part(first, size):
+        owner = downs * depth
+        for low in range(0, size, owner):
+            chip, core = (first + low) // owner // 2, (first + low) // owner % 2
+            cols = pl.ds(first + low, owner)
+            pre = dot(second[...], wu_all[:, :, :, cols].reshape(width, owner))
+            value, slope = gelu_pair(pre)
+            value = value.astype(BF16)
+            d_act = dot_nt(d_mlp[...], wd_all[chip, core].reshape(owner, width))
+            act[:, pl.ds(low, owner)] = value
+            d_pre[:, cols] = (d_act * slope).astype(BF16)
+            act_t[chip, core] = value.T.reshape(downs, depth, entries)
+        chip, core = first // owner // 2, first // owner % 2
+
+        @over(width, tile)
+        def _(low):
+            cols = pl.ds(low, tile)
+            if size == owner:
+                down = wd_all[chip, core, :, :, cols]
+            else:
+                down = wd_all[chip, :, :, :, cols]
+            part = dot(act[:, 0:size], down.reshape(size, tile))
+            chips = pl.ds(low // (2 * depth), chips_of_tile)
+            up = wu_all[chips, :, :, pl.ds(first, size)]
+            back = dot_nt(d_pre[:, pl.ds(first, size)], up.reshape(tile, size))
+            if first == 0:
+                mlp_out[:, cols] = part
+                d_second[:, cols] = back
+            else:
+                mlp_out[:, cols] += part
+                d_second[:, cols] += back
+
+    def close():
+        small_acc[0] = jnp.zeros((8, width), F32)
+
+        @over(entries, 32)
+        def _(low):
+            rows = pl.ds(low, 32)
+            value = rows_low[rows, :].astype(F32)
+            dout = (kept[1, rows] + got[1, rows]).astype(F32)
+            gate = router_val[rows, :]
+            branch = attend_out[rows, :] + mlp_out[rows, :]
+            out_low[rows, :] = (value + gate * branch).astype(BF16)
+            d_gate = jnp.sum(dout * branch, axis=-1, keepdims=True)
+            normed_value = second_n[rows, :]
+            back = d_second[rows, :]
+            small_acc[0, 1:2, :] += jnp.sum(back * normed_value, axis=0, keepdims=True)
+            small_acc[0, 2:3, :] += jnp.sum(d_gate * value, axis=0, keepdims=True)
+            back = back * scales[1:2, :]
+            back = inverse_two[rows, :] * (
+                back - normed_value * jnp.mean(back * normed_value, axis=-1, keepdims=True)
+            )
+            d_attend[rows, :] = (gate * dout + back).astype(BF16)
+            base[rows, :] = dout + back + d_gate * router[...]
+
+    def heads_grad():
+        @over(width, tile)
+        def _(low):
+            chips = pl.ds(low // (2 * depth), chips_of_tile)
+            weight = wo_all[chips].reshape(tile, width)
+            heads[:, pl.ds(low, tile)] = dot_nt(d_attend[...], weight).astype(BF16)
+
+    def attention_back(first, last):
+        span = 2 * HEAD_DIM
+
+        @pl.loop(first, last)
+        def _(p):
+            places = [lanes(j * width + p * span, span) for j in range(3)]
+            q, k, v = [project[:, place] for place in places]
+            d_pair = heads[:, places[0]]
+            d_q = jnp.zeros((entries, span), F32)
+            d_k = jnp.zeros((entries, span), F32)
+            d_v = jnp.zeros((entries, span), F32)
+            for head in (0, 1):
+                probs = probabilities(live[...], only(q, head), k)
+                d_own = only(d_pair, head)
+                d_probs = dot_nt(d_own, v)
+                d_scores = probs * (d_probs - jnp.sum(probs * d_probs, axis=-1, keepdims=True))
+                d_scores = d_scores.astype(BF16)
+                d_q = d_q + only(dot(d_scores, k), head)
+                d_k = d_k + only(dot_tn(d_scores, q), head)
+                d_v = d_v + dot_tn(probs.astype(BF16), d_own)
+            d_project[:, places[0]] = (d_q * 0.125).astype(BF16)
+            d_project[:, places[1]] = (d_k * 0.125).astype(BF16)
+            d_project[:, places[2]] = d_v.astype(BF16)
+
+    def normed_grad(j):
+        @over(width, tile)
+        def _(low):
+            chips = pl.ds(low // (2 * depth), chips_of_tile)
+            weight = wq_all[chips, :, :, pl.ds(j * width, width)].reshape(tile, width)
+            part = dot_nt(d_project[:, pl.ds(j * width, width)], weight)
+            cols = pl.ds(low, tile)
+            if j == 0:
+                d_second[:, cols] = part
+            else:
+                d_second[:, cols] += part
+
+    def finish():
+        @over(entries, 32)
+        def _(low):
+            rows = pl.ds(low, 32)
+            value = rows_low[rows, :].astype(F32)
+            inverse = lax.rsqrt(jnp.mean(value * value, axis=-1, keepdims=True) + epsilon)
+            value = value * inverse
+            back = d_second[rows, :]
+            small_acc[0, 0:1, :] += jnp.sum(back * value, axis=0, keepdims=True)
+            back = back * scales[0:1, :]
+            back = inverse * (back - value * jnp.mean(back * value, axis=-1, keepdims=True))
+            grad_low[rows, :] = (base[rows, :] + back).astype(BF16)
+
+    count = len(chunks)
+    reused = [k for k in range(count) if chunks[k].panel >= ups]
+
+    def spread(k, first, size):
+        return lanes(chunks[k].panel * width + chunks[k].off + first, size)
+
+    def sums(k, chip, rows, first, size):
+        c = chunks[k]
+        if c.panel < ups:
+            return mine.at[chip, rows, spread(k, first, size)]
+        p = c.panel - ups
+        return wd_all.at[chip, p // downs, p % downs, rows, lanes(c.off + first, size)]
+
+    def passing(k, t, d, rows, first, size):
+        c = chunks[k]
+        if c.panel < ups:
+            if t == 0:
+                return landed.at[d, rows, spread(k, first, size)]
+            return moving.at[t - 1, d, rows, spread(k, first, size)]
+        p = c.panel - ups
+        cols = lanes(p % ups * width + c.off + first, size)
+        slab = 12 + p // ups if t == 0 else p // ups * 6 + (t - 1) * 2 + d
+        if t == 0:
+            rows = pl.ds(d * half + rows.start, rows.size)
+        return wu_all.at[slab // 2, slab % 2, rows, cols]
+
+    every = pl.ds(0, depth)
+
+    def ride(k):
+        return chunks[k].give * at.n if chunks[k].give else 0, chunks[k].size - chunks[k].give
+
+    def product(k, core, put):
+        c = chunks[k]
+        if c.kind == "down":
+            left, right = act_t[:, core, c.j], d_mlp
+        else:
+            tall, right = {
+                "up": (second_t, d_pre),
+                "out": (heads_t, d_attend),
+                "qkv": (normed_t, d_project),
+            }[c.kind]
+            left = tall[:, core]
+        left = left.reshape(ring * depth, entries)
+
+        @pl.loop(0, c.size // tile)
+        def _(t):
+            cols = pl.ds(pl.multiple_of(t * tile, tile), tile)
+            take = pl.ds(pl.multiple_of(c.first + t * tile, tile), tile)
+            put(cols, dot(left, right[:, take]).reshape(ring, depth, tile))
+
+    def out_copy(k):
+        c = chunks[k]
+        out = {"up": o_up, "down": o_down, "out": o_out, "qkv": o_qkv}[c.kind]
+        rows = pl.ds(c.j * depth if c.kind == "down" else 0, depth)
+        return pltpu.make_async_copy(
+            staged.at[k % 2, :, pl.ds(0, c.size)], out.at[rows, pl.ds(c.first, c.size)], out_sem.at[k]
+        )
+
+    def sib(k):
+        src = to_sib.at[k % 2, :, :, pl.ds(0, chunks[k].size)]
+        dst = sums(k, slice(None), slice(None), 0, chunks[k].size)
+        return remote(src, dst, sib_send.at[k], sib_recv.at[k], at.sibling())
+
+    def pre(k):
+        c = chunks[k]
+        src = sums(k, slice(None), slice(None), (c.size - c.give) * (1 - at.n), c.give)
+        dst = x_pre.at[:, :, lanes(c.given_at, c.give)]
+        return remote(src, dst, pre_send.at[k], pre_recv.at[k], at.across())
+
+    def dest(t, d):
+        return at.chip(steps - t if d == 0 else t - steps)
+
+    def ring_out(k, t, d):
+        rows = pl.ds(d * half, half) if t == 0 else every
+        src = sums(k, dest(t, d), rows, *ride(k))
+        land = passing(k, t, d, pl.ds(0, half) if t == 0 else every, *ride(k))
+        return remote(src, land, ring_send.at[k, t, d], ring_recv.at[k, t, d], toward(d))
+
+    def cross(k):
+        first, size = ride(k)
+        dst = x_in.at[:, lanes(chunks[k].start + first, size)]
+        return remote(sums(k, at.q, every, first, size), dst, x_send.at[k], x_recv.at[k], at.across())
+
+    bits = [1 << b for b in range(ring.bit_length() - 1)]
+    partners = [at.sibling(), at.across()] + [at.flipped(bit) for bit in bits]
+    stages = len(partners)
+
+    def small_copy(j):
+        return remote(
+            small_acc.at[j], small_in.at[j], small_send.at[j], small_recv.at[j], partners[j]
+        )
+
+    def row_copy(j, p):
+        rows = pl.ds(p * (entries // ROW_PIECES), entries // ROW_PIECES)
+        src = out_low if j == 0 else grad_low
+        return remote(
+            src.at[rows], rows_got.at[j, rows], row_send.at[j, p], row_recv.at[j, p], at.across()
+        )
+
+    def release():
+        for k in range(parts_count):
+            g_sib(k).wait_send()
+            if k > 0:
+                g_cross(k).wait_send()
+            for s in range(1, steps + 1):
+                for d in (0, 1):
+                    if not idle(k, s, d):
+                        g_ring_out(k, s, d).wait_send()
+        for j, device in enumerate((at.at_ring(-1), at.at_ring(1), at.sibling())):
+            pl.semaphore_signal(free.at[j], inc=1, device_id=device, device_id_type=MESH)
+
+    pairs = width // (2 * HEAD_DIM)
+    cuts = [pairs * j // 8 for j in (0, 2, 5, 8)]
+    work = {
+        0: [normalise, lambda: turned(normed, normed_t)],
+        1: [lambda: project_part(0)],
+        2: [lambda: project_part(1)],
+        3: [lambda: project_part(2), lambda: attention(cuts[0], cuts[1])],
+        4: [lambda: attention(cuts[1], cuts[2])],
+        5: [lambda: attention(cuts[2], cuts[3]), attend_project],
+        6: [lambda: turned(heads, heads_t), lambda: turned(second, second_t)],
+        7: [branch_grad],
+    }
+    back_cuts = [pairs * j // 4 for j in range(5)]
+    back_work = [heads_grad]
+    back_work += [functools.partial(attention_back, back_cuts[j], back_cuts[j + 1]) for j in range(4)]
+    back_work += [functools.partial(normed_grad, j) for j in range(3)]
+    back_work += [finish]
+
+    def gather_turn(i):
+        if i < parts_count:
+            for d in (0, 1):
+                g_ring_out(i, 1, d).start()
+            own_copy(i).start()
+        if i == 2:
+            in_copy(1).start()
+        for s in range(1, steps + 1):
+            k = i - lag * s
+            if 0 <= k < parts_count:
+                for d in (0, 1):
+                    if not idle(k, s, d):
+                        g_ring_in(k, s, d).wait_recv()
+                    if s < steps and not idle(k, s + 1, d):
+                        g_ring_out(k, s + 1, d).start()
+                if s == steps:
+                    own_copy(k).wait()
+                    if k > 0:
+                        g_cross(k).start()
+        k = i - lag * (steps + 1)
+        if 0 <= k < parts_count:
+            if k > 0:
+                g_cross(k, True).wait_recv()
+            g_sib(k).start()
+        k = i - lag * (steps + 1) - 1
+        if 0 <= k < parts_count:
+            g_sib(k, True).wait_recv()
+            if k == 0:
+                for j in (0, 1):
+                    in_copy(j).wait_recv()
+            for piece in ready.get(k, ()):
+                if isinstance(piece, int):
+                    for job in work.get(piece, ()):
+                        job()
+                else:
+                    up_part(*piece)
+
+    ring_at = 1 + lag
+    work_at = up_chunks
+    small_at = work_at + len(back_work)
+
+    def reduce_turn(i):
+        k = i - ring_at - lag * steps - lag
+        if 0 <= k < count:
+            c = chunks[k]
+            cross(k).wait_recv()
+            if k >= 2:
+                out_copy(k - 2).wait()
+            inner = c.size - 2 * c.give
+
+            @over(depth, step)
+            def _(row):
+                rows = pl.ds(row, step)
+
+                def mixed(first, size):
+                    return sums(k, at.q, rows, first, size)[...].astype(F32), x_in[
+                        rows, lanes(c.start + first, size)
+                    ].astype(F32)
+
+                here, there = mixed(c.give, inner)
+                staged[k % 2, rows, c.give : c.give + inner] = here + there
+                if c.give:
+                    alone = (c.size - c.give) * at.n
+                    staged[k % 2, rows, lanes(alone, c.give)] = mixed(alone, c.give)[0]
+                    alone = (c.size - c.give) * (1 - at.n)
+                    staged[k % 2, rows, lanes(alone, c.give)] = mixed(alone, c.give)[1]
+
+            out_copy(k).start()
+        k = i - ring_at - lag * steps
+        if 0 <= k < count:
+            for d in (0, 1):
+                land = passing(k, steps - 1, d, every, *ride(k))
+                remote(
+                    land,
+                    land,
+                    ring_send.at[k, steps - 1, d],
+                    ring_recv.at[k, steps - 1, d],
+                    toward(d),
+                ).wait_recv()
+
+            @over(depth, step)
+            def _(row):
+                rows = pl.ds(row, step)
+                total = sums(k, at.q, rows, *ride(k))
+                value = total[...].astype(F32)
+                for d in (0, 1):
+                    value = value + passing(k, steps - 1, d, rows, *ride(k))[...].astype(F32)
+                total[...] = value.astype(BF16)
+
+            cross(k).start()
+        for t in range(steps - 1, 0, -1):
+            k = i - ring_at - lag * t
+            if 0 <= k < count:
+                for d in (0, 1):
+                    size = half if t == 1 else depth
+                    land = passing(k, t - 1, d, pl.ds(0, size), *ride(k))
+                    remote(
+                        land, land, ring_send.at[k, t - 1, d], ring_recv.at[k, t - 1, d], toward(d)
+                    ).wait_recv()
+                    to = dest(t, d)
+                    low = d * half if t == 1 else 0
+
+                    @over(size, step)
+                    def _(row):
+                        total = sums(k, to, pl.ds(low + row, step), *ride(k))
+                        came = passing(k, t - 1, d, pl.ds(row, step), *ride(k))
+                        value = total[...].astype(F32) + came[...].astype(F32)
+                        total[...] = value.astype(BF16)
+
+                    ring_out(k, t, d).start()
+        k = i - ring_at
+        if 0 <= k < count:
+            c = chunks[k]
+            if c.give > 0:
+                pre(k).wait_recv()
+                alone = (c.size - c.give) * at.n
+
+                @pl.loop(0, ring)
+                def _(chip):
+                    total = sums(k, chip, every, alone, c.give)
+                    came = x_pre[chip, :, lanes(c.given_at, c.give)]
+                    total[...] = (total[...].astype(F32) + came.astype(F32)).astype(BF16)
+
+            for d in (0, 1):
+                if k == reused[0]:
+                    pl.semaphore_wait(free.at[d], 1)
+                ring_out(k, 0, d).start()
+        k = i - 1
+        if 0 <= k < count:
+            c = chunks[k]
+            all_sums = sums(k, slice(None), slice(None), 0, c.size)
+            remote(all_sums, all_sums, sib_send.at[k], sib_recv.at[k], at.sibling()).wait_recv()
+
+            @pl.loop(0, ring)
+            def _(chip):
+                total = sums(k, chip, every, 0, c.size)
+                total[...] = (total[...].astype(F32) + own[chip, :, 0 : c.size]).astype(BF16)
+
+            if c.give > 0:
+                pre(k).start()
+        k = i
+        if 0 <= k < count:
+            if k >= 2:
+                sib(k - 2).wait_send()
+
+            def keep_other(cols, value):
+                to_sib[k % 2, :, :, cols] = value.astype(BF16)
+
+            def keep_own(cols, value):
+                own[:, :, cols] = value
+
+            product(k, 1 - at.c, keep_other)
+            if k == reused[0]:
+                pl.semaphore_wait(free.at[2], 1)
+            sib(k).start()
+            product(k, at.c, keep_own)
+        j = i - work_at
+        if 0 <= j < len(back_work):
+            back_work[j]()
+        if 0 <= j < ROW_PIECES:
+            row_copy(0, j).start()
+        p = i - small_at
+        if 0 <= p < ROW_PIECES:
+            row_copy(1, p).start()
+        j = i - small_at
+        if 0 <= j <= stages:
+            if j > 0:
+                small_copy(j - 1).wait_recv()
+                small_acc[j] = small_acc[j - 1] + small_in[j - 1]
+            if j < stages:
+                small_copy(j).start()
+            else:
+                o_small[...] = small_acc[stages]
+
+    greet(partners + [at.at_ring(1), at.at_ring(-1)])
+    in_copy(0).start()
+    offset = up_at + lag * (steps + 1) + 1
+    for i in range(offset + count + ring_at + lag * steps + lag + 1):
+        gather_turn(i)
+        if i == offset + up_chunks - 1:
+            release()
+            close()
+        reduce_turn(i - offset)
+
+    for j in (0, 1):
+        in_copy(j).wait_send()
+    for k in range(count):
+        if k >= count - 2:
+            sib(k).wait_send()
+            out_copy(k).wait()
+        if chunks[k].give > 0:
+            pre(k).wait_send()
+        cross(k).wait_send()
+        for t in range(steps):
+            for d in (0, 1):
+                ring_out(k, t, d).wait_send()
+    for j in range(stages):
+        small_copy(j).wait_send()
+    for j in (0, 1):
+        for p in range(ROW_PIECES):
+            row_copy(j, p).wait()
+
+
+class Chunk(NamedTuple):
+    kind: str
+    j: int
+    first: int
+    size: int
+    panel: int
+    off: int
+    start: int
+    give: int
+    given_at: int
+
+
+def cut_chunks(width, ff):
+    panels = [("up", j, j * width) for j in range(ff // width)]
+    panels += [("down", j, 0) for j in range(ff // width)]
+    panels += [("out", 0, 0)] + [("qkv", j, j * width) for j in range(3)]
+    plain = []
+    for panel, (kind, j, first) in enumerate(panels):
+        off = 0
+        last = panel in (ff // width - 1, len(panels) - 1)
+        for size in LAST_PIECES if last else PIECES:
+            plain.append((kind, j, first + off, size, panel, off))
+            off += size
+    chunks, start, given = [], 0, 0
+    for k, piece in enumerate(plain):
+        inside = GIVE_SKIP[0] <= k < len(plain) - GIVE_SKIP[1]
+        give = GIVE if inside and piece[3] == 512 else 0
+        chunks.append(Chunk(*piece, start, give, given))
+        start += piece[3]
+        given += give
+    return tuple(chunks), start, given
+
+
+def layer(wide, gains, wq, wo, wu, wd, kept, given, router, live):
+    depth, width = wo.shape
+    ring, steps = wide // 2, wide // 4
+    entries = kept.shape[1]
+    ff = wu.shape[1]
+    ups = downs = ff // width
+    chunks, columns, given_columns = cut_chunks(width, ff)
+    parts = 1 + (3 + downs + ups) * len(PIECES) + len(LAST_PIECES)
+    count = len(chunks)
+    stages = 2 + (ring.bit_length() - 1)
+    in_vmem = pl.BlockSpec(memory_space=pltpu.VMEM)
+    anywhere = pl.BlockSpec(memory_space=pl.ANY)
+    dma = pltpu.SemaphoreType.DMA
+    vmem = pltpu.VMEM
+    shape = jax.ShapeDtypeStruct
+    tall = (ring, 2, depth, entries)
+    square = (entries, width)
+    return pl.pallas_call(
+        functools.partial(layer_kernel, wide, chunks),
+        out_shape=[
+            shape((depth, 3 * width), F32),
+            shape((depth, width), F32),
+            shape((depth, ff), F32),
+            shape((ff // wide, width), F32),
+            shape((8, width), F32),
+            shape((2, entries, width), BF16),
+            shape(square, BF16),
+            shape(square, BF16),
+        ],
+        in_specs=[anywhere] * 5 + [in_vmem, anywhere, in_vmem, in_vmem],
+        out_specs=[anywhere] * 4 + [in_vmem, anywhere, in_vmem, in_vmem],
+        scratch_shapes=[
+            vmem((ring, 2, depth, 3 * width), BF16),
+            vmem((ring, 2, depth, width), BF16),
+            vmem((ring, 2, depth, ff), BF16),
+            vmem((ring, 2, downs, depth, width), BF16),
+            vmem((ring, 2) + gains.shape, BF16),
+            vmem((8, width), F32),
+            vmem((2,) + square, BF16),
+            vmem(square, BF16),
+            vmem(square, BF16),
+            vmem((entries, 3 * width), BF16),
+            vmem(square, BF16),
+            vmem(square, F32),
+            vmem(square, F32),
+            vmem(square, BF16),
+            vmem((entries, 512), BF16),
+            vmem((entries, ff), BF16),
+            vmem(square, F32),
+            vmem(square, F32),
+            vmem(square, BF16),
+            vmem(square, BF16),
+            vmem(square, F32),
+            vmem((entries, 3 * width), BF16),
+            vmem(tall, BF16),
+            vmem(tall, BF16),
+            vmem(tall, BF16),
+            vmem((ring, 2, downs, depth, entries), BF16),
+            vmem((entries, 1), F32),
+            vmem((entries, 1), F32),
+            vmem((ring, depth, 512), F32),
+            vmem((2, ring, depth, 512), BF16),
+            vmem((ring, depth, ups * width), BF16),
+            vmem((2, depth // 2, ups * width), BF16),
+            vmem((steps - 1, 2, depth, ups * width), BF16),
+            vmem((ring, depth, max(given_columns, 128)), BF16),
+            vmem((depth, columns), BF16),
+            vmem((2, depth, 512), F32),
+            vmem((stages + 1, 8, width), F32),
+            vmem((stages, 8, width), F32),
+            dma((parts,)),
+            dma((parts, steps, 2)),
+            dma((parts, steps, 2)),
+            dma((parts,)),
+            dma((parts,)),
+            dma((parts,)),
+            dma((parts,)),
+            dma((2,)),
+            dma((2,)),
+            dma((count,)),
+            dma((count,)),
+            dma((count,)),
+            dma((count,)),
+            dma((count, steps, 2)),
+            dma((count, steps, 2)),
+            dma((count,)),
+            dma((count,)),
+            dma((count,)),
+            dma((stages,)),
+            dma((stages,)),
+            dma((2, ROW_PIECES)),
+            dma((2, ROW_PIECES)),
+            pltpu.SemaphoreType.REGULAR((3,)),
+        ],
+        compiler_params=pltpu.CompilerParams(
+            collective_id=1, has_side_effects=True, vmem_limit_bytes=63 * 1024 * 1024
+        ),
+        name="layer",
+    )(gains, wq, wo, wu, wd.reshape(downs, depth, width), kept, given, router, live)
+
+
+def paired_body(
+    wide, tokens, cotangent, lengths, routes, w_qkv, w_out, w_up, w_down, gain_attn, gain_mlp, router
+):
+    place = lax.axis_index("narrow")
+    seqs, span, width = tokens.shape
+    list_len = routes.shape[1]
+    depth = gain_attn.shape[0]
+    counts = lengths // 8
+    entry = jnp.arange(list_len, dtype=jnp.int32)
+    live = entry[None, :] < counts[:, None]
+    local_slot = jnp.where(live, routes - place * span, -1)
+    spots = jnp.arange(span, dtype=jnp.int32)
+    chosen = (local_slot[:, :, None] == spots[None, None, :]).astype(BF16)
+
+    def take(source):
+        return jnp.einsum("sep,spd->sed", chosen, source, preferred_element_type=F32).astype(BF16)
+
+    picked = jnp.stack([take(tokens), take(cotangent)])
+    kept = lax.dynamic_index_in_dim(picked, place, 1, keepdims=False)
+    given = lax.dynamic_index_in_dim(picked, 1 - place, 1, keepdims=False)
+    gains = jnp.stack(
+        [jnp.concatenate([gain_attn, gain_attn]), jnp.concatenate([gain_mlp, gain_mlp])]
+    )
+    gains = jnp.pad(gains, ((0, 14), (0, 0)))
+    router_row = router.astype(F32)[None, :]
+    live_row = lax.dynamic_index_in_dim(live, place, 0, keepdims=True).astype(jnp.int32)
+    grad_qkv, grad_out, grad_up, grad_down, small, back_got, out_low, grad_low = layer(
+        wide, gains, w_qkv, w_out, w_up, w_down, kept, given, router_row, live_row
+    )
+    back = jnp.stack([out_low, grad_low])
+    first = place == 0
+    rows_out = jnp.stack([jnp.where(first, back, back_got), jnp.where(first, back_got, back)], axis=1)
+    hit = jnp.any(local_slot[:, :, None] == spots[None, None, :], axis=1)
+
+    def put(base, fresh):
+        spread = jnp.einsum("sep,sed->spd", chosen, fresh, preferred_element_type=F32)
+        return jnp.where(hit[:, :, None], spread.astype(BF16), base)
+
+    start = lax.axis_index("wide") * depth
+    return (
+        put(tokens, rows_out[0]),
+        put(cotangent, rows_out[1]),
+        grad_qkv,
+        grad_out,
+        grad_up,
+        grad_down,
+        lax.dynamic_slice_in_dim(small[0], start, depth),
+        lax.dynamic_slice_in_dim(small[1], start, depth),
+        small[2],
+    )
+
+
+def body(wide, narrow, tokens, *others):
+    if narrow == 2 and tokens.shape[0] == 2 and wide == 16:
+        return paired_body(wide, tokens, *others)
+    return general_body(tokens, *others)
+
+
 def solution(mesh):
     in_specs = (
         P("wide", "narrow", None),
@@ -243,4 +1216,5 @@
         P("wide"),
         P(),
     )
-    return jax.shard_map(body, mesh=mesh, in_specs=in_specs, out_specs=out_specs, check_vma=False)
+    sizes = mesh.shape["wide"], mesh.shape["narrow"]
+    return jax.shard_map(functools.partial(body, *sizes), mesh=mesh, in_specs=in_specs, out_specs=out_specs, check_vma=False)

time: 1290 us -> 279 us (0.22)
  waiting for transfers between devices: 835 us -> 0 us
  Pallas kernels: 0 us -> 248 us
  local copies, waits for them, and re-layouts: 208 us -> 6.26 us
  blocking collectives: 108 us -> 0 us
  matrix products: 91.4 us -> 11.1 us
  between operations: 17.9 us -> 1.15 us
    reduce_scatter x8 -> x0, waiting for transfers between devices: 588 us -> none  [the longest x1 182 us: body(): lax.psum_scatter(grad_up_full, 'wide', scatter_dimension=0, tiled=True)]
    pallas_call x0 -> x1, Pallas kernels: none -> 248 us  [layer(): pl.pallas_call(functools.partial(layer_kernel, wide, chunks), out_shape=[...]
    all_gather x8 -> x0, waiting for transfers between devices: 243 us -> none  [the longest x1 72.4 us: body(): lax.all_gather(w_down, 'wide', axis=0, tiled=True)]
    scatter x2 -> x0, local copies, waits for them, and re-layouts: 137 us -> none  [body(): base.at[where_to].set(fresh, mode='drop')]
    dot_general x20 -> x4, matrix products: 91.4 us -> 11.1 us  [the longest x2 6.12 us: put(): jnp.einsum('sep,sed->spd', chosen, fresh, preferred_element_type=F32)]
    unnamed x2 -> x0, blocking collectives: 63.4 us -> none
    psum x2 -> x0, blocking collectives: 44.9 us -> none  [the longest x1 39.4 us: body(): grad_router = lax.psum(grad_router_part, ('wide', 'narrow'))]
    gather x2 -> x0, local copies, waits for them, and re-layouts: 36.5 us -> none  [the longest x1 18.2 us: body(): taken_cot = jnp.take_along_axis(cotangent, pick[:, :, None], axis=1)]
  transfers between devices with their start and end apart: 17 -> 0, of which waited for: 12 -> 0; matrix products, arithmetic and copies ran while one was open for 17% -> 0% of each run, Pallas kernels for 0% -> 0%
where the time goes in v4:
time: 279 us; the launch traced here: 275 us
  Pallas kernels  248 us (89%)
  matrix products  11.1 us (4%)
  other arithmetic  8.42 us (3%)
  local copies, waits for them, and re-layouts  6.26 us (2%)
    pallas_call x1, Pallas kernels, layer(): pl.pallas_call(functools.partial(layer_kernel, wide, chunks), out_shape=[...  248 us
    dot_general x2, matrix products, put(): jnp.einsum('sep,sed->spd', chosen, fresh, preferred_element_type=F32)  6.12 us

profile of v4, /device:TPU:0, one launch (start us, length us, event | category | flops | bytes accessed | tf_op | source)
XLA Modules:
  0.0 275.1 jit_solution(6952857983913069125)
XLA Ops:
  0.6 0.7 and_select_fusion
  1.3 0.1 iota_compare_fusion.14
  1.4 0.6 dynamic-slice_convert_fusion.live
  2.0 0.8 subtract_select_fusion
  2.7 0.8 maximum_bitcast_fusion
  3.5 0.6 fusion.23.gains
  4.1 0.4 fusion.2
  4.5 1.3 broadcast_in_dim.32
  5.8 0.0 copy-start.5
  5.8 3.6 %fusion.5 = bf16[1,2,256,1024]{3,2,1,0:T(8,128)(2,1)S(1)} fusion(bf16[2,1024,1024]{2,1,0:T(8,128)(2,1)} %param.12, s32[2,256]{1,0:T(2,128)S(1)} %subtract_select_fusion), kind=kOutput, calls=%fused_computation.14 | convolution fusion | flops 1074790400 | bytes 5244928 | tf_op jit(solution)/shard_map/sep,spd->sed/dot_general | solution.py:1151
  9.4 0.0 copy-done.5
  9.4 1.3 fusion.6
  10.7 1.5 fusion.11
  12.2 248.2 %layer.1 = (f32[64,3072]{1,0:T(8,128)}, f32[64,1024]{1,0:T(8,128)}, f32[64,4096]{1,0:T(8,128)}, f32[256,1024]{1,0:T(8,128)}, f32[8,1024]{1,0:T(8,128)}, /*index=...) custom-call(bf16[16,128]{1,0:T(8,128)(2,1)} %fusion.23.gains, bf16[64,3072]{1,0:T(8,128)(2,1)} %wq.1, ...), custom_call_target="tpu_custom_call" | custom-call | tf_op jit(solution)/shard_map/layer/pallas_call | solution.py:1052
  260.5 0.0 copy-start.4
  260.5 1.8 select_bitcast_fusion
  262.3 1.5 fusion.28
  263.8 0.6 fusion.25
  264.4 0.6 fusion.24
  264.9 0.0 copy-done.4
  264.9 0.0 copy-start.6
  264.9 3.1 %convert_select_fusion = bf16[2,1024,1024]{2,1,0:T(8,128)(2,1)} fusion(bf16[2,1024,1024]{2,1,0:T(8,128)(2,1)S(1)} %copy-done.4, pred[2,1024]{1,0:T(4,128)(4,1)S(1)} %fusion.2, bf16[2,1,256,1024]{3,2,0,1:T(8,128)(2,1)S(1)} %get-tuple-element.25, bf16[2,1,256,1024]{3,2,0,1:T(8,128)(2,1)S(1)} %get-tuple-element.26, s32[2,256]{1,0:T(2,128)S(1)} %subtract_select_fusion), kind=kOutput, calls=%fused_computation | convolution fusion | flops 1078984704 | bytes 10489856 | tf_op jit(solution)/shard_map/sep,sed->spd/dot_general | solution.py:1171
  268.0 0.1 copy-done.6
  268.1 0.0 copy-start.2
  268.1 0.0 copy-start.3
  268.1 3.1 %convert_select_fusion.1 = bf16[2,1024,1024]{2,1,0:T(8,128)(2,1)} fusion(bf16[2,1024,1024]{2,1,0:T(8,128)(2,1)S(1)} %copy-done.6, pred[2,1024]{1,0:T(4,128)(4,1)S(1)} %fusion.2, bf16[2,1,256,1024]{3,2,0,1:T(8,128)(2,1)S(1)} %get-tuple-element.26, bf16[2,1,256,1024]{3,2,0,1:T(8,128)(2,1)S(1)} %get-tuple-element.25, s32[2,256]{1,0:T(2,128)S(1)} %subtract_select_fusion), kind=kOutput, calls=%fused_computation.1 | convolution fusion | flops 1078984704 | bytes 10489856 | tf_op jit(solution)/shard_map/sep,sed->spd/dot_general | solution.py:1171
  271.1 0.0 copy-done.2
  271.1 0.0 copy-start.1
  271.1 0.0 copy-start
  271.1 0.9 copy.28
  272.0 0.0 copy-done.3
  272.0 0.7 copy.29
  272.7 0.0 copy-done.1
  272.7 1.0 copy.30
  273.7 0.0 copy-done
  273.7 1.0 copy.31
Async XLA Ops:
  5.8 3.6 %copy-start.5 = (bf16[2,1024,1024]{2,1,0:T(8,128)(2,1)S(1)}, bf16[2,1024,1024]{2,1,0:T(8,128)(2,1)}, u32[]{:S(2)}) copy-start(bf16[2,1024,1024]{2,1,0:T(8,128)(2,1)} %param.11) | copy-start | bytes 12582916
  260.5 4.5 %copy-start.4 = (bf16[2,1024,1024]{2,1,0:T(8,128)(2,1)S(1)}, bf16[2,1024,1024]{2,1,0:T(8,128)(2,1)}, u32[]{:S(2)}) copy-start(bf16[2,1024,1024]{2,1,0:T(8,128)(2,1)} %param.12) | copy-start | bytes 12582916
  264.9 3.1 %copy-start.6 = (bf16[2,1024,1024]{2,1,0:T(8,128)(2,1)S(1)}, bf16[2,1024,1024]{2,1,0:T(8,128)(2,1)}, u32[]{:S(2)}) copy-start(bf16[2,1024,1024]{2,1,0:T(8,128)(2,1)} %param.11) | copy-start | bytes 12582916
  268.1 3.1 %copy-start.2 = (f32[64,3072]{1,0:T(8,128)S(1)}, f32[64,3072]{1,0:T(8,128)}, u32[]{:S(2)}) copy-start(f32[64,3072]{1,0:T(8,128)} %get-tuple-element.45) | copy-start | bytes 2359300
  268.1 4.0 %copy-start.3 = (f32[64,1024]{1,0:T(8,128)S(1)}, f32[64,1024]{1,0:T(8,128)}, u32[]{:S(2)}) copy-start(f32[64,1024]{1,0:T(8,128)} %get-tuple-element.46) | copy-start | bytes 786436
  271.1 1.6 copy-start.1
  271.1 2.6 copy-start
